TPU v7x, 256 devices: a whole 4x4x8 slice. The times are simulated.
256 devices in a mesh: ctx: 64 (over y, z, core), dp: 4 (over x).
Axes of the slice: x: 4, y: 4, z: 8, core: 2. Of those that a mesh axis runs over, the one named last changes fastest.
Arguments:
- tokens: bfloat16 [4, 16384, 4096], P('dp', 'ctx'), may hold values from -16 to 16
- projected: bfloat16 [4, 16384, 6144], P('dp', 'ctx'), may hold values from -6 to 6
- down_proj: bfloat16 [3, 4096, 32], replicated, may hold values from -0.09375 to 0.09375
- up_projection: bfloat16 [3, 32, 2048], replicated, may hold values from -1 to 1
- block_ids: int32 [4, 64, 3], P('dp'), may hold values from 0 to 63, as said below
- cotangent: bfloat16 [4, 16384, 2048], P('dp', 'ctx'), may hold values from -192 to 192
Outputs:
- attn_out: bfloat16 [4, 16384, 2048], P('dp', 'ctx')
- grad_proj: bfloat16 [4, 16384, 6144], P('dp', 'ctx')
- grad_down: float32 [3, 4096, 32], P(None, ('ctx', 'dp'))
- grad_up: float32 [3, 32, 2048], P(None, None, ('ctx', 'dp'))
Inputs may be any that keep to these rules, and one draw needn't show every extreme that they name: block_ids[r, b, 0] = b. Slots 1 and 2 name two different blocks below b, or b itself where the slot is empty (both empty for b = 0, slot 2 for b = 1). In each replica no block is named in the other slots of more than 6 query blocks, and some block is named by exactly 6.
All inputs are finite; a program needn't handle non-finite values.
Results may differ from a plain program's by a relative error of at most 0.012.
The roundings to bfloat16 on the way count: a program that leaves them out, or rounds other values in their place, can miss the bound.
Values may be sent and summed in bfloat16 or wider, within the bound.
No kernel may reach another device: no remote copies, remote signals or barrier semaphores. Data moves between devices by JAX's collectives and lax.ppermute only.
A program may use at most 192 MiB of HBM per device.

v0:
```python
import jax
import jax.numpy as jnp
from jax import lax
from jax.sharding import PartitionSpec as P

HD = 128
MOST = 6


adapter_scale = 0.5


def with_adapters(inputs, frozen_proj, down_proj, up_projection, feat_width):
    low_rank_states = []
    field_list = []
    for group_member in range(3):
        low_rank = jnp.dot(
            inputs, down_proj[group_member], preferred_element_type=jnp.float32
        ).astype(jnp.bfloat16)
        adapter_result = jnp.dot(
            low_rank, up_projection[group_member], preferred_element_type=jnp.float32
        )
        frozen_weight = frozen_proj[
            :, group_member * feat_width : (group_member + 1) * feat_width
        ].astype(jnp.float32)
        field_list.append((frozen_weight + adapter_scale * adapter_result).astype(jnp.bfloat16))
        low_rank_states.append(low_rank)
    return (low_rank_states, field_list)


def shards(tokens, projected, down_proj, up_projection, block_ids, cotangent):
    inputs = tokens[0]
    grad_out = cotangent[0]
    block_count = lax.axis_size("ctx")
    my_block = lax.axis_index("ctx")
    block_rows = inputs.shape[0]
    feat_width = up_projection.shape[2]
    head_count = feat_width // HD
    slice_rows = block_rows // block_count
    chosen = block_ids[0]
    slot_count = chosen.shape[1]
    low_rank_states, field_list = with_adapters(
        inputs, projected[0], down_proj, up_projection, feat_width
    )
    queries, own_keys, own_values = field_list
    packed = jnp.concatenate([own_keys, own_values], axis=1)
    spread = lax.all_to_all(
        packed.reshape(block_count, slice_rows, 2 * feat_width),
        "ctx",
        split_axis=0,
        concat_axis=0,
        tiled=True,
    )
    wanted = jnp.transpose(chosen[:, 1:])
    picked = jnp.take(spread, wanted, axis=0)
    fetched = lax.all_to_all(picked, "ctx", split_axis=1, concat_axis=1, tiled=True)
    key_value = jnp.concatenate(
        [packed[None], fetched.reshape(slot_count - 1, block_rows, 2 * feat_width)], axis=0
    )
    key_count = slot_count * block_rows
    key_value = key_value.reshape(key_count, 2 * feat_width)
    my_slots = lax.dynamic_index_in_dim(chosen, my_block, 0, keepdims=False)
    usable = (my_slots != my_block) | (jnp.arange(slot_count) == 0)
    key_slot = jnp.arange(key_count) // block_rows
    slot_open = jnp.any(
        (key_slot[:, None] == jnp.arange(slot_count)[None, :]) & usable[None, :], axis=1
    )
    causal = (jnp.arange(key_count) % block_rows)[None, :] <= jnp.arange(block_rows)[:, None]
    visible = jnp.where((key_slot == 0)[None, :], causal, slot_open[None, :])
    score_scale = HD ** (-0.5)
    contract_last = (((1,), (1,)), ((), ()))
    contract_first = (((0,), (0,)), ((), ()))
    attended_list = []
    dquery_list = []
    dkey_list = []
    dvalue_list = []
    for head_index in range(head_count):
        lower = head_index * HD
        query_head = queries[:, lower : lower + HD]
        key_head = key_value[:, lower : lower + HD]
        value_head = key_value[:, feat_width + lower : feat_width + lower + HD]
        grad_head = grad_out[:, lower : lower + HD]
        scores = (
            lax.dot_general(query_head, key_head, contract_last, preferred_element_type=jnp.float32)
            * score_scale
        )
        scores = jnp.where(visible, scores, -jnp.inf)
        shifted = jnp.exp(scores - jnp.max(scores, axis=1, keepdims=True))
        attn_probs = shifted / jnp.sum(shifted, axis=1, keepdims=True)
        weights = attn_probs.astype(jnp.bfloat16)
        attended = jnp.dot(weights, value_head, preferred_element_type=jnp.float32).astype(
            jnp.bfloat16
        )
        drift = jnp.sum(
            attended.astype(jnp.float32) * grad_head.astype(jnp.float32), axis=1, keepdims=True
        )
        dprobs = lax.dot_general(
            grad_head, value_head, contract_last, preferred_element_type=jnp.float32
        )
        dscores = (attn_probs * (dprobs - drift) * score_scale).astype(jnp.bfloat16)
        dquery_list.append(jnp.dot(dscores, key_head, preferred_element_type=jnp.float32))
        dkey_list.append(
            lax.dot_general(dscores, query_head, contract_first, preferred_element_type=jnp.float32)
        )
        dvalue_list.append(
            lax.dot_general(weights, grad_head, contract_first, preferred_element_type=jnp.float32)
        )
        attended_list.append(attended)
    attn_rows = jnp.concatenate(attended_list, axis=1)
    dquery = jnp.concatenate(dquery_list, axis=1).astype(jnp.bfloat16)
    dpacked = jnp.concatenate(dkey_list + dvalue_list, axis=1).reshape(
        slot_count, block_rows, 2 * feat_width
    )
    own_part = dpacked[0]
    remote = (
        dpacked[1:]
        .astype(jnp.bfloat16)
        .reshape(slot_count - 1, block_count, slice_rows, 2 * feat_width)
    )
    arrived = lax.all_to_all(remote, "ctx", split_axis=1, concat_axis=1, tiled=True)
    pair_count = (slot_count - 1) * block_count
    arrived_flat = arrived.reshape(pair_count, slice_rows * 2 * feat_width)
    owners = wanted.reshape(-1)
    requesters = jnp.broadcast_to(jnp.arange(block_count)[None, :], wanted.shape).reshape(-1)
    live_pair = owners != requesters
    matched = (owners[None, :] == jnp.arange(block_count)[:, None]) & live_pair[None, :]
    block_ranking = jnp.cumsum(matched.astype(jnp.int32), axis=1) - 1
    taken = matched[:, None, :] & (block_ranking[:, None, :] == jnp.arange(MOST)[None, :, None])
    filled = jnp.any(taken, axis=2)
    source_row = jnp.sum(taken.astype(jnp.int32) * jnp.arange(pair_count)[None, None, :], axis=2)
    source_row = jnp.where(filled, source_row, pair_count)
    padded = jnp.concatenate(
        [arrived_flat, jnp.zeros((1, arrived_flat.shape[1]), jnp.bfloat16)], axis=0
    )
    slot_rows = jnp.take(padded, source_row, axis=0).reshape(
        block_count, MOST, slice_rows, 2 * feat_width
    )
    received = lax.all_to_all(slot_rows, "ctx", split_axis=0, concat_axis=0, tiled=True)
    returned = jnp.sum(received, axis=1, dtype=jnp.float32).reshape(block_rows, 2 * feat_width)
    key_total = own_part + returned
    grad_fields = jnp.concatenate(
        [
            dquery,
            key_total[:, :feat_width].astype(jnp.bfloat16),
            key_total[:, feat_width:].astype(jnp.bfloat16),
        ],
        axis=1,
    )
    grad_scale = (lax.axis_size("ctx") * lax.axis_size("dp") * block_rows) ** (-0.5)
    down_terms = []
    up_projection_terms = []
    for group_member in range(3):
        gradient_piece = grad_fields[:, group_member * feat_width : (group_member + 1) * feat_width]
        up_projection_terms.append(
            adapter_scale
            * grad_scale
            * lax.dot_general(
                low_rank_states[group_member],
                gradient_piece,
                contract_first,
                preferred_element_type=jnp.float32,
            )
        )
        low_rank_gradient = (
            adapter_scale
            * lax.dot_general(
                gradient_piece,
                up_projection[group_member],
                contract_last,
                preferred_element_type=jnp.float32,
            )
        ).astype(jnp.bfloat16)
        down_terms.append(
            grad_scale
            * lax.dot_general(
                inputs, low_rank_gradient, contract_first, preferred_element_type=jnp.float32
            )
        )
    grad_down, grad_up = (
        lax.psum_scatter(jnp.stack(down_terms), ("ctx", "dp"), scatter_dimension=1, tiled=True),
        lax.psum_scatter(
            jnp.stack(up_projection_terms), ("ctx", "dp"), scatter_dimension=2, tiled=True
        ),
    )
    return (attn_rows[None], grad_fields[None], grad_down, grad_up)


def solution(mesh):
    placed = (
        P("dp", "ctx", None),
        P("dp", "ctx", None),
        P(),
        P(),
        P("dp", None, None),
        P("dp", "ctx", None),
    )
    return jax.shard_map(
        shards,
        mesh=mesh,
        in_specs=placed,
        out_specs=(
            P("dp", "ctx", None),
            P("dp", "ctx", None),
            P(None, ("ctx", "dp"), None),
            P(None, None, ("ctx", "dp")),
        ),
        check_vma=False,
    )
```

profile of v0, /device:TPU:1, one launch (start us, length us, event | category | flops | bytes accessed | tf_op | source)
XLA Modules:
  0.0 1107.0 jit_solution(5183981762004650565)
XLA Ops:
  16.2 2.5 fusion.356
  18.8 4.1 reshape.243
  22.9 13.7 %all-to-all-start = ((bf16[64,4,4096]{2,1,0:T(4,128)(2,1)}), bf16[64,4,4096]{2,1,0:T(4,128)(2,1)}, u32[]{:S(2)}, u32[]{:S(2)}) async-start(bf16[64,4,4096]{2,1,0:T(4,128)(2,1)} %reshape.243), calls=%async_computation | async-start | bytes 4194304 | tf_op jit(solution)/shard_map/all_to_all | solution.py:47
  36.7 50.9 %all-to-all-done = bf16[64,4,4096]{2,1,0:T(4,128)(2,1)} async-done(((bf16[64,4,4096]{2,1,0:T(4,128)(2,1)}), bf16[64,4,4096]{2,1,0:T(4,128)(2,1)}, u32[]{:S(2)}, u32[]{:S(2)}) %all-to-all-start) | async-done | bytes 2097184 | tf_op jit(solution)/shard_map/all_to_all | solution.py:47
  87.6 9.1 gather_fusion
  96.7 4.5 copy.145
  101.7 5.2 copy.146
  106.9 6.3 all-to-all-start.1
  114.7 8.4 copy.148
  125.7 2.6 fusion.7
  128.4 80.5 %all-to-all-done.1 = bf16[2,64,4,4096]{3,2,0,1:T(4,128)(2,1)} async-done(((bf16[2,64,4,4096]{3,2,0,1:T(4,128)(2,1)}), bf16[2,64,4,4096]{3,2,0,1:T(4,128)(2,1)}, u32[]{:S(2)}, u32[]{:S(2)}) %all-to-all-start.1) | async-done | bytes 4194336 | tf_op jit(solution)/shard_map/all_to_all | solution.py:56
  208.9 8.5 copy.147
  217.5 10.4 pad_maximum_fusion
  227.9 7.2 copy.149
  275.8 4.6 copy-done.3
  280.4 2.3 slice.729
  282.7 6.4 copy.168
  289.1 7.2 convert_element_type.385
  296.3 7.9 copy.169
  304.2 5.9 all-to-all-start.2
  311.4 94.6 %all-to-all-done.2 = bf16[2,64,4,4096]{3,2,0,1:T(4,128)(2,1)} async-done(((bf16[2,64,4,4096]{3,2,0,1:T(4,128)(2,1)}), bf16[2,64,4,4096]{3,2,0,1:T(4,128)(2,1)}, u32[]{:S(2)}, u32[]{:S(2)}) %all-to-all-start.2) | async-done | bytes 4194336 | tf_op jit(solution)/shard_map/all_to_all | solution.py:120
  406.0 4.2 copy.170
  410.2 2.9 copy.196
  413.1 2.5 concatenate.27
  415.6 30.9 %gather_fusion.1 = bf16[384,16384]{1,0:T(8,128)(2,1)} fusion(bf16[129,16384]{1,0:T(8,128)(2,1)} %concatenate.27, s32[1024]{0:T(1024)S(1)} %pad_clamp_fusion), kind=kCustom, calls=%fused_computation.1 | custom fusion | bytes 25167360 | tf_op jit(solution)/shard_map/jit(_take)/gather | solution.py:135
  446.5 21.3 %gather.12 = bf16[64,6,4,4096]{3,2,1,0:T(4,128)(2,1)} reshape(bf16[384,16384]{1,0:T(8,128)(2,1)} %gather_fusion.1) | data formatting | bytes 25165824 | tf_op jit(solution)/shard_map/jit(_take)/gather | solution.py:135
  467.7 11.5 %broadcast_select_fusion = bf16[64,6,4,4096]{3,2,1,0:T(4,128)(2,1)} fusion(bf16[64,6,4,4096]{3,2,1,0:T(4,128)(2,1)} %gather.12, pred[64,6]{1,0:T(8,128)(4,1)S(1)} %copy.167), kind=kLoop, calls=%fused_computation.3 | loop fusion | flops 6291456 | bytes 25166208 | tf_op jit(solution)/shard_map/jit(_take)/select_n | solution.py:135
  479.3 5.9 all-to-all-start.3
  485.3 2.1 constant_dynamic-update-slice_fusion.48
  489.4 2.0 constant_dynamic-update-slice_fusion.46
  491.4 2.0 constant_dynamic-update-slice_fusion.45
  493.3 2.0 constant_dynamic-update-slice_fusion.44
  495.3 2.0 constant_dynamic-update-slice_fusion.43
  497.2 2.0 constant_dynamic-update-slice_fusion.42
  501.2 2.0 constant_dynamic-update-slice_fusion.40
  517.2 2.6 fusion.2
  519.9 241.0 %all-to-all-done.3 = bf16[64,6,4,4096]{3,2,1,0:T(4,128)(2,1)} async-done(((bf16[64,6,4,4096]{3,2,1,0:T(4,128)(2,1)}), bf16[64,6,4,4096]{3,2,1,0:T(4,128)(2,1)}, u32[]{:S(2)}, u32[]{:S(2)}) %all-to-all-start.3) | async-done | bytes 12582944 | tf_op jit(solution)/shard_map/all_to_all | solution.py:138
  760.9 14.9 %convert_reduce_fusion = f32[64,4,4096]{2,1,0:T(4,128)} fusion(bf16[64,6,4,4096]{3,2,1,0:T(4,128)(2,1)} %all-to-all-done.3), kind=kLoop, calls=%fused_computation.2 | loop fusion | flops 11534336 | bytes 16777216 | tf_op jit(solution)/shard_map/reduce_sum | solution.py:139
  775.8 5.3 reshape.248
  781.1 5.6 copy.172
  786.7 5.4 constant_dynamic-update-slice_fusion.16
  794.6 3.0 fusion
  797.6 3.0 fusion.1
  801.7 3.1 copy.174
  804.8 2.4 pad_maximum_fusion.2
  807.3 7.2 copy.173
  817.1 4.6 copy.176
  821.8 275.5 %all-reduce.6.cloned.1.call-done = (f32[3,4096,32]{2,0,1:T(4,128)}, f32[3,32,2048]{1,0,2:T(4,128)}) async-done(((f32[3,4096,32]{2,0,1:T(4,128)}, f32[3,32,2048]{1,0,2:T(4,128)}), (f32[3,4096,32]{2,0,1:T(4,128)}, f32[3,32,2048]{1,0,2:T(4,128)})) %all-reduce.6.cloned.1.call-update) | async-done | bytes 2359312
  (229 shorter events, 82.1 us)
Async XLA Ops:
  7.2 1.6 copy-start
  7.2 7.3 copy-start.30
  10.4 4.1 copy-start.34
  12.1 0.6 copy-start.32
  16.2 20.4 %copy-start.38 = (s32[1,64,3]{1,0,2:T(1,128)S(1)}, s32[1,64,3]{1,0,2:T(1,128)}, u32[]{:S(2)}) copy-start(s32[1,64,3]{1,0,2:T(1,128)} %param.10) | copy-start | bytes 2308
  22.9 64.8 %all-to-all-start = ((bf16[64,4,4096]{2,1,0:T(4,128)(2,1)}), bf16[64,4,4096]{2,1,0:T(4,128)(2,1)}, u32[]{:S(2)}, u32[]{:S(2)}) async-start(bf16[64,4,4096]{2,1,0:T(4,128)(2,1)} %reshape.243), calls=%async_computation | async-start | bytes 4194304 | tf_op jit(solution)/shard_map/all_to_all | solution.py:47
  106.9 102.0 %all-to-all-start.1 = ((bf16[2,64,4,4096]{3,2,0,1:T(4,128)(2,1)}), bf16[2,64,4,4096]{3,2,0,1:T(4,128)(2,1)}, u32[]{:S(2)}, u32[]{:S(2)}) async-start(bf16[2,64,4,4096]{3,2,0,1:T(4,128)(2,1)} %copy.146), calls=%async_computation.1 | async-start | bytes 8388608 | tf_op jit(solution)/shard_map/all_to_all | solution.py:56
  125.1 0.6 copy-start.36
  227.9 7.2 copy-start.28
  235.1 7.2 copy-start.2
  258.3 1.3 copy-start.26
  259.2 5.5 copy-start.25
  259.6 5.7 copy-start.24
  260.0 5.6 copy-start.22
  260.4 5.5 copy-start.21
  260.8 5.7 copy-start.18
  261.1 5.6 copy-start.15
  261.5 5.5 copy-start.14
  261.9 5.4 copy-start.11
  262.4 6.5 copy-start.5
  262.8 5.9 copy-start.9
  263.2 5.2 copy-start.12
  263.6 4.6 copy-start.16
  263.6 1.5 copy-start.29
  263.9 3.9 copy-start.19
  264.3 4.1 copy-start.23
  265.1 4.4 copy-start.7
  275.8 4.6 copy-start.3
  304.2 101.8 %all-to-all-start.2 = ((bf16[2,64,4,4096]{3,2,0,1:T(4,128)(2,1)}), bf16[2,64,4,4096]{3,2,0,1:T(4,128)(2,1)}, u32[]{:S(2)}, u32[]{:S(2)}) async-start(bf16[2,64,4,4096]{3,2,0,1:T(4,128)(2,1)} %copy.169), calls=%async_computation.2 | async-start | bytes 8388608 | tf_op jit(solution)/shard_map/all_to_all | solution.py:120
  479.3 281.6 %all-to-all-start.3 = ((bf16[64,6,4,4096]{3,2,1,0:T(4,128)(2,1)}), bf16[64,6,4,4096]{3,2,1,0:T(4,128)(2,1)}, u32[]{:S(2)}, u32[]{:S(2)}) async-start(bf16[64,6,4,4096]{3,2,1,0:T(4,128)(2,1)} %broadcast_select_fusion), calls=%async_computation.3 | async-start | bytes 25165824 | tf_op jit(solution)/shard_map/all_to_all | solution.py:138
  485.2 30.9 %copy-start.37 = (bf16[256,32]{0,1:T(8,128)(2,1)S(1)}, bf16[256,32]{0,1:T(8,128)(2,1)}, u32[]{:S(2)}) copy-start(bf16[256,32]{0,1:T(8,128)(2,1)} %copy-done.36) | copy-start | bytes 49156
  485.2 612.0 %all-reduce.6.cloned.1.call-start = ((), (), s32[]{:S(2)}) async-start(), calls=%async_computation.4 | async-start | bytes 25165824
  485.3 17.8 %copy-start.20 = (bf16[256,768]{1,0:T(8,128)(2,1)S(1)}, bf16[256,768]{1,0:T(8,128)(2,1)}, u32[]{:S(2)}) copy-start(bf16[256,768]{1,0:T(8,128)(2,1)} %copy-done.19) | copy-start | bytes 1179652
  485.3 19.7 %copy-start.17 = (bf16[256,768]{1,0:T(8,128)(2,1)S(1)}, bf16[256,768]{1,0:T(8,128)(2,1)}, u32[]{:S(2)}) copy-start(bf16[256,768]{1,0:T(8,128)(2,1)} %copy-done.16) | copy-start | bytes 1179652
  485.3 21.5 %copy-start.13 = (bf16[256,768]{1,0:T(8,128)(2,1)S(1)}, bf16[256,768]{1,0:T(8,128)(2,1)}, u32[]{:S(2)}) copy-start(bf16[256,768]{1,0:T(8,128)(2,1)} %copy-done.12) | copy-start | bytes 1179652
  485.3 23.4 %copy-start.10 = (bf16[256,768]{1,0:T(8,128)(2,1)S(1)}, bf16[256,768]{1,0:T(8,128)(2,1)}, u32[]{:S(2)}) copy-start(bf16[256,768]{1,0:T(8,128)(2,1)} %copy-done.9) | copy-start | bytes 1179652
  485.3 25.2 %copy-start.6 = (bf16[256,768]{1,0:T(8,128)(2,1)S(1)}, bf16[256,768]{1,0:T(8,128)(2,1)}, u32[]{:S(2)}) copy-start(bf16[256,768]{1,0:T(8,128)(2,1)} %copy-done.5) | copy-start | bytes 1179652
  485.3 27.1 %copy-start.8 = (bf16[256,768]{1,0:T(8,128)(2,1)S(1)}, bf16[256,768]{1,0:T(8,128)(2,1)}, u32[]{:S(2)}) copy-start(bf16[256,768]{1,0:T(8,128)(2,1)} %copy-done.7) | copy-start | bytes 1179652
  786.7 5.4 copy-start.35
  786.7 6.8 copy-start.33
  786.7 7.9 copy-start.31
  792.1 1.4 copy-start.1
  794.6 10.2 copy-start.4
  814.5 1.2 copy-start.27
Sparse Core Ops, SparseCore 0:
  814.6 282.5 all-reduce.5
where the time goes:
time: 1110 us
  waiting for transfers between devices  743 us (67%)
  local copies, waits for them, and re-layouts  174 us (16%)
  matrix products  88.8 us (8%)
  other arithmetic  54.9 us (5%)
  starting transfers between devices  31.9 us (3%)
  between operations  15.2 us (1%)
    unnamed x2, waiting for transfers between devices  276 us
    all_to_all x1, waiting for transfers between devices, shards(): lax.all_to_all(slot_rows, 'ctx', split_axis=0, concat_axis=0, tiled=True)  241 us
    all_to_all x1, waiting for transfers between devices, shards(): lax.all_to_all(remote, 'ctx', split_axis=1, concat_axis=1, tiled=True)  94.6 us
    all_to_all x1, waiting for transfers between devices, shards(): lax.all_to_all(picked, 'ctx', split_axis=1, concat_axis=1, tiled=True)  80.5 us
    gather x2, local copies, waits for them, and re-layouts, shards(): jnp.take(padded, source_row, axis=0)  52.2 us
    all_to_all x1, waiting for transfers between devices, shards(): lax.all_to_all(packed.reshape(block_count, slice_rows, 2 * feat_width), '...  50.9 us
    dot_general x16, matrix products, shards(): jnp.dot(dscores, key_head, preferred_element_type=jnp.float32)  30.7 us
  transfers between devices with their start and end apart: 5, of which 5 were waited for; matrix products, arithmetic and copies ran while one was open for 5% of the time, Pallas kernels for 0%

commit v1 on v0

v1 whole, which is shorter than its diff:
```python
import functools
import math

import jax
import jax.numpy as jnp
from jax import lax
from jax.experimental import pallas as pl
from jax.experimental.pallas import tpu as pltpu
from jax.sharding import PartitionSpec as P

BLK = 256
HD = 128
HEADS = 16
HQ = HEADS * HD
D = 4096
R = 32
ADAPTER_SCALE = 0.5
SCORE_SCALE = HD ** -0.5
LOG2_SCALE = SCORE_SCALE * math.log2(math.e)
GRAD_SCALE = (4 * 16384) ** -0.5
VMEM_BYTES = 50 * 1024 * 1024
NT = (((1,), (1,)), ((), ()))
TN = (((0,), (0,)), ((), ()))
TILES = 32


def place(y, z, core):
    return (y * 8 + z) * 2 + core


def group_row(half, low):
    return low if half == 0 else 3 - low


HEAD_GROUPS = [
    [place(group_row(half, low), z, core) for low in range(2) for z in range(8)]
    for half in range(2)
    for core in range(2)
]
TILE_GROUPS = [[place(y, z, core) for y in range(4) for z in range(8)] for core in range(2)]
CORE_PAIRS = [(i, i ^ 1) for i in range(64)]
TO_LATER = [(place(y, z, c), place(3 - y, z, c)) for y in range(2) for z in range(8) for c in range(2)]
TO_EARLIER = [(b, a) for a, b in TO_LATER]


def to_heads(x):
    return lax.all_to_all(x, "ctx", 0, 0, axis_index_groups=HEAD_GROUPS, tiled=True)


def field_kernel(tok_ref, proj_ref, down_ref, up_ref, out_ref, low_ref, low_s):
    @pl.when(pl.program_id(0) == 0)
    def _():
        low = jnp.dot(tok_ref[...], down_ref[0], preferred_element_type=jnp.float32)
        low_s[...] = low.astype(jnp.bfloat16)
        low_ref[...] = low.astype(jnp.bfloat16)

    adapter = jnp.dot(low_s[...], up_ref[0], preferred_element_type=jnp.float32)
    field = (proj_ref[...].astype(jnp.float32) + ADAPTER_SCALE * adapter).astype(jnp.bfloat16)
    for h in range(4):
        out_ref[h] = field[:, h * HD : (h + 1) * HD]


def make_field(tokens, projected, down_proj, up_projection, m):
    return pl.pallas_call(
        field_kernel,
        grid=(4,),
        in_specs=[
            pl.BlockSpec((BLK, D), lambda i: (0, 0)),
            pl.BlockSpec((BLK, 512), lambda i: (0, m * 4 + i)),
            pl.BlockSpec((1, D, R), lambda i: (m, 0, 0)),
            pl.BlockSpec((1, R, 512), lambda i: (m, 0, i)),
        ],
        out_specs=[
            pl.BlockSpec((4, BLK, HD), lambda i: (i, 0, 0)),
            pl.BlockSpec((BLK, R), lambda i: (0, 0)),
        ],
        out_shape=[
            jax.ShapeDtypeStruct((HEADS, BLK, HD), jnp.bfloat16),
            jax.ShapeDtypeStruct((BLK, R), jnp.bfloat16),
        ],
        scratch_shapes=[pltpu.VMEM((BLK, R), jnp.bfloat16)],
        compiler_params=pltpu.CompilerParams(vmem_limit_bytes=24 * 1024 * 1024),
        cost_estimate=pl.CostEstimate(
            flops=2 * BLK * D * R + 2 * BLK * R * HQ, bytes_accessed=6 * 2**20, transcendentals=0
        ),
        name="field_%d" % m,
    )(tokens, projected, down_proj, up_projection)


def stored_at(block, half, core):
    y = block >> 4
    block_half = y >> 1
    row = jnp.where(block_half == 0, y, 3 - y)
    source = jnp.where(block_half == half, 0, 2) + jnp.where((block & 1) == core, 0, 1)
    return source * 16 + row * 8 + ((block >> 1) & 7)


def slots_of(ids_ref, me_ref, p):
    me = me_ref[0]
    core = me & 1
    half = me >> 5
    low = p >> 3
    y = jnp.where(half == 0, low, 3 - low)
    own = (y * 8 + (p & 7)) * 2 + core
    found = []
    for t in (1, 2):
        block = ids_ref[own * 3 + t]
        bias = jnp.where(block == own, -jnp.inf, 0.0).astype(jnp.float32)
        found.append((stored_at(block, half, core), bias))
    return found


def load_all(sources, targets, sem):
    copies = []
    for source, target in zip(sources, targets):
        for j, ref in enumerate(source):
            copies.append(
                pltpu.make_async_copy(ref, target.at[pl.ds(j * 16, 16)], sem.at[len(copies)])
            )
    for copy in copies:
        copy.start()
    for copy in copies:
        copy.wait()


def transposed_scores(q, keys, biases):
    key_row = lax.broadcasted_iota(jnp.int32, (BLK, BLK), 0)
    query_col = lax.broadcasted_iota(jnp.int32, (BLK, BLK), 1)
    scores = []
    for t in range(3):
        s = lax.dot_general(keys[t], q, NT, preferred_element_type=jnp.float32) * LOG2_SCALE
        if t == 0:
            s = jnp.where(key_row <= query_col, s, -jnp.inf)
        else:
            s = s + biases[t - 1]
        scores.append(s)
    return scores


def forward_kernel(ids_ref, me_ref, q_ref, k0, k1, k2, k3, v0, v1, v2, v3, attn_ref, stat_ref, ks, vs, sem):
    p = pl.program_id(0)

    @pl.when(p == 0)
    def _():
        load_all(((k0, k1, k2, k3), (v0, v1, v2, v3)), (ks, vs), sem)

    (at1, bias1), (at2, bias2) = slots_of(ids_ref, me_ref, p)
    spots = (p, at1, at2)
    scores = transposed_scores(q_ref[0], [ks[i] for i in spots], (bias1, bias2))
    top = jnp.max(jnp.maximum(jnp.maximum(scores[0], scores[1]), scores[2]), axis=0, keepdims=True)
    shifted = [jnp.exp2(s - top) for s in scores]
    inverse = 1.0 / jnp.sum(shifted[0] + shifted[1] + shifted[2], axis=0, keepdims=True)
    out = None
    for t in range(3):
        weights = (shifted[t] * inverse).astype(jnp.bfloat16)
        part = lax.dot_general(vs[spots[t]], weights, TN, preferred_element_type=jnp.float32)
        out = part if out is None else out + part
    attn_ref[0] = out.T.astype(jnp.bfloat16)
    stat_ref[0] = jnp.concatenate([top, inverse, jnp.zeros((6, BLK), jnp.float32)], axis=0)


def backward_kernel(
    ids_ref, me_ref, q_ref, g_ref, attn_ref, stat_ref, k0, k1, k2, k3, v0, v1, v2, v3,
    dq_ref, own_k, own_v, core_k, core_v, far_k, far_v, farcore_k, farcore_v,
    ks, vs, acc_k, acc_v, staged, sem,
):
    p = pl.program_id(0)

    @pl.when(p == 0)
    def _():
        def clear(i, _):
            acc_k[i] = jnp.zeros((BLK, HD), jnp.float32)
            acc_v[i] = jnp.zeros((BLK, HD), jnp.float32)
            return 0

        lax.fori_loop(0, 64, clear, 0)
        load_all(((k0, k1, k2, k3), (v0, v1, v2, v3)), (ks, vs), sem)

    (at1, bias1), (at2, bias2) = slots_of(ids_ref, me_ref, p)
    spots = (p, at1, at2)
    q = q_ref[0]
    g = g_ref[0]
    keys = [ks[i] for i in spots]
    scores = transposed_scores(q, keys, (bias1, bias2))
    top = stat_ref[0, 0:1, :]
    inverse = stat_ref[0, 1:2, :]
    product = attn_ref[0].astype(jnp.float32) * g.astype(jnp.float32)
    delta = jnp.sum(product.T, axis=0, keepdims=True)
    dq = None
    for t in range(3):
        probs = jnp.exp2(scores[t] - top) * inverse
        weights = probs.astype(jnp.bfloat16)
        dprobs = lax.dot_general(vs[spots[t]], g, NT, preferred_element_type=jnp.float32)
        dscores = (probs * (dprobs - delta) * SCORE_SCALE).astype(jnp.bfloat16)
        part = lax.dot_general(keys[t], dscores, TN, preferred_element_type=jnp.float32)
        dq = part if dq is None else dq + part
        dk = jnp.dot(dscores, q, preferred_element_type=jnp.float32)
        dv = jnp.dot(weights, g, preferred_element_type=jnp.float32)
        if t > 0:
            dk = dk.astype(jnp.bfloat16).astype(jnp.float32)
            dv = dv.astype(jnp.bfloat16).astype(jnp.float32)
        acc_k[spots[t]] += dk
        acc_v[spots[t]] += dv
    dq_ref[0] = dq.T.astype(jnp.bfloat16)

    @pl.when(p == 15)
    def _():
        copies = []

        def send(source, target):
            copy = pltpu.make_async_copy(source, target, sem.at[len(copies)])
            copy.start()
            copies.append(copy)

        send(acc_k.at[pl.ds(0, 16)], own_k)
        send(acc_v.at[pl.ds(0, 16)], own_v)
        send(acc_k.at[pl.ds(32, 16)], far_k)
        send(acc_v.at[pl.ds(32, 16)], far_v)

        for n, (acc, at) in enumerate(((acc_k, 48), (acc_v, 48), (acc_k, 16), (acc_v, 16))):
            def cast(i, _, n=n, acc=acc, at=at):
                staged[n * 16 + i] = acc[at + i].astype(jnp.bfloat16)
                return 0

            lax.fori_loop(0, 16, cast, 0)
            send(staged.at[pl.ds(n * 16, 16)], (farcore_k, farcore_v, core_k, core_v)[n])
        for copy in copies:
            copy.wait()


ANY = pl.BlockSpec(memory_space=pl.ANY)


def one_block(rows=BLK, width=HD):
    return pl.BlockSpec((1, rows, width), lambda p, *_: (p, 0, 0))


def blocks_of(kind):
    return jax.ShapeDtypeStruct((16, BLK, HD), kind)


def attend_forward(ids, me, q, keys, values):
    return pl.pallas_call(
        forward_kernel,
        grid_spec=pltpu.PrefetchScalarGridSpec(
            num_scalar_prefetch=2,
            grid=(16,),
            in_specs=[one_block()] + [ANY] * 8,
            out_specs=[one_block(), one_block(8, BLK)],
            scratch_shapes=[
                pltpu.VMEM((64, BLK, HD), jnp.bfloat16),
                pltpu.VMEM((64, BLK, HD), jnp.bfloat16),
                pltpu.SemaphoreType.DMA((8,)),
            ],
        ),
        out_shape=[blocks_of(jnp.bfloat16), jax.ShapeDtypeStruct((16, 8, BLK), jnp.float32)],
        compiler_params=pltpu.CompilerParams(vmem_limit_bytes=VMEM_BYTES),
        cost_estimate=pl.CostEstimate(
            flops=16 * 2 * 2 * BLK * 3 * BLK * HD, bytes_accessed=11 * 2**20, transcendentals=16 * 3 * BLK * BLK
        ),
        name="attend_forward",
    )(ids, me, q, *keys, *values)


def attend_backward(ids, me, q, g, attn, stats, keys, values):
    wide = blocks_of(jnp.float32)
    narrow = blocks_of(jnp.bfloat16)
    return pl.pallas_call(
        backward_kernel,
        grid_spec=pltpu.PrefetchScalarGridSpec(
            num_scalar_prefetch=2,
            grid=(16,),
            in_specs=[one_block(), one_block(), one_block(), one_block(8, BLK)] + [ANY] * 8,
            out_specs=[one_block()] + [ANY] * 8,
            scratch_shapes=[
                pltpu.VMEM((64, BLK, HD), jnp.bfloat16),
                pltpu.VMEM((64, BLK, HD), jnp.bfloat16),
                pltpu.VMEM((64, BLK, HD), jnp.float32),
                pltpu.VMEM((64, BLK, HD), jnp.float32),
                pltpu.VMEM((64, BLK, HD), jnp.bfloat16),
                pltpu.SemaphoreType.DMA((8,)),
            ],
        ),
        out_shape=[narrow, wide, wide, narrow, narrow, wide, wide, narrow, narrow],
        compiler_params=pltpu.CompilerParams(vmem_limit_bytes=VMEM_BYTES),
        cost_estimate=pl.CostEstimate(
            flops=16 * 5 * 2 * BLK * 3 * BLK * HD, bytes_accessed=24 * 2**20, transcendentals=16 * 3 * BLK * BLK
        ),
        name="attend_backward",
    )(ids, me, q, g, attn, stats, *keys, *values)


def grads_kernel(first, me_ref, *refs):
    if first:
        g_ref, tok_ref, low_ref, up_ref, gp_ref, keep_ref, send_ref, terms = refs
    else:
        _, g_ref, tok_ref, low_ref, up_ref, gp_ref, keep_ref, send_ref, terms = refs
    dlow = None
    low = low_ref[...]
    for h in range(HEADS):
        g = g_ref[h]
        cols = slice(h * HD, (h + 1) * HD)
        gp_ref[:, cols] = g
        part = lax.dot_general(up_ref[0, :, cols], g, NT, preferred_element_type=jnp.float32)
        dlow = part if dlow is None else dlow + part
        up_term = jnp.dot(low, g, preferred_element_type=jnp.float32) * (ADAPTER_SCALE * GRAD_SCALE)
        for side in range(2):
            cut = up_term[:, side * 64 : (side + 1) * 64]
            terms[2 * h + side, 32:48, :] = jnp.concatenate([cut[0:16], cut[16:32]], axis=1)
    dlow = (dlow * ADAPTER_SCALE).astype(jnp.bfloat16)
    for t in range(TILES):
        down_term = jnp.dot(dlow, tok_ref[:, t * 128 : (t + 1) * 128], preferred_element_type=jnp.float32)
        terms[t, 0:32, :] = down_term * GRAD_SCALE
    core = me_ref[0] & 1

    @pl.when(core == 0)
    def _():
        keep_ref[...] = terms[:, 0:24, :]
        send_ref[...] = terms[:, 24:48, :]

    @pl.when(core == 1)
    def _():
        keep_ref[...] = terms[:, 24:48, :]
        send_ref[...] = terms[:, 0:24, :]


def member_grads(me, grad_proj, g, tokens, low, up_projection, m):
    first = grad_proj is None
    piece = jax.ShapeDtypeStruct((TILES, 24, 128), jnp.float32)
    whole = lambda *shape: pl.BlockSpec(shape, lambda i, *_: (0,) * len(shape))
    in_specs = [
        whole(HEADS, BLK, HD),
        whole(BLK, D),
        whole(R, BLK),
        pl.BlockSpec((1, R, HQ), lambda i, *_: (m, 0, 0)),
    ]
    operands = [g, tokens, low, up_projection]
    if not first:
        in_specs = [ANY] + in_specs
        operands = [grad_proj] + operands
    return pl.pallas_call(
        functools.partial(grads_kernel, first),
        grid_spec=pltpu.PrefetchScalarGridSpec(
            num_scalar_prefetch=1,
            grid=(1,),
            in_specs=in_specs,
            out_specs=[
                pl.BlockSpec((BLK, HQ), lambda i, *_: (0, m)),
                whole(TILES, 24, 128),
                whole(TILES, 24, 128),
            ],
            scratch_shapes=[pltpu.VMEM((TILES, 48, 128), jnp.float32)],
        ),
        out_shape=[jax.ShapeDtypeStruct((BLK, 3 * HQ), jnp.bfloat16), piece, piece],
        input_output_aliases={} if first else {1: 0},
        compiler_params=pltpu.CompilerParams(vmem_limit_bytes=24 * 1024 * 1024),
        cost_estimate=pl.CostEstimate(
            flops=2 * BLK * R * (D + 2 * HQ), bytes_accessed=5 * 2**20, transcendentals=0
        ),
        name="grads_%d" % m,
    )(me, *operands)


def shards(tokens, projected, down_proj, up_projection, block_ids, cotangent):
    tokens = tokens[0]
    projected = projected[0]
    me = lax.axis_index("ctx").astype(jnp.int32)
    core = me & 1
    lane = core * 4 + lax.axis_index("dp")
    me = me.reshape(1)
    ids = block_ids[0].reshape(-1)

    swap = lambda x: lax.ppermute(x, "ctx", CORE_PAIRS)
    later = lambda x: lax.ppermute(x, "ctx", TO_LATER)
    earlier = lambda x: lax.ppermute(x, "ctx", TO_EARLIER)

    field_k, low_k = make_field(tokens, projected, down_proj, up_projection, 1)
    field_v, low_v = make_field(tokens, projected, down_proj, up_projection, 2)
    field_q, low_q = make_field(tokens, projected, down_proj, up_projection, 0)
    grad_heads = jnp.transpose(cotangent[0].reshape(BLK, HEADS, HD), (1, 0, 2))

    key = to_heads(field_k)
    field_v, key = lax.optimization_barrier((field_v, key))
    key_far = later(key)
    key_core = swap(key)
    value = to_heads(field_v)
    field_q, value = lax.optimization_barrier((field_q, value))
    value_far = later(value)
    value_core = swap(value)
    query = to_heads(field_q)
    grad_heads, query = lax.optimization_barrier((grad_heads, query))
    keys = (key, key_core, key_far, swap(key_far))
    values = (value, value_core, value_far, swap(value_far))
    grad = to_heads(grad_heads)

    attn, stats = attend_forward(ids, me, query, keys, values)
    dq, own_k, own_v, core_k, core_v, far_k, far_v, farcore_k, farcore_v = attend_backward(
        ids, me, query, grad, attn, stats, keys, values
    )
    attn_home = to_heads(attn)
    dq, attn_home = lax.optimization_barrier((dq, attn_home))
    dq_home = to_heads(dq)

    def gather_parts(own, core_part, far, farcore):
        far_sum = (far + swap(farcore).astype(jnp.float32)).astype(jnp.bfloat16)
        returned = earlier(far_sum)
        total = own + swap(core_part).astype(jnp.float32) + returned.astype(jnp.float32)
        return total.astype(jnp.bfloat16)

    dk = gather_parts(own_k, core_k, far_k, farcore_k)
    dv = gather_parts(own_v, core_v, far_v, farcore_v)
    dk, dq_home = lax.optimization_barrier((dk, dq_home))
    dk_home = to_heads(dk)
    dv, dk_home = lax.optimization_barrier((dv, dk_home))
    dv_home = to_heads(dv)

    attn_rows = jnp.transpose(attn_home, (1, 0, 2)).reshape(BLK, HQ)
    grad_proj, keep_q, send_q = member_grads(me, None, dq_home, tokens, low_q.T, up_projection, 0)
    grad_proj, keep_k, send_k = member_grads(me, grad_proj, dk_home, tokens, low_k.T, up_projection, 1)
    grad_proj, keep_v, send_v = member_grads(me, grad_proj, dv_home, tokens, low_v.T, up_projection, 2)

    pieces = jnp.concatenate(
        [keep_q + swap(send_q), keep_k + swap(send_k), keep_v + swap(send_v)], axis=1
    )
    pieces = lax.all_to_all(pieces, "ctx", 0, 0, axis_index_groups=TILE_GROUPS, tiled=True)
    mine = jnp.sum(pieces, axis=0)
    others = [
        lax.ppermute(mine, "dp", [(j, (j + step) % 4) for j in range(4)]) for step in (1, 2, 3)
    ]
    mine = (mine + others[0]) + (others[1] + others[2])
    other = swap(mine)
    low_rows = jnp.where(core == 0, mine, other).reshape(3, 24, 128)
    high_rows = jnp.where(core == 0, other, mine).reshape(3, 24, 128)
    full = jnp.concatenate([low_rows, high_rows], axis=1)
    down_piece = lax.dynamic_slice_in_dim(full[:, 0:32], lane * 16, 16, axis=2)
    up_low = lax.dynamic_slice_in_dim(full[:, 32:48, 0:64], lane * 8, 8, axis=2)
    up_high = lax.dynamic_slice_in_dim(full[:, 32:48, 64:128], lane * 8, 8, axis=2)
    grad_down = jnp.transpose(down_piece, (0, 2, 1))
    grad_up = jnp.concatenate([up_low, up_high], axis=1)
    return attn_rows[None], grad_proj[None], grad_down, grad_up


def solution(mesh):
    placed = (
        P("dp", "ctx", None),
        P("dp", "ctx", None),
        P(),
        P(),
        P("dp", None, None),
        P("dp", "ctx", None),
    )
    return jax.shard_map(
        shards,
        mesh=mesh,
        in_specs=placed,
        out_specs=(
            P("dp", "ctx", None),
            P("dp", "ctx", None),
            P(None, ("ctx", "dp"), None),
            P(None, None, ("ctx", "dp")),
        ),
        check_vma=False,
    )
```

time: 1110 us -> 365 us (0.33)
  waiting for transfers between devices: 743 us -> 135 us
  local copies, waits for them, and re-layouts: 174 us -> 40.1 us
  matrix products: 88.8 us -> 0 us
  Pallas kernels: 0 us -> 56.7 us
  starting transfers between devices: 31.9 us -> 83.3 us
  other arithmetic: 54.9 us -> 10.3 us
  blocking collectives: 0 us -> 36.5 us
  between operations: 15.2 us -> 1.01 us
    all_to_all x4 -> x8, waiting for transfers between devices: 467 us -> 64.2 us  [to_heads(): lax.all_to_all(x, 'ctx', 0, 0, axis_index_groups=HEAD_GROUPS, tiled=True)]
    unnamed x2 -> x0, waiting for transfers between devices: 276 us -> none
    dot_general x108 -> x0, matrix products: 88.8 us -> none  [the longest x16 30.7 us: shards(): jnp.dot(dscores, key_head, preferred_element_type=jnp.float32)]
    ppermute x0 -> x19, waiting for transfers between devices: none -> 70.6 us  [the longest x2 52.6 us: shards(): earlier = lambda x: lax.ppermute(x, 'ctx', TO_EARLIER)]
    gather x4 -> x0, local copies, waits for them, and re-layouts: 65.8 us -> none  [the longest x2 52.2 us: shards(): jnp.take(padded, source_row, axis=0)]
    pallas_call x0 -> x8, Pallas kernels: none -> 56.7 us  [the longest x1 25 us: attend_backward(): pl.pallas_call(backward_kernel, grid_spec=pltpu.PrefetchScalarGridSpec(nu...]
    all_to_all x0 -> x1, blocking collectives: none -> 36.5 us  [shards(): lax.all_to_all(pieces, 'ctx', 0, 0, axis_index_groups=TILE_GROUPS, tiled=...]
    all_to_all x4 -> x8, starting transfers between devices: 31.9 us -> 57.6 us  [to_heads(): lax.all_to_all(x, 'ctx', 0, 0, axis_index_groups=HEAD_GROUPS, tiled=True)]
  transfers between devices with their start and end apart: 5 -> 27, of which waited for: 5 -> 10; matrix products, arithmetic and copies ran while one was open for 5% -> 6% of each run, Pallas kernels for 0% -> 15%
where the time goes in v1:
time: 365 us; the launch traced here: 363 us
  waiting for transfers between devices  135 us (37%)
  starting transfers between devices  83.3 us (23%)
  Pallas kernels  56.7 us (16%)
  local copies, waits for them, and re-layouts  40.1 us (11%)
  blocking collectives  36.5 us (10%)
  other arithmetic  10.3 us (3%)
    all_to_all x8, waiting for transfers between devices, to_heads(): lax.all_to_all(x, 'ctx', 0, 0, axis_index_groups=HEAD_GROUPS, tiled=True)  64.2 us
    all_to_all x8, starting transfers between devices, to_heads(): lax.all_to_all(x, 'ctx', 0, 0, axis_index_groups=HEAD_GROUPS, tiled=True)  57.6 us
    ppermute x2, waiting for transfers between devices, shards(): earlier = lambda x: lax.ppermute(x, 'ctx', TO_EARLIER)  52.6 us
    all_to_all x1, blocking collectives, shards(): lax.all_to_all(pieces, 'ctx', 0, 0, axis_index_groups=TILE_GROUPS, tiled=...  36.5 us
    unnamed x61, local copies, waits for them, and re-layouts  31.2 us
    pallas_call x1, Pallas kernels, attend_backward(): pl.pallas_call(backward_kernel, grid_spec=pltpu.PrefetchScalarGridSpec(nu...  25 us
    pallas_call x1, Pallas kernels, attend_forward(): pl.pallas_call(forward_kernel, grid_spec=pltpu.PrefetchScalarGridSpec(num...  17.3 us
    ppermute x2, waiting for transfers between devices, shards(): later = lambda x: lax.ppermute(x, 'ctx', TO_LATER)  14.8 us
  transfers between devices with their start and end apart: 27, of which 10 were waited for; matrix products, arithmetic and copies ran while one was open for 6% of the time, Pallas kernels for 15%

profile of v1, /device:TPU:1, one launch (start us, length us, event | category | flops | bytes accessed | tf_op | source)
XLA Modules:
  0.0 362.7 jit_solution(11108188678943994566)
XLA Ops:
  0.7 3.9 %copy.34.down_ref = bf16[3,4096,32]{2,1,0:T(8,128)(2,1)} copy(bf16[3,4096,32]{1,2,0:T(8,128)(2,1)} %param.8) | data formatting | bytes 1572864 | tf_op args[2]
  4.5 1.9 copy-done.1
  6.4 1.9 copy-done.4
  8.3 1.7 field_1.1
  11.6 10.2 %all-to-all-start = ((bf16[16,256,128]{2,1,0:T(8,128)(2,1)}), bf16[16,256,128]{2,1,0:T(8,128)(2,1)S(1)}, u32[]{:S(2)}, u32[]{:S(2)}) async-start(bf16[16,256,128]{2,1,0:T(8,128)(2,1)} %copy-done.13), calls=%async_computation | async-start | bytes 2097152 | tf_op jit(solution)/shard_map/all_to_all | solution.py:47
  21.8 1.9 copy-done.2
  23.6 1.9 copy-done.5
  25.5 1.7 field_2.1
  28.9 18.5 %all-to-all-done.k0 = bf16[16,256,128]{2,1,0:T(8,128)(2,1)S(1)} async-done(((bf16[16,256,128]{2,1,0:T(8,128)(2,1)}), bf16[16,256,128]{2,1,0:T(8,128)(2,1)S(1)}, u32[]{:S(2)}, u32[]{:S(2)}) %all-to-all-start) | async-done | bytes 1048608 | tf_op jit(solution)/shard_map/all_to_all | solution.py:47
  47.4 6.0 %all-to-all-start.1 = ((bf16[16,256,128]{2,1,0:T(8,128)(2,1)}), bf16[16,256,128]{2,1,0:T(8,128)(2,1)}, u32[]{:S(2)}, u32[]{:S(2)}) async-start(bf16[16,256,128]{2,1,0:T(8,128)(2,1)} %copy-done.12), calls=%async_computation.1 | async-start | bytes 2097152 | tf_op jit(solution)/shard_map/all_to_all | solution.py:47
  53.5 1.9 copy-done.3
  55.4 1.9 copy-done.6
  57.3 1.7 field_0.1
  60.5 18.5 %all-to-all-done.1.v0 = bf16[16,256,128]{2,1,0:T(8,128)(2,1)} async-done(((bf16[16,256,128]{2,1,0:T(8,128)(2,1)}), bf16[16,256,128]{2,1,0:T(8,128)(2,1)}, u32[]{:S(2)}, u32[]{:S(2)}) %all-to-all-start.1) | async-done | bytes 1048608 | tf_op jit(solution)/shard_map/all_to_all | solution.py:47
  79.0 6.2 %all-to-all-start.2 = ((bf16[16,256,128]{2,1,0:T(8,128)(2,1)}), bf16[16,256,128]{2,1,0:T(8,128)(2,1)}, u32[]{:S(2)}, u32[]{:S(2)}) async-start(bf16[16,256,128]{2,1,0:T(8,128)(2,1)} %copy-done.11), calls=%async_computation.2 | async-start | bytes 2097152 | tf_op jit(solution)/shard_map/all_to_all | solution.py:47
  85.2 4.8 %collective-permute-start.1 = (bf16[16,256,128]{2,1,0:T(8,128)(2,1)S(1)}, bf16[16,256,128]{2,1,0:T(8,128)(2,1)}, u32[]{:S(2)}, u32[]{:S(2)}) collective-permute-start(bf16[16,256,128]{2,1,0:T(8,128)(2,1)S(1)} %all-to-all-done.k0), channel_id=1, source_target_pairs={{0,192},{4,196},{8,200},{12,204},{16,208},{20,212},{24,216},{28,22... | collective-permute-start | bytes 3145736 | tf_op jit(solution)/shard_map/ppermute | solution.py:374
  90.0 2.3 collective-permute-start.4
  92.3 2.3 copy.32
  94.6 2.3 copy.33
  96.9 13.9 %all-to-all-done.2.q_ref = bf16[16,256,128]{2,1,0:T(8,128)(2,1)} async-done(((bf16[16,256,128]{2,1,0:T(8,128)(2,1)}), bf16[16,256,128]{2,1,0:T(8,128)(2,1)}, u32[]{:S(2)}, u32[]{:S(2)}) %all-to-all-start.2) | async-done | bytes 1048608 | tf_op jit(solution)/shard_map/all_to_all | solution.py:47
  110.8 6.2 %all-to-all-start.3 = ((bf16[16,256,128]{2,1,0:T(8,128)(2,1)}), bf16[16,256,128]{2,1,0:T(8,128)(2,1)}, u32[]{:S(2)}, u32[]{:S(2)}) async-start(bf16[16,256,128]{2,1,0:T(8,128)(2,1)} %bitcast.28), calls=%async_computation.3 | async-start | bytes 2097152 | tf_op jit(solution)/shard_map/all_to_all | solution.py:47
  118.5 14.8 %collective-permute-done.4.v2 = bf16[16,256,128]{2,1,0:T(8,128)(2,1)} collective-permute-done((bf16[16,256,128]{2,1,0:T(8,128)(2,1)}, bf16[16,256,128]{2,1,0:T(8,128)(2,1)}, u32[]{:S(2)}, u32[]{:S(2)}) %collective-permute-start.4) | collective-permute-done | bytes 1048608 | tf_op jit(solution)/shard_map/ppermute | solution.py:374
  133.3 1.7 collective-permute-start.5
  137.6 17.3 %attend_forward.1 = (bf16[16,256,128]{2,1,0:T(8,128)(2,1)S(1)}, f32[16,8,256]{2,1,0:T(8,128)S(1)}) custom-call(s32[192]{0:T(256)S(1)} %reshape_squeeze.6.ids_ref, s32[1]{0:T(128)} %bitcast.me_ref, bf16[16,256,128]{2,1,0:T(8,128)(2,1)} %all-to-all-done.2.q_ref, bf16[16,256,128]{2,1,0:T(8,128)(2,1)S(1)} %all-to-all-done.k0, ...), custom_call_target="tpu_custom_call" | custom-call | flops 1610612736 | bytes 11534336 | tf_op jit(solution)/shard_map/attend_forward/pallas_call | solution.py:243
  156.5 7.1 %all-to-all-start.4 = ((bf16[16,256,128]{2,1,0:T(8,128)(2,1)}), bf16[16,256,128]{2,1,0:T(8,128)(2,1)}, u32[]{:S(2)}, u32[]{:S(2)}) async-start(bf16[16,256,128]{2,1,0:T(8,128)(2,1)} %copy-done.10), calls=%async_computation.4 | async-start | bytes 2097152 | tf_op jit(solution)/shard_map/all_to_all | solution.py:47
  163.6 25.0 %attend_backward.1 = (bf16[16,256,128]{2,1,0:T(8,128)(2,1)S(1)}, f32[16,256,128]{2,1,0:T(8,128)}, f32[16,256,128]{2,1,0:T(8,128)}, bf16[16,256,128]{2,1,0:T(8,12...) custom-call(s32[192]{0:T(256)S(1)} %reshape_squeeze.6.ids_ref, ...), custom_call_target="tpu_custom_call" | custom-call | flops 4026531840 | bytes 25165824 | tf_op jit(solution)/shard_map/attend_backward/pallas_call | solution.py:268
  192.2 7.8 %all-to-all-start.5 = ((bf16[16,256,128]{2,1,0:T(8,128)(2,1)}), bf16[16,256,128]{2,1,0:T(8,128)(2,1)S(1)}, u32[]{:S(2)}, u32[]{:S(2)}) async-start(bf16[16,256,128]{2,1,0:T(8,128)(2,1)} %copy-done.9), calls=%async_computation.5 | async-start | bytes 2097152 | tf_op jit(solution)/shard_map/all_to_all | solution.py:47
  200.4 2.3 add_convert_fusion.3
  204.3 26.0 %collective-permute-done.8 = bf16[16,256,128]{2,1,0:T(8,128)(2,1)S(1)} collective-permute-done((bf16[16,256,128]{2,1,0:T(8,128)(2,1)S(1)}, bf16[16,256,128]{2,1,0:T(8,128)(2,1)S(1)}, u32[]{:S(2)}, u32[]{:S(2)}) %collective-permute-start.8) | collective-permute-done | bytes 1048608 | tf_op jit(solution)/shard_map/ppermute | solution.py:375
  230.3 1.3 add_convert_fusion.2
  231.7 7.5 %all-to-all-start.6 = ((bf16[16,256,128]{2,1,0:T(8,128)(2,1)}), bf16[16,256,128]{2,1,0:T(8,128)(2,1)}, u32[]{:S(2)}, u32[]{:S(2)}) async-start(bf16[16,256,128]{2,1,0:T(8,128)(2,1)} %add_convert_fusion.2), calls=%async_computation.6 | async-start | bytes 2097152 | tf_op jit(solution)/shard_map/all_to_all | solution.py:47
  240.3 2.3 add_convert_fusion.1
  243.9 26.6 %collective-permute-done.11 = bf16[16,256,128]{2,1,0:T(8,128)(2,1)S(1)} collective-permute-done((bf16[16,256,128]{2,1,0:T(8,128)(2,1)S(1)}, bf16[16,256,128]{2,1,0:T(8,128)(2,1)S(1)}, u32[]{:S(2)}, u32[]{:S(2)}) %collective-permute-start.11) | collective-permute-done | bytes 1048608 | tf_op jit(solution)/shard_map/ppermute | solution.py:375
  270.4 1.4 add_convert_fusion
  271.8 6.7 %all-to-all-start.7 = ((bf16[16,256,128]{2,1,0:T(8,128)(2,1)}), bf16[16,256,128]{2,1,0:T(8,128)(2,1)}, u32[]{:S(2)}, u32[]{:S(2)}) async-start(bf16[16,256,128]{2,1,0:T(8,128)(2,1)} %add_convert_fusion), calls=%async_computation.7 | async-start | bytes 2097152 | tf_op jit(solution)/shard_map/all_to_all | solution.py:47
  278.5 1.5 copy.38
  280.0 1.5 copy.39
  283.2 2.4 grads_0.1
  287.4 3.5 grads_1.1
  290.9 13.3 %all-to-all-done.7.refs_1_ = bf16[16,256,128]{2,1,0:T(8,128)(2,1)} async-done(((bf16[16,256,128]{2,1,0:T(8,128)(2,1)}), bf16[16,256,128]{2,1,0:T(8,128)(2,1)}, u32[]{:S(2)}, u32[]{:S(2)}) %all-to-all-start.7) | async-done | bytes 1048608 | tf_op jit(solution)/shard_map/all_to_all | solution.py:47
  304.1 3.5 grads_2.1
  307.7 2.2 collective-permute-start.14
  312.2 36.5 %all_to_all.45 = f32[32,72,128]{2,1,0:T(8,128)S(1)} all-to-all(f32[32,72,128]{2,1,0:T(8,128)S(1)} %pad_maximum_fusion), channel_id=1, replica_groups={{0,8,16,24,32,40,48,56,64,72,80,88,96,104,112,120,128,136,144,152,160,1..., dimensions={0} | all-to-all | bytes 2359296 | tf_op jit(solution)/shard_map/all_to_all | solution.py:425
  350.0 2.5 collective-permute-start.16
  354.4 1.4 collective-permute-done.17
  355.8 2.2 collective-permute-start.18
  358.0 1.5 copy.37
  359.5 1.4 copy.43
  (99 shorter events, 29.3 us)
Async XLA Ops:
  0.6 3.9 %copy-start = (bf16[1,256,4096]{2,1,0:T(8,128)(2,1)S(1)}, bf16[1,256,4096]{2,1,0:T(8,128)(2,1)}, u32[]{:S(2)}) copy-start(bf16[1,256,4096]{2,1,0:T(8,128)(2,1)} %param.6) | copy-start | bytes 6291460
  0.6 3.9 %copy-start.7 = (bf16[3,32,2048]{2,1,0:T(8,128)(2,1)S(1)}, bf16[3,32,2048]{2,1,0:T(8,128)(2,1)}, u32[]{:S(2)}) copy-start(bf16[3,32,2048]{2,1,0:T(8,128)(2,1)} %refs_4_.3) | copy-start | bytes 1179652
  4.5 1.9 copy-start.1
  6.4 1.9 copy-start.4
  10.0 1.0 copy-start.13
  11.6 35.8 %all-to-all-start = ((bf16[16,256,128]{2,1,0:T(8,128)(2,1)}), bf16[16,256,128]{2,1,0:T(8,128)(2,1)S(1)}, u32[]{:S(2)}, u32[]{:S(2)}) async-start(bf16[16,256,128]{2,1,0:T(8,128)(2,1)} %copy-done.13), calls=%async_computation | async-start | bytes 2097152 | tf_op jit(solution)/shard_map/all_to_all | solution.py:47
  21.8 1.9 copy-start.2
  23.6 1.9 copy-start.5
  27.2 1.0 copy-start.12
  47.4 90.2 %copy-start.8 = (bf16[16,256,128]{2,1,0:T(8,128)(2,1)}, bf16[16,256,128]{2,1,0:T(8,128)(2,1)S(1)}, u32[]{:S(2)}) copy-start(bf16[16,256,128]{2,1,0:T(8,128)(2,1)S(1)} %all-to-all-done.k0) | copy-start | bytes 3145732
  47.4 31.6 %all-to-all-start.1 = ((bf16[16,256,128]{2,1,0:T(8,128)(2,1)}), bf16[16,256,128]{2,1,0:T(8,128)(2,1)}, u32[]{:S(2)}, u32[]{:S(2)}) async-start(bf16[16,256,128]{2,1,0:T(8,128)(2,1)} %copy-done.12), calls=%async_computation.1 | async-start | bytes 2097152 | tf_op jit(solution)/shard_map/all_to_all | solution.py:47
  53.5 1.9 copy-start.3
  55.4 1.9 copy-start.6
  58.9 1.0 copy-start.11
  79.0 31.8 %all-to-all-start.2 = ((bf16[16,256,128]{2,1,0:T(8,128)(2,1)}), bf16[16,256,128]{2,1,0:T(8,128)(2,1)}, u32[]{:S(2)}, u32[]{:S(2)}) async-start(bf16[16,256,128]{2,1,0:T(8,128)(2,1)} %copy-done.11), calls=%async_computation.2 | async-start | bytes 2097152 | tf_op jit(solution)/shard_map/all_to_all | solution.py:47
  85.2 32.7 %collective-permute-start.1 = (bf16[16,256,128]{2,1,0:T(8,128)(2,1)S(1)}, bf16[16,256,128]{2,1,0:T(8,128)(2,1)}, u32[]{:S(2)}, u32[]{:S(2)}) collective-permute-start(bf16[16,256,128]{2,1,0:T(8,128)(2,1)S(1)} %all-to-all-done.k0), channel_id=1, source_target_pairs={{0,192},{4,196},{8,200},{12,204},{16,208},{20,212},{24,216},{28,22... | collective-permute-start | bytes 3145736 | tf_op jit(solution)/shard_map/ppermute | solution.py:374
  90.0 43.2 %collective-permute-start.4 = (bf16[16,256,128]{2,1,0:T(8,128)(2,1)}, bf16[16,256,128]{2,1,0:T(8,128)(2,1)}, u32[]{:S(2)}, u32[]{:S(2)}) collective-permute-start(bf16[16,256,128]{2,1,0:T(8,128)(2,1)} %all-to-all-done.1.v0), channel_id=1, source_target_pairs={{0,192},{4,196},{8,200},{12,204},{16,208},{20,212},{24,216},{28,22... | collective-permute-start | bytes 3145736 | tf_op jit(solution)/shard_map/ppermute | solution.py:374
  94.6 40.4 %copy-start.27 = (s32[1,64,3]{1,0,2:T(1,128)S(1)}, s32[1,64,3]{1,0,2:T(1,128)}, u32[]{:S(2)}) copy-start(s32[1,64,3]{1,0,2:T(1,128)} %param.10) | copy-start | bytes 2308
  110.8 45.7 %all-to-all-start.3 = ((bf16[16,256,128]{2,1,0:T(8,128)(2,1)}), bf16[16,256,128]{2,1,0:T(8,128)(2,1)}, u32[]{:S(2)}, u32[]{:S(2)}) async-start(bf16[16,256,128]{2,1,0:T(8,128)(2,1)} %bitcast.28), calls=%async_computation.3 | async-start | bytes 2097152 | tf_op jit(solution)/shard_map/all_to_all | solution.py:47
  117.0 19.6 %collective-permute-start = (bf16[16,256,128]{2,1,0:T(8,128)(2,1)S(1)}, bf16[16,256,128]{2,1,0:T(8,128)(2,1)}, u32[]{:S(2)}, u32[]{:S(2)}) collective-permute-start(bf16[16,256,128]{2,1,0:T(8,128)(2,1)S(1)} %all-to-all-done.k0), channel_id=1, source_target_pairs={{0,4},{4,0},{8,12},{12,8},{16,20},{20,16},{24,28},{28,24},{32,36},... | collective-permute-start | bytes 3145736 | tf_op jit(solution)/shard_map/ppermute | solution.py:373
  117.9 18.7 %collective-permute-start.2 = (bf16[16,256,128]{2,1,0:T(8,128)(2,1)}, bf16[16,256,128]{2,1,0:T(8,128)(2,1)}, u32[]{:S(2)}, u32[]{:S(2)}) collective-permute-start(bf16[16,256,128]{2,1,0:T(8,128)(2,1)} %collective-permute-done.1.k2), channel_id=1, source_target_pairs={{0,4},{4,0},{8,12},{12,8},{16,20},{20,16},{24,28},{28,24},{32,36},... | collective-permute-start | bytes 3145736 | tf_op jit(solution)/shard_map/ppermute | solution.py:373
  118.1 18.6 %collective-permute-start.3 = (bf16[16,256,128]{2,1,0:T(8,128)(2,1)}, bf16[16,256,128]{2,1,0:T(8,128)(2,1)}, u32[]{:S(2)}, u32[]{:S(2)}) collective-permute-start(bf16[16,256,128]{2,1,0:T(8,128)(2,1)} %all-to-all-done.1.v0), channel_id=1, source_target_pairs={{0,4},{4,0},{8,12},{12,8},{16,20},{20,16},{24,28},{28,24},{32,36},... | collective-permute-start | bytes 3145736 | tf_op jit(solution)/shard_map/ppermute | solution.py:373
  133.3 4.4 %collective-permute-start.5 = (bf16[16,256,128]{2,1,0:T(8,128)(2,1)}, bf16[16,256,128]{2,1,0:T(8,128)(2,1)}, u32[]{:S(2)}, u32[]{:S(2)}) collective-permute-start(bf16[16,256,128]{2,1,0:T(8,128)(2,1)} %collective-permute-done.4.v2), channel_id=1, source_target_pairs={{0,4},{4,0},{8,12},{12,8},{16,20},{20,16},{24,28},{28,24},{32,36},... | collective-permute-start | bytes 3145736 | tf_op jit(solution)/shard_map/ppermute | solution.py:373
  154.9 1.0 copy-start.10
  156.5 7.1 %copy-start.24 = (f32[16,8,256]{2,1,0:T(8,128)S(1)}, f32[16,8,256]{2,1,0:T(8,128)}, u32[]{:S(2)}) copy-start(f32[16,8,256]{2,1,0:T(8,128)} %copy-done.23) | copy-start | bytes 393220
  156.5 35.7 %all-to-all-start.4 = ((bf16[16,256,128]{2,1,0:T(8,128)(2,1)}), bf16[16,256,128]{2,1,0:T(8,128)(2,1)}, u32[]{:S(2)}, u32[]{:S(2)}) async-start(bf16[16,256,128]{2,1,0:T(8,128)(2,1)} %copy-done.10), calls=%async_computation.4 | async-start | bytes 2097152 | tf_op jit(solution)/shard_map/all_to_all | solution.py:47
  188.6 1.0 copy-start.9
  190.5 1.0 copy-start.22
  191.6 8.8 %collective-permute-start.7 = (bf16[16,256,128]{2,1,0:T(8,128)(2,1)}, bf16[16,256,128]{2,1,0:T(8,128)(2,1)}, u32[]{:S(2)}, u32[]{:S(2)}) collective-permute-start(bf16[16,256,128]{2,1,0:T(8,128)(2,1)} %get-tuple-element.58), channel_id=1, source_target_pairs={{0,4},{4,0},{8,12},{12,8},{16,20},{20,16},{24,28},{28,24},{32,36},... | collective-permute-start | bytes 3145736 | tf_op jit(solution)/shard_map/ppermute | solution.py:373
  192.2 39.4 %all-to-all-start.5 = ((bf16[16,256,128]{2,1,0:T(8,128)(2,1)}), bf16[16,256,128]{2,1,0:T(8,128)(2,1)S(1)}, u32[]{:S(2)}, u32[]{:S(2)}) async-start(bf16[16,256,128]{2,1,0:T(8,128)(2,1)} %copy-done.9), calls=%async_computation.5 | async-start | bytes 2097152 | tf_op jit(solution)/shard_map/all_to_all | solution.py:47
  200.0 4.3 %collective-permute-start.6 = (bf16[16,256,128]{2,1,0:T(8,128)(2,1)}, bf16[16,256,128]{2,1,0:T(8,128)(2,1)S(1)}, u32[]{:S(2)}, u32[]{:S(2)}) collective-permute-start(bf16[16,256,128]{2,1,0:T(8,128)(2,1)} %copy-done.22), channel_id=1, source_target_pairs={{0,4},{4,0},{8,12},{12,8},{16,20},{20,16},{24,28},{28,24},{32,36},... | collective-permute-start | bytes 3145736 | tf_op jit(solution)/shard_map/ppermute | solution.py:373
  200.4 29.9 %copy-start.26 = (f32[16,256,128]{2,1,0:T(8,128)S(1)}, f32[16,256,128]{2,1,0:T(8,128)}, u32[]{:S(2)}) copy-start(f32[16,256,128]{2,1,0:T(8,128)} %get-tuple-element.55) | copy-start | bytes 6291460
  202.7 27.6 %collective-permute-start.8 = (bf16[16,256,128]{2,1,0:T(8,128)(2,1)S(1)}, bf16[16,256,128]{2,1,0:T(8,128)(2,1)S(1)}, u32[]{:S(2)}, u32[]{:S(2)}) collective-permute-start(bf16[16,256,128]{2,1,0:T(8,128)(2,1)S(1)} %add_convert_fusion.3), channel_id=1, source_target_pairs={{192,0},{196,4},{200,8},{204,12},{208,16},{212,20},{216,24},{220,2... | collective-permute-start | bytes 3145736 | tf_op jit(solution)/shard_map/ppermute | solution.py:375
  204.0 36.3 %collective-permute-start.10 = (bf16[16,256,128]{2,1,0:T(8,128)(2,1)}, bf16[16,256,128]{2,1,0:T(8,128)(2,1)}, u32[]{:S(2)}, u32[]{:S(2)}) collective-permute-start(bf16[16,256,128]{2,1,0:T(8,128)(2,1)} %get-tuple-element.66), channel_id=1, source_target_pairs={{0,4},{4,0},{8,12},{12,8},{16,20},{20,16},{24,28},{28,24},{32,36},... | collective-permute-start | bytes 3145736 | tf_op jit(solution)/shard_map/ppermute | solution.py:373
  231.7 40.2 %all-to-all-start.6 = ((bf16[16,256,128]{2,1,0:T(8,128)(2,1)}), bf16[16,256,128]{2,1,0:T(8,128)(2,1)}, u32[]{:S(2)}, u32[]{:S(2)}) async-start(bf16[16,256,128]{2,1,0:T(8,128)(2,1)} %add_convert_fusion.2), calls=%async_computation.6 | async-start | bytes 2097152 | tf_op jit(solution)/shard_map/all_to_all | solution.py:47
  239.1 4.7 %collective-permute-start.9 = (bf16[16,256,128]{2,1,0:T(8,128)(2,1)}, bf16[16,256,128]{2,1,0:T(8,128)(2,1)S(1)}, u32[]{:S(2)}, u32[]{:S(2)}) collective-permute-start(bf16[16,256,128]{2,1,0:T(8,128)(2,1)} %copy-done.21), channel_id=1, source_target_pairs={{0,4},{4,0},{8,12},{12,8},{16,20},{20,16},{24,28},{28,24},{32,36},... | collective-permute-start | bytes 3145736 | tf_op jit(solution)/shard_map/ppermute | solution.py:373
  240.3 30.2 %copy-start.25 = (f32[16,256,128]{2,1,0:T(8,128)S(1)}, f32[16,256,128]{2,1,0:T(8,128)}, u32[]{:S(2)}) copy-start(f32[16,256,128]{2,1,0:T(8,128)} %get-tuple-element.63) | copy-start | bytes 6291460
  242.6 27.9 %collective-permute-start.11 = (bf16[16,256,128]{2,1,0:T(8,128)(2,1)S(1)}, bf16[16,256,128]{2,1,0:T(8,128)(2,1)S(1)}, u32[]{:S(2)}, u32[]{:S(2)}) collective-permute-start(bf16[16,256,128]{2,1,0:T(8,128)(2,1)S(1)} %add_convert_fusion.1), channel_id=1, source_target_pairs={{192,0},{196,4},{200,8},{204,12},{208,16},{212,20},{216,24},{220,2... | collective-permute-start | bytes 3145736 | tf_op jit(solution)/shard_map/ppermute | solution.py:375
  271.8 32.3 %all-to-all-start.7 = ((bf16[16,256,128]{2,1,0:T(8,128)(2,1)}), bf16[16,256,128]{2,1,0:T(8,128)(2,1)}, u32[]{:S(2)}, u32[]{:S(2)}) async-start(bf16[16,256,128]{2,1,0:T(8,128)(2,1)} %add_convert_fusion), calls=%async_computation.7 | async-start | bytes 2097152 | tf_op jit(solution)/shard_map/all_to_all | solution.py:47
  282.4 4.9 %copy-start.16 = (bf16[256,32]{0,1:T(8,128)(2,1)S(1)}, bf16[256,32]{0,1:T(8,128)(2,1)}, u32[]{:S(2)}) copy-start(bf16[256,32]{0,1:T(8,128)(2,1)} %copy.39) | copy-start | bytes 49156
  286.3 23.6 %collective-permute-start.12 = (f32[32,24,128]{2,1,0:T(8,128)}, f32[32,24,128]{2,1,0:T(8,128)}, u32[]{:S(2)}, u32[]{:S(2)}) collective-permute-start(f32[32,24,128]{2,1,0:T(8,128)} %get-tuple-element.75), channel_id=1, source_target_pairs={{0,4},{4,0},{8,12},{12,8},{16,20},{20,16},{24,28},{28,24},{32,36},... | collective-permute-start | bytes 1179656 | tf_op jit(solution)/shard_map/ppermute | solution.py:373
  290.9 20.1 %collective-permute-start.13 = (f32[32,24,128]{2,1,0:T(8,128)S(1)}, f32[32,24,128]{2,1,0:T(8,128)}, u32[]{:S(2)}, u32[]{:S(2)}) collective-permute-start(f32[32,24,128]{2,1,0:T(8,128)S(1)} %get-tuple-element.77), channel_id=1, source_target_pairs={{0,4},{4,0},{8,12},{12,8},{16,20},{20,16},{24,28},{28,24},{32,36},... | collective-permute-start | bytes 1179656 | tf_op jit(solution)/shard_map/ppermute | solution.py:373
  304.1 5.8 %copy-start.15 = (f32[32,24,128]{2,1,0:T(8,128)S(1)}, f32[32,24,128]{2,1,0:T(8,128)}, u32[]{:S(2)}) copy-start(f32[32,24,128]{2,1,0:T(8,128)} %copy-done.14) | copy-start | bytes 1179652
  307.7 4.4 %collective-permute-start.14 = (f32[32,24,128]{2,1,0:T(8,128)S(1)}, f32[32,24,128]{2,1,0:T(8,128)S(1)}, u32[]{:S(2)}, u32[]{:S(2)}) collective-permute-start(f32[32,24,128]{2,1,0:T(8,128)S(1)} %get-tuple-element.79), channel_id=1, source_target_pairs={{0,4},{4,0},{8,12},{12,8},{16,20},{20,16},{24,28},{28,24},{32,36},... | collective-permute-start | bytes 1179656 | tf_op jit(solution)/shard_map/ppermute | solution.py:373
  348.7 4.9 %collective-permute-start.15 = (f32[72,128]{1,0:T(8,128)S(1)}, f32[72,128]{1,0:T(8,128)S(1)}, u32[]{:S(2)}, u32[]{:S(2)}) collective-permute-start(f32[72,128]{1,0:T(8,128)S(1)} %reduce_sum.9), channel_id=1, source_target_pairs={{0,1},{1,2},{2,3},{3,0},{4,5},{5,6},{6,7},{7,4},{8,9},{9,10},{10,1... | collective-permute-start | bytes 110600 | tf_op jit(solution)/shard_map/ppermute | solution.py:428
  350.0 4.4 %collective-permute-start.16 = (f32[72,128]{1,0:T(8,128)S(1)}, f32[72,128]{1,0:T(8,128)S(1)}, u32[]{:S(2)}, u32[]{:S(2)}) collective-permute-start(f32[72,128]{1,0:T(8,128)S(1)} %reduce_sum.9), channel_id=1, source_target_pairs={{0,2},{1,3},{2,0},{3,1},{4,6},{5,7},{6,4},{7,5},{8,10},{9,11},{10,... | collective-permute-start | bytes 110600 | tf_op jit(solution)/shard_map/ppermute | solution.py:428
  352.4 3.3 collective-permute-start.17
  355.8 5.2 %collective-permute-start.18 = (f32[72,128]{1,0:T(8,128)S(1)}, f32[72,128]{1,0:T(8,128)S(1)}, u32[]{:S(2)}, u32[]{:S(2)}) collective-permute-start(f32[72,128]{1,0:T(8,128)S(1)} %add_add_fusion), channel_id=1, source_target_pairs={{0,4},{4,0},{8,12},{12,8},{16,20},{20,16},{24,28},{28,24},{32,36},... | collective-permute-start | bytes 110600 | tf_op jit(solution)/shard_map/ppermute | solution.py:373
  (7 other events, 4.9 us)

commit v2 on v1

v2 whole, which is shorter than its diff:
```python
import math

import jax
import jax.numpy as jnp
from jax import lax
from jax.experimental import pallas as pl
from jax.experimental.pallas import tpu as pltpu
from jax.sharding import PartitionSpec as P

BLK = 256
HD = 128
HEADS = 16
HQ = HEADS * HD
D = 4096
R = 32
ADAPTER_SCALE = 0.5
SCORE_SCALE = HD ** -0.5
LOG2_SCALE = SCORE_SCALE * math.log2(math.e)
GRAD_SCALE = (4 * 16384) ** -0.5
VMEM_BYTES = 56 * 1024 * 1024
NT = (((1,), (1,)), ((), ()))
TN = (((0,), (0,)), ((), ()))
TILES = 32
PER_STEP = 4


def place(y, z, core):
    return (y * 8 + z) * 2 + core


def group_row(half, low):
    return low if half == 0 else 3 - low


EVERY = [(y, z, c) for y in range(4) for z in range(8) for c in range(2)]
HEAD_GROUPS = [
    [place(group_row(half, low), z, core) for low in range(2) for z in range(8)]
    for half in range(2)
    for core in range(2)
]
CORE_PAIRS = [(i, i ^ 1) for i in range(64)]
TO_LATER = [(place(y, z, c), place(3 - y, z, c)) for y, z, c in EVERY if y < 2]
TO_EARLIER = [(b, a) for a, b in TO_LATER]
TILE_GROUPS = [[place(y, z, core) for y in range(4) for z in range(8)] for core in range(2)]


def to_heads(x):
    return lax.all_to_all(x, "ctx", 0, 0, axis_index_groups=HEAD_GROUPS, tiled=True)


def swap(x):
    return lax.ppermute(x, "ctx", CORE_PAIRS)


def after(x, first):
    return lax.optimization_barrier((x, first))


def whole(*shape):
    return pl.BlockSpec(shape, lambda i, *_: (0,) * len(shape))


def add_adapter(proj, low, up):
    adapter = jnp.dot(low, up, preferred_element_type=jnp.float32)
    return (proj.astype(jnp.float32) + ADAPTER_SCALE * adapter).astype(jnp.bfloat16)


def key_value_kernel(tok_ref, down_ref, k_ref, v_ref, up_ref, out_ref, low_ref, low_s):
    @pl.when(pl.program_id(0) == 0)
    def _():
        low = lax.dot_general(
            tok_ref[...], down_ref[...].reshape(3 * R, D), NT, preferred_element_type=jnp.float32
        )
        low_s[...] = low.astype(jnp.bfloat16)
        low_ref[...] = low.astype(jnp.bfloat16)

    low = low_s[...]
    for side, ref in enumerate((k_ref, v_ref)):
        m = side + 1
        field = add_adapter(ref[...], low[:, m * R : (m + 1) * R], up_ref[m])
        for h in range(8):
            out_ref[h, side] = field[:, h * HD : (h + 1) * HD]


def make_key_value(tokens, projected, down_t, up_projection):
    return pl.pallas_call(
        key_value_kernel,
        grid=(2,),
        in_specs=[
            whole(BLK, D),
            whole(3, R, D),
            pl.BlockSpec((BLK, 1024), lambda i: (0, 2 + i)),
            pl.BlockSpec((BLK, 1024), lambda i: (0, 4 + i)),
            pl.BlockSpec((3, R, 1024), lambda i: (0, 0, i)),
        ],
        out_specs=[pl.BlockSpec((8, 2, BLK, HD), lambda i: (i, 0, 0, 0)), whole(BLK, 3 * R)],
        out_shape=[
            jax.ShapeDtypeStruct((HEADS, 2, BLK, HD), jnp.bfloat16),
            jax.ShapeDtypeStruct((BLK, 3 * R), jnp.bfloat16),
        ],
        scratch_shapes=[pltpu.VMEM((BLK, 3 * R), jnp.bfloat16)],
        compiler_params=pltpu.CompilerParams(vmem_limit_bytes=VMEM_BYTES),
        cost_estimate=pl.CostEstimate(
            flops=2 * BLK * D * 3 * R + 4 * BLK * R * HQ, bytes_accessed=7 * 2**20, transcendentals=0
        ),
        name="make_key_value",
    )(tokens, down_t, projected, projected, up_projection)


def query_kernel(low_ref, proj_ref, up_ref, cot_ref, out_ref):
    field = add_adapter(proj_ref[...], low_ref[:, 0:R], up_ref[0])
    for h in range(4):
        cols = slice(h * HD, (h + 1) * HD)
        out_ref[h, 0] = field[:, cols]
        out_ref[h, 1] = cot_ref[:, cols]


def make_query(low, projected, up_projection, cotangent):
    return pl.pallas_call(
        query_kernel,
        grid=(4,),
        in_specs=[
            whole(BLK, 3 * R),
            pl.BlockSpec((BLK, 512), lambda i: (0, i)),
            pl.BlockSpec((1, R, 512), lambda i: (0, 0, i)),
            pl.BlockSpec((BLK, 512), lambda i: (0, i)),
        ],
        out_specs=pl.BlockSpec((4, 2, BLK, HD), lambda i: (i, 0, 0, 0)),
        out_shape=jax.ShapeDtypeStruct((HEADS, 2, BLK, HD), jnp.bfloat16),
        compiler_params=pltpu.CompilerParams(vmem_limit_bytes=VMEM_BYTES),
        cost_estimate=pl.CostEstimate(
            flops=2 * BLK * R * HQ, bytes_accessed=4 * 2**20, transcendentals=0
        ),
        name="make_query",
    )(low, projected, up_projection, cotangent)


def stored_at(block, half, core):
    y = block >> 4
    block_half = y >> 1
    row = jnp.where(block_half == 0, y, 3 - y)
    source = jnp.where(block_half == half, 0, 2) + jnp.where((block & 1) == core, 0, 1)
    return source * 16 + row * 8 + ((block >> 1) & 7)


def slots_of(ids_ref, me_ref, p):
    me = me_ref[0]
    core = me & 1
    half = me >> 5
    low = p >> 3
    y = jnp.where(half == 0, low, 3 - low)
    own = (y * 8 + (p & 7)) * 2 + core
    spots = [p]
    biases = [None]
    for t in (1, 2):
        block = ids_ref[own * 3 + t]
        spots.append(stored_at(block, half, core))
        biases.append(jnp.where(block == own, -jnp.inf, 0.0).astype(jnp.float32))
    return spots, biases


def attend_kernel(
    ids_ref, me_ref, qg_ref, kv0, kv1, kv2, kv3,
    out_ref, own_ref, far_ref, core_ref, farcore_ref, kvs, acc, staged, sem,
):
    step = pl.program_id(0)

    @pl.when(step == 0)
    def _():
        copies = [
            pltpu.make_async_copy(ref, kvs.at[pl.ds(16 * n, 16)], sem.at[n])
            for n, ref in enumerate((kv0, kv1, kv2, kv3))
        ]
        for copy in copies:
            copy.start()

        def clear(i, _):
            acc[i] = jnp.zeros((2, BLK, HD), jnp.float32)
            return 0

        lax.fori_loop(0, 64, clear, 0)
        for copy in copies:
            copy.wait()

    key_row = lax.broadcasted_iota(jnp.int32, (BLK, BLK), 0)
    query_col = lax.broadcasted_iota(jnp.int32, (BLK, BLK), 1)
    causal = key_row <= query_col
    work = []
    for sub in range(PER_STEP):
        spots, biases = slots_of(ids_ref, me_ref, step * PER_STEP + sub)
        work.append((spots, biases, qg_ref[sub, 0], qg_ref[sub, 1]))
    scores = []
    for spots, biases, q, g in work:
        parts = []
        for t in range(3):
            s = lax.dot_general(kvs[spots[t], 0], q, NT, preferred_element_type=jnp.float32)
            s = s * LOG2_SCALE
            parts.append(jnp.where(causal, s, -jnp.inf) if t == 0 else s + biases[t])
        scores.append(parts)
    middle = []
    for (spots, biases, q, g), s in zip(work, scores):
        top = jnp.max(jnp.maximum(jnp.maximum(s[0], s[1]), s[2]), axis=0, keepdims=True)
        shifted = [jnp.exp2(x - top) for x in s]
        inverse = 1.0 / jnp.sum(shifted[0] + shifted[1] + shifted[2], axis=0, keepdims=True)
        probs = [x * inverse for x in shifted]
        weights = [x.astype(jnp.bfloat16) for x in probs]
        out = None
        for t in range(3):
            part = lax.dot_general(kvs[spots[t], 1], weights[t], TN, preferred_element_type=jnp.float32)
            out = part if out is None else out + part
        middle.append((probs, weights, out))
    for sub in range(PER_STEP):
        spots, biases, q, g = work[sub]
        probs, weights, out = middle[sub]
        attn = out.T.astype(jnp.bfloat16)
        out_ref[sub, 0] = attn
        product = attn.astype(jnp.float32) * g.astype(jnp.float32)
        delta = jnp.sum(product.T, axis=0, keepdims=True)
        dq = None
        for t in range(3):
            dprobs = lax.dot_general(kvs[spots[t], 1], g, NT, preferred_element_type=jnp.float32)
            dscores = (probs[t] * (dprobs - delta) * SCORE_SCALE).astype(jnp.bfloat16)
            part = lax.dot_general(kvs[spots[t], 0], dscores, TN, preferred_element_type=jnp.float32)
            dq = part if dq is None else dq + part
            dk = jnp.dot(dscores, q, preferred_element_type=jnp.float32)
            dv = jnp.dot(weights[t], g, preferred_element_type=jnp.float32)
            if t > 0:
                dk = dk.astype(jnp.bfloat16).astype(jnp.float32)
                dv = dv.astype(jnp.bfloat16).astype(jnp.float32)
            acc[spots[t], 0] += dk
            acc[spots[t], 1] += dv
        out_ref[sub, 1] = dq.T.astype(jnp.bfloat16)

    @pl.when(step == pl.num_programs(0) - 1)
    def _():
        copies = []

        def send(source, target):
            copy = pltpu.make_async_copy(source, target, sem.at[len(copies)])
            copy.start()
            copies.append(copy)

        for n, (at, target) in enumerate(((48, farcore_ref), (16, core_ref))):

            def cast(i, _, n=n, at=at):
                staged[n * 16 + i] = acc[at + i].astype(jnp.bfloat16)
                return 0

            if n == 1:
                send(acc.at[pl.ds(32, 16)], far_ref)
                send(acc.at[pl.ds(0, 16)], own_ref)
            lax.fori_loop(0, 16, cast, 0)
            send(staged.at[pl.ds(n * 16, 16)], target)
        for copy in copies:
            copy.wait()


ANY = pl.BlockSpec(memory_space=pl.ANY)


def attend(ids, me, query, key_values):
    wide = jax.ShapeDtypeStruct((16, 2, BLK, HD), jnp.float32)
    narrow = jax.ShapeDtypeStruct((16, 2, BLK, HD), jnp.bfloat16)
    rows = pl.BlockSpec((PER_STEP, 2, BLK, HD), lambda p, *_: (p, 0, 0, 0))
    return pl.pallas_call(
        attend_kernel,
        grid_spec=pltpu.PrefetchScalarGridSpec(
            num_scalar_prefetch=2,
            grid=(16 // PER_STEP,),
            in_specs=[rows] + [ANY] * 4,
            out_specs=[rows] + [ANY] * 4,
            scratch_shapes=[
                pltpu.VMEM((64, 2, BLK, HD), jnp.bfloat16),
                pltpu.VMEM((64, 2, BLK, HD), jnp.float32),
                pltpu.VMEM((32, 2, BLK, HD), jnp.bfloat16),
                pltpu.SemaphoreType.DMA((4,)),
            ],
        ),
        out_shape=[narrow, wide, wide, narrow, narrow],
        compiler_params=pltpu.CompilerParams(vmem_limit_bytes=VMEM_BYTES),
        cost_estimate=pl.CostEstimate(
            flops=16 * 6 * 2 * BLK * 3 * BLK * HD,
            bytes_accessed=26 * 2**20,
            transcendentals=16 * 3 * BLK * BLK,
        ),
        name="attend",
    )(ids, me, query, *key_values)


def write_terms(terms, base, head, tok_ref, low, up):
    dlow = None
    for h in range(HEADS):
        g = head(h)
        cols = slice(h * HD, (h + 1) * HD)
        part = lax.dot_general(up[:, cols], g, NT, preferred_element_type=jnp.float32)
        dlow = part if dlow is None else dlow + part
        up_term = jnp.dot(low, g, preferred_element_type=jnp.float32) * (ADAPTER_SCALE * GRAD_SCALE)
        for side in range(2):
            cut = up_term[:, side * 64 : (side + 1) * 64]
            terms[2 * h + side, base + 32 : base + 48, :] = jnp.concatenate([cut[0:16], cut[16:32]], axis=1)
    dlow = (dlow * ADAPTER_SCALE).astype(jnp.bfloat16)
    for t in range(TILES):
        down_term = jnp.dot(dlow, tok_ref[:, t * 128 : (t + 1) * 128], preferred_element_type=jnp.float32)
        terms[t, base : base + 32, :] = down_term * GRAD_SCALE


def query_grads_kernel(home_ref, tok_ref, low_ref, up_ref, attn_ref, gp_ref, terms):
    for h in range(HEADS):
        cols = slice(h * HD, (h + 1) * HD)
        attn_ref[:, cols] = home_ref[h, 0]
        gp_ref[:, cols] = home_ref[h, 1]
    write_terms(terms, 0, lambda h: home_ref[h, 1], tok_ref, low_ref[...], up_ref[0])


def key_value_grads_kernel(
    me_ref, _, other_ref, home_ref, tok_ref, low_ref, up_ref, gp_ref, keep_ref, send_ref, terms, rows, sem
):
    for side in range(2):
        for h in range(HEADS):
            rows[:, side * HQ + h * HD : side * HQ + (h + 1) * HD] = home_ref[h, side]
    copy = pltpu.make_async_copy(rows, gp_ref.at[:, pl.ds(HQ, 2 * HQ)], sem)
    copy.start()
    for side in range(2):
        write_terms(
            terms,
            side * 48,
            lambda h: home_ref[h, side],
            tok_ref,
            low_ref[(side + 1) * R : (side + 2) * R, :],
            up_ref[side + 1],
        )

    def first(ref):
        ref[:, 0:48, :] = other_ref[...]
        ref[:, 48:72, :] = terms[:, 0:24, :]

    def second(ref):
        ref[...] = terms[:, 24:96, :]

    core = me_ref[0] & 1

    @pl.when(core == 0)
    def _():
        first(keep_ref)
        second(send_ref)

    @pl.when(core == 1)
    def _():
        first(send_ref)
        second(keep_ref)

    copy.wait()


def query_grads(home, tokens, low_t, up_projection):
    return pl.pallas_call(
        query_grads_kernel,
        grid=(1,),
        in_specs=[
            whole(HEADS, 2, BLK, HD),
            whole(BLK, D),
            whole(R, BLK),
            whole(1, R, HQ),
        ],
        out_specs=[whole(BLK, HQ), whole(BLK, HQ), whole(TILES, 48, 128)],
        out_shape=[
            jax.ShapeDtypeStruct((BLK, HQ), jnp.bfloat16),
            jax.ShapeDtypeStruct((BLK, 3 * HQ), jnp.bfloat16),
            jax.ShapeDtypeStruct((TILES, 48, 128), jnp.float32),
        ],
        compiler_params=pltpu.CompilerParams(vmem_limit_bytes=24 * 1024 * 1024),
        cost_estimate=pl.CostEstimate(
            flops=2 * BLK * R * (D + 2 * HQ), bytes_accessed=8 * 2**20, transcendentals=0
        ),
        name="query_grads",
    )(home, tokens, low_t, up_projection)


def key_value_grads(me, grad_proj, terms_q, home, tokens, low_t, up_projection):
    piece = jax.ShapeDtypeStruct((TILES, 72, 128), jnp.float32)
    return pl.pallas_call(
        key_value_grads_kernel,
        grid_spec=pltpu.PrefetchScalarGridSpec(
            num_scalar_prefetch=1,
            grid=(1,),
            in_specs=[
                ANY,
                whole(TILES, 48, 128),
                whole(HEADS, 2, BLK, HD),
                whole(BLK, D),
                whole(3 * R, BLK),
                whole(3, R, HQ),
            ],
            out_specs=[
                ANY,
                whole(TILES, 72, 128),
                whole(TILES, 72, 128),
            ],
            scratch_shapes=[
                pltpu.VMEM((TILES, 96, 128), jnp.float32),
                pltpu.VMEM((BLK, 2 * HQ), jnp.bfloat16),
                pltpu.SemaphoreType.DMA,
            ],
        ),
        out_shape=[jax.ShapeDtypeStruct((BLK, 3 * HQ), jnp.bfloat16), piece, piece],
        input_output_aliases={1: 0},
        compiler_params=pltpu.CompilerParams(vmem_limit_bytes=28 * 1024 * 1024),
        cost_estimate=pl.CostEstimate(
            flops=4 * BLK * R * (D + 2 * HQ), bytes_accessed=10 * 2**20, transcendentals=0
        ),
        name="key_value_grads",
    )(me, grad_proj, terms_q, home, tokens, low_t, up_projection)


def finish_kernel(lane_ref, mine_ref, other_ref, down_ref, up_ref, full, down_t, up_t):
    lane = lane_ref[0]

    @pl.when(lane < 4)
    def _():
        full[0:72] = mine_ref[...]
        full[72:144] = other_ref[...]

    @pl.when(lane >= 4)
    def _():
        full[0:72] = other_ref[...]
        full[72:144] = mine_ref[...]

    for m in range(3):
        down_t[...] = full[m * 48 : m * 48 + 32, :].T
        down_ref[m] = down_t[pl.ds(lane * 16, 16), :]
        up_t[...] = full[m * 48 + 32 : m * 48 + 48, :].T
        up_ref[m, :, 0:16] = up_t[pl.ds(lane * 8, 8), :]
        up_ref[m, :, 16:32] = up_t[pl.ds(lane * 8 + 64, 8), :]


def finish(lane, mine, other):
    return pl.pallas_call(
        finish_kernel,
        grid_spec=pltpu.PrefetchScalarGridSpec(
            num_scalar_prefetch=1,
            grid=(1,),
            in_specs=[whole(72, 128), whole(72, 128)],
            out_specs=[whole(3, 16, R), whole(3, 8, R)],
            scratch_shapes=[
                pltpu.VMEM((144, 128), jnp.float32),
                pltpu.VMEM((128, R), jnp.float32),
                pltpu.VMEM((128, 16), jnp.float32),
            ],
        ),
        out_shape=[
            jax.ShapeDtypeStruct((3, 16, R), jnp.float32),
            jax.ShapeDtypeStruct((3, 8, R), jnp.float32),
        ],
        compiler_params=pltpu.CompilerParams(vmem_limit_bytes=8 * 1024 * 1024),
        name="finish",
    )(lane, mine, other)


def shards(tokens, projected, down_proj, up_projection, block_ids, cotangent):
    tokens = tokens[0]
    projected = projected[0]
    me = lax.axis_index("ctx").astype(jnp.int32)
    lane = ((me & 1) * 4 + lax.axis_index("dp")).astype(jnp.int32).reshape(1)
    me = me.reshape(1)
    ids = block_ids[0].reshape(-1)

    local, low = make_key_value(tokens, projected, jnp.transpose(down_proj, (0, 2, 1)), up_projection)
    key_value = to_heads(local)
    local = make_query(low, projected, up_projection, cotangent[0])
    low_t = low.T
    local, key_value = after(local, key_value)
    far = lax.ppermute(key_value, "ctx", TO_LATER)
    query = to_heads(local)
    out, own, far_part, core_part, farcore_part = attend(
        ids, me, query, (key_value, swap(key_value), far, swap(far))
    )

    far_sum = (far_part + swap(farcore_part).astype(jnp.float32)).astype(jnp.bfloat16)
    returned = lax.ppermute(far_sum, "ctx", TO_EARLIER)
    out_home = to_heads(out)
    total = own + swap(core_part).astype(jnp.float32) + returned.astype(jnp.float32)
    total, out_home = after(total.astype(jnp.bfloat16), out_home)
    total_home = to_heads(total)
    attn_rows, grad_proj, terms_q = query_grads(out_home, tokens, low_t, up_projection)
    grad_proj, keep, send = key_value_grads(
        me, grad_proj, terms_q, total_home, tokens, low_t, up_projection
    )
    pieces = (keep + swap(send)).astype(jnp.bfloat16)
    pieces = lax.all_to_all(pieces, "ctx", 0, 0, axis_index_groups=TILE_GROUPS, tiled=True)
    mine = jnp.sum(pieces.astype(jnp.float32), axis=0)
    others = [
        lax.ppermute(mine, "dp", [(j, (j + step) % 4) for j in range(4)]) for step in (1, 2, 3)
    ]
    mine = (mine + others[0]) + (others[1] + others[2])
    grad_down, grad_up = finish(lane, mine, swap(mine))
    return attn_rows[None], grad_proj[None], grad_down, jnp.transpose(grad_up, (0, 2, 1))


def solution(mesh):
    placed = (
        P("dp", "ctx", None),
        P("dp", "ctx", None),
        P(),
        P(),
        P("dp", None, None),
        P("dp", "ctx", None),
    )
    return jax.shard_map(
        shards,
        mesh=mesh,
        in_specs=placed,
        out_specs=(
            P("dp", "ctx", None),
            P("dp", "ctx", None),
            P(None, ("ctx", "dp"), None),
            P(None, None, ("ctx", "dp")),
        ),
        check_vma=False,
    )
```

time: 365 us -> 313 us (0.86)
  waiting for transfers between devices: 135 us -> 185 us
  local copies, waits for them, and re-layouts: 40.1 us -> 0.92 us
  starting transfers between devices: 83.3 us -> 54.6 us
  blocking collectives: 36.5 us -> 20.7 us
  Pallas kernels: 56.7 us -> 45.7 us
  other arithmetic: 10.3 us -> 5.33 us
    all_to_all x8 -> x4, waiting for transfers between devices: 64.2 us -> 95.4 us  [to_heads(): lax.all_to_all(x, 'ctx', 0, 0, axis_index_groups=HEAD_GROUPS, tiled=True)]
    unnamed x61 -> x13, local copies, waits for them, and re-layouts: 31.2 us -> 0.12 us
    all_to_all x8 -> x4, starting transfers between devices: 57.6 us -> 29.1 us  [to_heads(): lax.all_to_all(x, 'ctx', 0, 0, axis_index_groups=HEAD_GROUPS, tiled=True)]
    ppermute x16 -> x8, waiting for transfers between devices: 68.4 us -> 85.6 us  [the longest x1 48.8 us: shards(): returned = lax.ppermute(far_sum, 'ctx', TO_EARLIER)]
    all_to_all x1, blocking collectives: 36.5 us -> 20.7 us  [shards(): lax.all_to_all(pieces, 'ctx', 0, 0, axis_index_groups=TILE_GROUPS, tiled=...]
    pallas_call x8 -> x6, Pallas kernels: 56.7 us -> 45.7 us  [the longest x1 26 us: attend(): pl.pallas_call(attend_kernel, grid_spec=pltpu.PrefetchScalarGridSpec(num_...]
    pallas_call x3 -> x1, local copies, waits for them, and re-layouts: 3.93 us -> 0.1 us  [make_key_value(): pl.pallas_call(key_value_kernel, grid=(2,), in_specs=[whole(BLK, D), whol...]
    ppermute x16 -> x8, starting transfers between devices: 20.8 us -> 21.8 us  [the longest x6 15.4 us: swap(): return lax.ppermute(x, 'ctx', CORE_PAIRS)]
  transfers between devices with their start and end apart: 27 -> 15, of which waited for: 10 -> 9; matrix products, arithmetic and copies ran while one was open for 6% -> 2% of each run, Pallas kernels for 15% -> 3%
where the time goes in v2:
time: 313 us
  waiting for transfers between devices  185 us (59%)
  starting transfers between devices  54.6 us (17%)
  Pallas kernels  45.7 us (15%)
  blocking collectives  20.7 us (7%)
  other arithmetic  5.33 us (2%)
    all_to_all x4, waiting for transfers between devices, to_heads(): lax.all_to_all(x, 'ctx', 0, 0, axis_index_groups=HEAD_GROUPS, tiled=True)  95.4 us
    ppermute x1, waiting for transfers between devices, shards(): returned = lax.ppermute(far_sum, 'ctx', TO_EARLIER)  48.8 us
    ppermute x1, waiting for transfers between devices, shards(): far = lax.ppermute(key_value, 'ctx', TO_LATER)  33.5 us
    all_to_all x4, starting transfers between devices, to_heads(): lax.all_to_all(x, 'ctx', 0, 0, axis_index_groups=HEAD_GROUPS, tiled=True)  29.1 us
    pallas_call x1, Pallas kernels, attend(): pl.pallas_call(attend_kernel, grid_spec=pltpu.PrefetchScalarGridSpec(num_...  26 us
    all_to_all x1, blocking collectives, shards(): lax.all_to_all(pieces, 'ctx', 0, 0, axis_index_groups=TILE_GROUPS, tiled=...  20.7 us
    ppermute x6, starting transfers between devices, swap(): return lax.ppermute(x, 'ctx', CORE_PAIRS)  15.4 us
  transfers between devices with their start and end apart: 15, of which 9 were waited for; matrix products, arithmetic and copies ran while one was open for 2% of the time, Pallas kernels for 3%

profile of v2, /device:TPU:1, one launch (start us, length us, event | category | flops | bytes accessed | tf_op | source)
XLA Modules:
  0.0 312.6 jit_solution(4708943810325142964)
XLA Ops:
  0.6 5.0 %make_key_value.1 = (bf16[16,2,256,128]{3,2,1,0:T(8,128)(2,1)}, bf16[256,96]{1,0:T(8,128)(2,1)}) custom-call(bf16[256,4096]{1,0:T(8,128)(2,1)} %bitcast.10, bf16[3,32,4096]{2,1,0:T(8,128)(2,1)} %bitcast.20, bf16[256,6144]{1,0:T(8,128)(2,1)} %bitcast.15, bf16[256,6144]{1,0:T(8,128)(2,1)} %bitcast.16, bf16[3,32,2048]{2,1,0:T(8,128)(2,1)} %up_ref.7), custom_call_target="tpu_custom_call" | custom-call | flops 268435456 | bytes 7340032 | tf_op jit(solution)/shard_map/make_key_value/pallas_call | solution.py:86
  5.6 10.1 %all-to-all-start = ((bf16[16,2,256,128]{3,2,1,0:T(8,128)(2,1)}), bf16[16,2,256,128]{3,2,1,0:T(8,128)(2,1)S(1)}, u32[]{:S(2)}, u32[]{:S(2)}) async-start(bf16[16,2,256,128]{3,2,1,0:T(8,128)(2,1)} %get-tuple-element.24), calls=%async_computation | async-start | bytes 4194304 | tf_op jit(solution)/shard_map/all_to_all | solution.py:48
  15.8 4.2 %make_query.1 = bf16[16,2,256,128]{3,2,1,0:T(8,128)(2,1)} custom-call(bf16[256,96]{1,0:T(8,128)(2,1)} %get-tuple-element.23.low_ref, bf16[256,6144]{1,0:T(8,128)(2,1)} %bitcast.17, bf16[3,32,2048]{2,1,0:T(8,128)(2,1)} %up_ref.7, bf16[256,2048]{1,0:T(8,128)(2,1)} %bitcast.19), custom_call_target="tpu_custom_call" | custom-call | flops 33554432 | bytes 4194304 | tf_op jit(solution)/shard_map/make_query/pallas_call | solution.py:119
  20.0 43.4 %all-to-all-done.kv0 = bf16[16,2,256,128]{3,2,1,0:T(8,128)(2,1)S(1)} async-done(((bf16[16,2,256,128]{3,2,1,0:T(8,128)(2,1)}), bf16[16,2,256,128]{3,2,1,0:T(8,128)(2,1)S(1)}, u32[]{:S(2)}, u32[]{:S(2)}) %all-to-all-start) | async-done | bytes 2097184 | tf_op jit(solution)/shard_map/all_to_all | solution.py:48
  63.4 5.1 %collective-permute-start.1 = (bf16[16,2,256,128]{3,2,1,0:T(8,128)(2,1)S(1)}, bf16[16,2,256,128]{3,2,1,0:T(8,128)(2,1)}, u32[]{:S(2)}, u32[]{:S(2)}) collective-permute-start(bf16[16,2,256,128]{3,2,1,0:T(8,128)(2,1)S(1)} %all-to-all-done.kv0), channel_id=1, source_target_pairs={{0,192},{4,196},{8,200},{12,204},{16,208},{20,212},{24,216},{28,22... | collective-permute-start | bytes 6291464 | tf_op jit(solution)/shard_map/ppermute | solution.py:472
  68.5 6.6 %all-to-all-start.1 = ((bf16[16,2,256,128]{3,2,1,0:T(8,128)(2,1)}), bf16[16,2,256,128]{3,2,1,0:T(8,128)(2,1)}, u32[]{:S(2)}, u32[]{:S(2)}) async-start(bf16[16,2,256,128]{3,2,1,0:T(8,128)(2,1)} %make_query.1), calls=%async_computation.1 | async-start | bytes 4194304 | tf_op jit(solution)/shard_map/all_to_all | solution.py:48
  75.1 1.2 collective-permute-start
  76.3 33.5 %collective-permute-done.1.kv2 = bf16[16,2,256,128]{3,2,1,0:T(8,128)(2,1)} collective-permute-done((bf16[16,2,256,128]{3,2,1,0:T(8,128)(2,1)S(1)}, bf16[16,2,256,128]{3,2,1,0:T(8,128)(2,1)}, u32[]{:S(2)}, u32[]{:S(2)}) %collective-permute-start.1) | collective-permute-done | bytes 2097184 | tf_op jit(solution)/shard_map/ppermute | solution.py:472
  109.8 3.3 %collective-permute-start.2 = (bf16[16,2,256,128]{3,2,1,0:T(8,128)(2,1)}, bf16[16,2,256,128]{3,2,1,0:T(8,128)(2,1)}, u32[]{:S(2)}, u32[]{:S(2)}) collective-permute-start(bf16[16,2,256,128]{3,2,1,0:T(8,128)(2,1)} %collective-permute-done.1.kv2), channel_id=1, source_target_pairs={{0,4},{4,0},{8,12},{12,8},{16,20},{20,16},{24,28},{28,24},{32,36},... | collective-permute-start | bytes 6291464 | tf_op jit(solution)/shard_map/ppermute | solution.py:52
  113.0 0.0 copy-done.3
  113.0 0.0 copy-done.5
  113.0 0.1 copy.12
  113.1 0.7 reshape_squeeze.3.ids_ref
  113.8 0.0 collective-permute-done.kv1
  113.8 8.8 %all-to-all-done.1.qg_ref = bf16[16,2,256,128]{3,2,1,0:T(8,128)(2,1)} async-done(((bf16[16,2,256,128]{3,2,1,0:T(8,128)(2,1)}), bf16[16,2,256,128]{3,2,1,0:T(8,128)(2,1)}, u32[]{:S(2)}, u32[]{:S(2)}) %all-to-all-start.1) | async-done | bytes 2097184 | tf_op jit(solution)/shard_map/all_to_all | solution.py:48
  122.7 0.0 collective-permute-done.2.kv3
  122.7 26.0 %attend.1 = (bf16[16,2,256,128]{3,2,1,0:T(8,128)(2,1)}, f32[16,2,256,128]{3,2,1,0:T(8,128)}, f32[16,2,256,128]{3,2,1,0:T(8,128)}, bf16[16,2,256,128]{3,2,1,0:T(8,128)(2,1)}, bf16[16,2,256,128]{3,2,1,0:T(8,128)(2,1)}) custom-call(s32[192]{0:T(256)} %reshape_squeeze.3.ids_ref, s32[1]{0:T(128)} %bitcast.me_ref, ...), custom_call_target="tpu_custom_call" | custom-call | flops 4831838208 | bytes 27262976 | tf_op jit(solution)/shard_map/attend/pallas_call | solution.py:265
  148.7 2.8 collective-permute-start.4
  151.5 5.2 %all-to-all-start.2 = ((bf16[16,2,256,128]{3,2,1,0:T(8,128)(2,1)}), bf16[16,2,256,128]{3,2,1,0:T(8,128)(2,1)}, u32[]{:S(2)}, u32[]{:S(2)}) async-start(bf16[16,2,256,128]{3,2,1,0:T(8,128)(2,1)} %get-tuple-element.31), calls=%async_computation.2 | async-start | bytes 4194304 | tf_op jit(solution)/shard_map/all_to_all | solution.py:48
  156.7 0.4 collective-permute-start.3
  157.0 0.0 collective-permute-done.4
  157.1 2.9 add_convert_fusion.1
  160.0 1.3 collective-permute-start.5
  161.3 0.0 collective-permute-done.3
  161.3 48.8 %collective-permute-done.5 = bf16[16,2,256,128]{3,2,1,0:T(8,128)(2,1)S(1)} collective-permute-done((bf16[16,2,256,128]{3,2,1,0:T(8,128)(2,1)S(1)}, bf16[16,2,256,128]{3,2,1,0:T(8,128)(2,1)S(1)}, u32[]{:S(2)}, u32[]{:S(2)}) %collective-permute-start.5) | collective-permute-done | bytes 2097184 | tf_op jit(solution)/shard_map/ppermute | solution.py:479
  210.1 2.2 add_convert_fusion
  212.3 0.0 all-to-all-done.2.home_ref
  212.3 7.2 %all-to-all-start.3 = ((bf16[16,2,256,128]{3,2,1,0:T(8,128)(2,1)}), bf16[16,2,256,128]{3,2,1,0:T(8,128)(2,1)}, u32[]{:S(2)}, u32[]{:S(2)}) async-start(bf16[16,2,256,128]{3,2,1,0:T(8,128)(2,1)} %add_convert_fusion), calls=%async_computation.3 | async-start | bytes 4194304 | tf_op jit(solution)/shard_map/all_to_all | solution.py:48
  219.5 0.1 copy.13
  219.7 0.0 copy-done
  219.7 0.0 copy-done.1
  219.7 4.3 %query_grads.1 = (bf16[256,2048]{1,0:T(8,128)(2,1)}, bf16[256,6144]{1,0:T(8,128)(2,1)}, f32[32,48,128]{2,1,0:T(8,128)S(1)}) custom-call(bf16[16,2,256,128]{3,2,1,0:T(8,128)(2,1)} %all-to-all-done.2.home_ref, bf16[256,4096]{1,0:T(8,128)(2,1)S(1)} %bitcast.11, bf16[96,256]{1,0:T(8,128)(2,1)S(1)} %bitcast.13, bf16[3,32,2048]{2,1,0:T(8,128)(2,1)S(1)} %copy-done.1), custom_call_target="tpu_custom_call" | custom-call | flops 134217728 | bytes 8388608 | tf_op jit(solution)/shard_map/query_grads/pallas_call | solution.py:356
  223.9 43.1 %all-to-all-done.3.home_ref = bf16[16,2,256,128]{3,2,1,0:T(8,128)(2,1)} async-done(((bf16[16,2,256,128]{3,2,1,0:T(8,128)(2,1)}), bf16[16,2,256,128]{3,2,1,0:T(8,128)(2,1)}, u32[]{:S(2)}, u32[]{:S(2)}) %all-to-all-start.3) | async-done | bytes 2097184 | tf_op jit(solution)/shard_map/all_to_all | solution.py:48
  267.0 5.4 %key_value_grads.1 = (bf16[256,6144]{1,0:T(8,128)(2,1)}, f32[32,72,128]{2,1,0:T(8,128)S(1)}, f32[32,72,128]{2,1,0:T(8,128)S(1)}) custom-call(s32[1]{0:T(128)} %bitcast.me_ref, bf16[256,6144]{1,0:T(8,128)(2,1)} %get-tuple-element.34._, f32[32,48,128]{2,1,0:T(8,128)S(1)} %get-tuple-element.35.other_ref, ...), custom_call_target="tpu_custom_call", output_to_operand_aliasing={{0}: (1, {})} | custom-call | flops 268435456 | bytes 10485760 | tf_op jit(solution)/shard_map/key_value_grads/pallas_call | solution.py:381
  272.4 2.8 collective-permute-start.6
  275.2 2.5 collective-permute-done.6
  277.7 0.1 add_convert_fusion.2
  277.8 20.7 %all_to_all.25 = bf16[32,72,128]{2,1,0:T(8,128)(2,1)S(1)} all-to-all(bf16[32,72,128]{2,1,0:T(8,128)(2,1)S(1)} %add_convert_fusion.2), channel_id=1, replica_groups={{0,8,16,24,32,40,48,56,64,72,80,88,96,104,112,120,128,136,144,152,160,1..., dimensions={0} | all-to-all | bytes 1179648 | tf_op jit(solution)/shard_map/all_to_all | solution.py:489
  298.5 0.1 convert_reduce_fusion
  298.6 2.5 collective-permute-start.9
  301.1 0.5 collective-permute-start.8
  301.7 0.6 collective-permute-start.7
  302.3 0.0 collective-permute-done.9
  302.3 3.2 %collective-permute-done.8 = f32[72,128]{1,0:T(8,128)S(1)} collective-permute-done((f32[72,128]{1,0:T(8,128)S(1)}, f32[72,128]{1,0:T(8,128)S(1)}, u32[]{:S(2)}, u32[]{:S(2)}) %collective-permute-start.8) | collective-permute-done | bytes 36896 | tf_op jit(solution)/shard_map/ppermute | solution.py:492
  305.5 0.4 collective-permute-done.7
  305.9 5.0 %collective-permute-start.10 = (f32[72,128]{1,0:T(8,128)S(1)}, f32[72,128]{1,0:T(8,128)S(1)}, u32[]{:S(2)}, u32[]{:S(2)}) collective-permute-start(f32[72,128]{1,0:T(8,128)S(1)} %add_add_fusion.mine_ref), channel_id=1, source_target_pairs={{0,4},{4,0},{8,12},{12,8},{16,20},{20,16},{24,28},{28,24},{32,36},... | collective-permute-start | bytes 110600 | tf_op jit(solution)/shard_map/ppermute | solution.py:52
  310.9 0.9 collective-permute-done.10.other_ref
  311.8 0.9 finish.1
  (9 shorter events, 0.0 us)
Async XLA Ops:
  5.6 57.8 %all-to-all-start = ((bf16[16,2,256,128]{3,2,1,0:T(8,128)(2,1)}), bf16[16,2,256,128]{3,2,1,0:T(8,128)(2,1)S(1)}, u32[]{:S(2)}, u32[]{:S(2)}) async-start(bf16[16,2,256,128]{3,2,1,0:T(8,128)(2,1)} %get-tuple-element.24), calls=%async_computation | async-start | bytes 4194304 | tf_op jit(solution)/shard_map/all_to_all | solution.py:48
  20.0 93.1 %copy-start.5 = (s32[1,64,3]{1,0,2:T(1,128)S(1)}, s32[1,64,3]{1,0,2:T(1,128)}, u32[]{:S(2)}) copy-start(s32[1,64,3]{1,0,2:T(1,128)} %param.10) | copy-start | bytes 2308
  63.4 49.6 %copy-start.3 = (bf16[16,2,256,128]{3,2,1,0:T(8,128)(2,1)}, bf16[16,2,256,128]{3,2,1,0:T(8,128)(2,1)S(1)}, u32[]{:S(2)}) copy-start(bf16[16,2,256,128]{3,2,1,0:T(8,128)(2,1)S(1)} %all-to-all-done.kv0) | copy-start | bytes 6291460
  63.4 46.4 %collective-permute-start.1 = (bf16[16,2,256,128]{3,2,1,0:T(8,128)(2,1)S(1)}, bf16[16,2,256,128]{3,2,1,0:T(8,128)(2,1)}, u32[]{:S(2)}, u32[]{:S(2)}) collective-permute-start(bf16[16,2,256,128]{3,2,1,0:T(8,128)(2,1)S(1)} %all-to-all-done.kv0), channel_id=1, source_target_pairs={{0,192},{4,196},{8,200},{12,204},{16,208},{20,212},{24,216},{28,22... | collective-permute-start | bytes 6291464 | tf_op jit(solution)/shard_map/ppermute | solution.py:472
  68.5 54.1 %all-to-all-start.1 = ((bf16[16,2,256,128]{3,2,1,0:T(8,128)(2,1)}), bf16[16,2,256,128]{3,2,1,0:T(8,128)(2,1)}, u32[]{:S(2)}, u32[]{:S(2)}) async-start(bf16[16,2,256,128]{3,2,1,0:T(8,128)(2,1)} %make_query.1), calls=%async_computation.1 | async-start | bytes 4194304 | tf_op jit(solution)/shard_map/all_to_all | solution.py:48
  75.1 38.7 %collective-permute-start = (bf16[16,2,256,128]{3,2,1,0:T(8,128)(2,1)S(1)}, bf16[16,2,256,128]{3,2,1,0:T(8,128)(2,1)}, u32[]{:S(2)}, u32[]{:S(2)}) collective-permute-start(bf16[16,2,256,128]{3,2,1,0:T(8,128)(2,1)S(1)} %all-to-all-done.kv0), channel_id=1, source_target_pairs={{0,4},{4,0},{8,12},{12,8},{16,20},{20,16},{24,28},{28,24},{32,36},... | collective-permute-start | bytes 6291464 | tf_op jit(solution)/shard_map/ppermute | solution.py:52
  109.8 12.9 %collective-permute-start.2 = (bf16[16,2,256,128]{3,2,1,0:T(8,128)(2,1)}, bf16[16,2,256,128]{3,2,1,0:T(8,128)(2,1)}, u32[]{:S(2)}, u32[]{:S(2)}) collective-permute-start(bf16[16,2,256,128]{3,2,1,0:T(8,128)(2,1)} %collective-permute-done.1.kv2), channel_id=1, source_target_pairs={{0,4},{4,0},{8,12},{12,8},{16,20},{20,16},{24,28},{28,24},{32,36},... | collective-permute-start | bytes 6291464 | tf_op jit(solution)/shard_map/ppermute | solution.py:52
  148.7 8.3 %collective-permute-start.4 = (bf16[16,2,256,128]{3,2,1,0:T(8,128)(2,1)}, bf16[16,2,256,128]{3,2,1,0:T(8,128)(2,1)S(1)}, u32[]{:S(2)}, u32[]{:S(2)}) collective-permute-start(bf16[16,2,256,128]{3,2,1,0:T(8,128)(2,1)} %get-tuple-element.30), channel_id=1, source_target_pairs={{0,4},{4,0},{8,12},{12,8},{16,20},{20,16},{24,28},{28,24},{32,36},... | collective-permute-start | bytes 6291464 | tf_op jit(solution)/shard_map/ppermute | solution.py:52
  151.5 60.8 %all-to-all-start.2 = ((bf16[16,2,256,128]{3,2,1,0:T(8,128)(2,1)}), bf16[16,2,256,128]{3,2,1,0:T(8,128)(2,1)}, u32[]{:S(2)}, u32[]{:S(2)}) async-start(bf16[16,2,256,128]{3,2,1,0:T(8,128)(2,1)} %get-tuple-element.31), calls=%async_computation.2 | async-start | bytes 4194304 | tf_op jit(solution)/shard_map/all_to_all | solution.py:48
  156.7 4.6 %collective-permute-start.3 = (bf16[16,2,256,128]{3,2,1,0:T(8,128)(2,1)}, bf16[16,2,256,128]{3,2,1,0:T(8,128)(2,1)S(1)}, u32[]{:S(2)}, u32[]{:S(2)}) collective-permute-start(bf16[16,2,256,128]{3,2,1,0:T(8,128)(2,1)} %get-tuple-element.28), channel_id=1, source_target_pairs={{0,4},{4,0},{8,12},{12,8},{16,20},{20,16},{24,28},{28,24},{32,36},... | collective-permute-start | bytes 6291464 | tf_op jit(solution)/shard_map/ppermute | solution.py:52
  157.1 53.1 %copy-start.2 = (f32[16,2,256,128]{3,2,1,0:T(8,128)S(1)}, f32[16,2,256,128]{3,2,1,0:T(8,128)}, u32[]{:S(2)}) copy-start(f32[16,2,256,128]{3,2,1,0:T(8,128)} %get-tuple-element.27) | copy-start | bytes 12582916
  160.0 50.1 %collective-permute-start.5 = (bf16[16,2,256,128]{3,2,1,0:T(8,128)(2,1)S(1)}, bf16[16,2,256,128]{3,2,1,0:T(8,128)(2,1)S(1)}, u32[]{:S(2)}, u32[]{:S(2)}) collective-permute-start(bf16[16,2,256,128]{3,2,1,0:T(8,128)(2,1)S(1)} %add_convert_fusion.1), channel_id=1, source_target_pairs={{192,0},{196,4},{200,8},{204,12},{208,16},{212,20},{216,24},{220,2... | collective-permute-start | bytes 6291464 | tf_op jit(solution)/shard_map/ppermute | solution.py:479
  212.3 7.2 %copy-start.4 = (bf16[256,96]{1,0:T(8,128)(2,1)S(1)}, bf16[256,96]{1,0:T(8,128)(2,1)}, u32[]{:S(2)}) copy-start(bf16[256,96]{1,0:T(8,128)(2,1)} %get-tuple-element.23.low_ref) | copy-start | bytes 147460
  212.3 7.3 %copy-start = (bf16[1,256,4096]{2,1,0:T(8,128)(2,1)S(1)}, bf16[1,256,4096]{2,1,0:T(8,128)(2,1)}, u32[]{:S(2)}) copy-start(bf16[1,256,4096]{2,1,0:T(8,128)(2,1)} %param.6) | copy-start | bytes 6291460
  212.3 7.4 %copy-start.1 = (bf16[3,32,2048]{2,1,0:T(8,128)(2,1)S(1)}, bf16[3,32,2048]{2,1,0:T(8,128)(2,1)}, u32[]{:S(2)}) copy-start(bf16[3,32,2048]{2,1,0:T(8,128)(2,1)} %up_ref.7) | copy-start | bytes 1179652
  212.3 54.7 %all-to-all-start.3 = ((bf16[16,2,256,128]{3,2,1,0:T(8,128)(2,1)}), bf16[16,2,256,128]{3,2,1,0:T(8,128)(2,1)}, u32[]{:S(2)}, u32[]{:S(2)}) async-start(bf16[16,2,256,128]{3,2,1,0:T(8,128)(2,1)} %add_convert_fusion), calls=%async_computation.3 | async-start | bytes 4194304 | tf_op jit(solution)/shard_map/all_to_all | solution.py:48
  272.4 5.3 %collective-permute-start.6 = (f32[32,72,128]{2,1,0:T(8,128)S(1)}, f32[32,72,128]{2,1,0:T(8,128)S(1)}, u32[]{:S(2)}, u32[]{:S(2)}) collective-permute-start(f32[32,72,128]{2,1,0:T(8,128)S(1)} %get-tuple-element.39), channel_id=1, source_target_pairs={{0,4},{4,0},{8,12},{12,8},{16,20},{20,16},{24,28},{28,24},{32,36},... | collective-permute-start | bytes 3538952 | tf_op jit(solution)/shard_map/ppermute | solution.py:52
  298.6 3.7 %collective-permute-start.9 = (f32[72,128]{1,0:T(8,128)S(1)}, f32[72,128]{1,0:T(8,128)S(1)}, u32[]{:S(2)}, u32[]{:S(2)}) collective-permute-start(f32[72,128]{1,0:T(8,128)S(1)} %convert_reduce_fusion), channel_id=1, source_target_pairs={{0,3},{1,0},{2,1},{3,2},{4,7},{5,4},{6,5},{7,6},{8,11},{9,8},{10,9... | collective-permute-start | bytes 110600 | tf_op jit(solution)/shard_map/ppermute | solution.py:492
  301.1 4.3 %collective-permute-start.8 = (f32[72,128]{1,0:T(8,128)S(1)}, f32[72,128]{1,0:T(8,128)S(1)}, u32[]{:S(2)}, u32[]{:S(2)}) collective-permute-start(f32[72,128]{1,0:T(8,128)S(1)} %convert_reduce_fusion), channel_id=1, source_target_pairs={{0,2},{1,3},{2,0},{3,1},{4,6},{5,7},{6,4},{7,5},{8,10},{9,11},{10,... | collective-permute-start | bytes 110600 | tf_op jit(solution)/shard_map/ppermute | solution.py:492
  301.7 4.2 %collective-permute-start.7 = (f32[72,128]{1,0:T(8,128)S(1)}, f32[72,128]{1,0:T(8,128)S(1)}, u32[]{:S(2)}, u32[]{:S(2)}) collective-permute-start(f32[72,128]{1,0:T(8,128)S(1)} %convert_reduce_fusion), channel_id=1, source_target_pairs={{0,1},{1,2},{2,3},{3,0},{4,5},{5,6},{6,7},{7,4},{8,9},{9,10},{10,1... | collective-permute-start | bytes 110600 | tf_op jit(solution)/shard_map/ppermute | solution.py:492
  305.9 5.9 %collective-permute-start.10 = (f32[72,128]{1,0:T(8,128)S(1)}, f32[72,128]{1,0:T(8,128)S(1)}, u32[]{:S(2)}, u32[]{:S(2)}) collective-permute-start(f32[72,128]{1,0:T(8,128)S(1)} %add_add_fusion.mine_ref), channel_id=1, source_target_pairs={{0,4},{4,0},{8,12},{12,8},{16,20},{20,16},{24,28},{28,24},{32,36},... | collective-permute-start | bytes 110600 | tf_op jit(solution)/shard_map/ppermute | solution.py:52

commit v3 on v2

--- a/solution.py
+++ b/solution.py
@@ -22,6 +22,7 @@
 TN = (((0,), (0,)), ((), ()))
 TILES = 32
 PER_STEP = 4
+STEPS = 4
 
 
 def place(y, z, core):
@@ -161,9 +162,11 @@
 
 def attend_kernel(
     ids_ref, me_ref, qg_ref, kv0, kv1, kv2, kv3,
-    out_ref, own_ref, far_ref, core_ref, farcore_ref, kvs, acc, staged, sem,
+    out_ref, own_ref, far_ref, core_ref, farcore_ref,
+    kvs, acc, staged, sem, out_sem,
 ):
     step = pl.program_id(0)
+    flip = (me_ref[0] >> 5) * 8
 
     @pl.when(step == 0)
     def _():
@@ -178,7 +181,7 @@
             acc[i] = jnp.zeros((2, BLK, HD), jnp.float32)
             return 0
 
-        lax.fori_loop(0, 64, clear, 0)
+        lax.fori_loop(16, 64, clear, 0)
         for copy in copies:
             copy.wait()
 
@@ -187,18 +190,15 @@
     causal = key_row <= query_col
     work = []
     for sub in range(PER_STEP):
-        spots, biases = slots_of(ids_ref, me_ref, step * PER_STEP + sub)
-        work.append((spots, biases, qg_ref[sub, 0], qg_ref[sub, 1]))
-    scores = []
-    for spots, biases, q, g in work:
-        parts = []
+        spots, biases = slots_of(ids_ref, me_ref, (step * PER_STEP + sub) ^ flip)
+        q = qg_ref[sub, 0]
+        s = []
         for t in range(3):
-            s = lax.dot_general(kvs[spots[t], 0], q, NT, preferred_element_type=jnp.float32)
-            s = s * LOG2_SCALE
-            parts.append(jnp.where(causal, s, -jnp.inf) if t == 0 else s + biases[t])
-        scores.append(parts)
+            x = lax.dot_general(kvs[spots[t], 0], q, NT, preferred_element_type=jnp.float32) * LOG2_SCALE
+            s.append(jnp.where(causal, x, -jnp.inf) if t == 0 else x + biases[t])
+        work.append((spots, q, qg_ref[sub, 1], s))
     middle = []
-    for (spots, biases, q, g), s in zip(work, scores):
+    for sub, (spots, q, g, s) in enumerate(work):
         top = jnp.max(jnp.maximum(jnp.maximum(s[0], s[1]), s[2]), axis=0, keepdims=True)
         shifted = [jnp.exp2(x - top) for x in s]
         inverse = 1.0 / jnp.sum(shifted[0] + shifted[1] + shifted[2], axis=0, keepdims=True)
@@ -209,46 +209,56 @@
             part = lax.dot_general(kvs[spots[t], 1], weights[t], TN, preferred_element_type=jnp.float32)
             out = part if out is None else out + part
         middle.append((probs, weights, out))
-    for sub in range(PER_STEP):
-        spots, biases, q, g = work[sub]
-        probs, weights, out = middle[sub]
-        attn = out.T.astype(jnp.bfloat16)
+    deltas = []
+    for sub, (spots, q, g, s) in enumerate(work):
+        attn = middle[sub][2].T.astype(jnp.bfloat16)
         out_ref[sub, 0] = attn
         product = attn.astype(jnp.float32) * g.astype(jnp.float32)
-        delta = jnp.sum(product.T, axis=0, keepdims=True)
+        deltas.append(jnp.sum(product.T, axis=0, keepdims=True))
+
+    def score_grads(sub):
+        spots, _, g, _ = work[sub]
+        probs = middle[sub][0]
+        found = []
+        for t in range(3):
+            dprobs = lax.dot_general(kvs[spots[t], 1], g, NT, preferred_element_type=jnp.float32)
+            found.append((probs[t] * (dprobs - deltas[sub]) * SCORE_SCALE).astype(jnp.bfloat16))
+        return found
+
+    ahead = score_grads(0)
+    for sub, (spots, q, g, s) in enumerate(work):
+        dscores = ahead
+        if sub + 1 < PER_STEP:
+            ahead = score_grads(sub + 1)
+        weights = middle[sub][1]
         dq = None
         for t in range(3):
-            dprobs = lax.dot_general(kvs[spots[t], 1], g, NT, preferred_element_type=jnp.float32)
-            dscores = (probs[t] * (dprobs - delta) * SCORE_SCALE).astype(jnp.bfloat16)
-            part = lax.dot_general(kvs[spots[t], 0], dscores, TN, preferred_element_type=jnp.float32)
+            part = lax.dot_general(kvs[spots[t], 0], dscores[t], TN, preferred_element_type=jnp.float32)
             dq = part if dq is None else dq + part
-            dk = jnp.dot(dscores, q, preferred_element_type=jnp.float32)
+            dk = jnp.dot(dscores[t], q, preferred_element_type=jnp.float32)
             dv = jnp.dot(weights[t], g, preferred_element_type=jnp.float32)
-            if t > 0:
-                dk = dk.astype(jnp.bfloat16).astype(jnp.float32)
-                dv = dv.astype(jnp.bfloat16).astype(jnp.float32)
-            acc[spots[t], 0] += dk
-            acc[spots[t], 1] += dv
+            if t == 0:
+                acc[spots[t], 0] = dk
+                acc[spots[t], 1] = dv
+            else:
+                acc[spots[t], 0] += dk.astype(jnp.bfloat16).astype(jnp.float32)
+                acc[spots[t], 1] += dv.astype(jnp.bfloat16).astype(jnp.float32)
         out_ref[sub, 1] = dq.T.astype(jnp.bfloat16)
 
-    @pl.when(step == pl.num_programs(0) - 1)
+    @pl.when(step == STEPS - 1)
     def _():
         copies = []
 
         def send(source, target):
-            copy = pltpu.make_async_copy(source, target, sem.at[len(copies)])
+            copy = pltpu.make_async_copy(source, target, out_sem.at[len(copies)])
             copy.start()
             copies.append(copy)
 
-        for n, (at, target) in enumerate(((48, farcore_ref), (16, core_ref))):
-
+        send(acc.at[pl.ds(0, 16)], own_ref)
+        for n, (at, target) in enumerate(((48, farcore_ref), (32, far_ref), (16, core_ref))):
             def cast(i, _, n=n, at=at):
                 staged[n * 16 + i] = acc[at + i].astype(jnp.bfloat16)
                 return 0
-
-            if n == 1:
-                send(acc.at[pl.ds(32, 16)], far_ref)
-                send(acc.at[pl.ds(0, 16)], own_ref)
             lax.fori_loop(0, 16, cast, 0)
             send(staged.at[pl.ds(n * 16, 16)], target)
         for copy in copies:
@@ -261,22 +271,25 @@
 def attend(ids, me, query, key_values):
     wide = jax.ShapeDtypeStruct((16, 2, BLK, HD), jnp.float32)
     narrow = jax.ShapeDtypeStruct((16, 2, BLK, HD), jnp.bfloat16)
-    rows = pl.BlockSpec((PER_STEP, 2, BLK, HD), lambda p, *_: (p, 0, 0, 0))
+    rows = pl.BlockSpec(
+        (PER_STEP, 2, BLK, HD), lambda i, ids_ref, me_ref: (i ^ ((me_ref[0] >> 5) * 2), 0, 0, 0)
+    )
     return pl.pallas_call(
         attend_kernel,
         grid_spec=pltpu.PrefetchScalarGridSpec(
             num_scalar_prefetch=2,
-            grid=(16 // PER_STEP,),
+            grid=(STEPS,),
             in_specs=[rows] + [ANY] * 4,
             out_specs=[rows] + [ANY] * 4,
             scratch_shapes=[
                 pltpu.VMEM((64, 2, BLK, HD), jnp.bfloat16),
                 pltpu.VMEM((64, 2, BLK, HD), jnp.float32),
-                pltpu.VMEM((32, 2, BLK, HD), jnp.bfloat16),
+                pltpu.VMEM((48, 2, BLK, HD), jnp.bfloat16),
+                pltpu.SemaphoreType.DMA((4,)),
                 pltpu.SemaphoreType.DMA((4,)),
             ],
         ),
-        out_shape=[narrow, wide, wide, narrow, narrow],
+        out_shape=[narrow, wide, narrow, narrow, narrow],
         compiler_params=pltpu.CompilerParams(vmem_limit_bytes=VMEM_BYTES),
         cost_estimate=pl.CostEstimate(
             flops=16 * 6 * 2 * BLK * 3 * BLK * HD,
@@ -287,97 +300,119 @@
     )(ids, me, query, *key_values)
 
 
-def write_terms(terms, base, head, tok_ref, low, up):
-    dlow = None
-    for h in range(HEADS):
-        g = head(h)
-        cols = slice(h * HD, (h + 1) * HD)
-        part = lax.dot_general(up[:, cols], g, NT, preferred_element_type=jnp.float32)
-        dlow = part if dlow is None else dlow + part
-        up_term = jnp.dot(low, g, preferred_element_type=jnp.float32) * (ADAPTER_SCALE * GRAD_SCALE)
-        for side in range(2):
-            cut = up_term[:, side * 64 : (side + 1) * 64]
-            terms[2 * h + side, base + 32 : base + 48, :] = jnp.concatenate([cut[0:16], cut[16:32]], axis=1)
-    dlow = (dlow * ADAPTER_SCALE).astype(jnp.bfloat16)
-    for t in range(TILES):
-        down_term = jnp.dot(dlow, tok_ref[:, t * 128 : (t + 1) * 128], preferred_element_type=jnp.float32)
-        terms[t, base : base + 32, :] = down_term * GRAD_SCALE
-
-
-def query_grads_kernel(home_ref, tok_ref, low_ref, up_ref, attn_ref, gp_ref, terms):
+def write_terms(heads, lows, ups, tok_ref, at):
+    dlows = []
+    for member, (head, low, up) in enumerate(zip(heads, lows, ups)):
+        dlow = None
+        for pair in range(HEADS // 2):
+            g = jnp.concatenate([head(2 * pair), head(2 * pair + 1)], axis=1)
+            part = lax.dot_general(up(pair), g, NT, preferred_element_type=jnp.float32)
+            dlow = part if dlow is None else dlow + part
+            up_term = jnp.dot(low, g, preferred_element_type=jnp.float32) * (ADAPTER_SCALE * GRAD_SCALE)
+            for n in range(4):
+                cut = up_term[:, n * 64 : (n + 1) * 64]
+                ref, slot = at(member, 4 * pair + n)
+                ref[slot, 32:48, :] = jnp.concatenate([cut[0:16], cut[16:32]], axis=1)
+        dlows.append((dlow * ADAPTER_SCALE).astype(jnp.bfloat16))
+    dlow = dlows[0] if len(dlows) == 1 else jnp.concatenate(dlows, axis=0)
+    for pair in range(TILES // 2):
+        rows = tok_ref[:, pair * 256 : (pair + 1) * 256]
+        down_term = jnp.dot(dlow, rows, preferred_element_type=jnp.float32) * GRAD_SCALE
+        for member in range(len(dlows)):
+            for side in range(2):
+                ref, slot = at(member, 2 * pair + side)
+                ref[slot, 0:32, :] = down_term[member * R : (member + 1) * R, side * 128 : (side + 1) * 128]
+
+
+def query_grads_kernel(me_ref, home_ref, tok_ref, low_ref, up_ref, attn_ref, gp_ref, keep_ref, send_ref, terms):
+    me = me_ref[0]
     for h in range(HEADS):
         cols = slice(h * HD, (h + 1) * HD)
         attn_ref[:, cols] = home_ref[h, 0]
         gp_ref[:, cols] = home_ref[h, 1]
-    write_terms(terms, 0, lambda h: home_ref[h, 1], tok_ref, low_ref[...], up_ref[0])
+
+    write_terms(
+        [lambda h: home_ref[h, 1]],
+        [low_ref[...]],
+        [lambda pair: up_ref[0, :, pair * 256 : (pair + 1) * 256]],
+        tok_ref,
+        lambda member, t: (terms, t),
+    )
+
+    @pl.when((me & 1) == 0)
+    def _():
+        keep_ref[...] = terms[:, 0:24, :]
+        send_ref[...] = terms[:, 24:48, :].astype(jnp.bfloat16)
+
+    @pl.when((me & 1) == 1)
+    def _():
+        keep_ref[...] = terms[:, 24:48, :]
+        send_ref[...] = terms[:, 0:24, :].astype(jnp.bfloat16)
 
 
 def key_value_grads_kernel(
-    me_ref, _, other_ref, home_ref, tok_ref, low_ref, up_ref, gp_ref, keep_ref, send_ref, terms, rows, sem
+    me_ref, _, home_ref, tok_ref, low_ref, up_ref, gp_ref, keep_ref, send_ref, terms_k, terms_v, rows, sem
 ):
     for side in range(2):
         for h in range(HEADS):
             rows[:, side * HQ + h * HD : side * HQ + (h + 1) * HD] = home_ref[h, side]
     copy = pltpu.make_async_copy(rows, gp_ref.at[:, pl.ds(HQ, 2 * HQ)], sem)
     copy.start()
-    for side in range(2):
-        write_terms(
-            terms,
-            side * 48,
-            lambda h: home_ref[h, side],
-            tok_ref,
-            low_ref[(side + 1) * R : (side + 2) * R, :],
-            up_ref[side + 1],
-        )
-
-    def first(ref):
-        ref[:, 0:48, :] = other_ref[...]
-        ref[:, 48:72, :] = terms[:, 0:24, :]
-
-    def second(ref):
-        ref[...] = terms[:, 24:96, :]
-
+    write_terms(
+        [lambda h: home_ref[h, 0], lambda h: home_ref[h, 1]],
+        [low_ref[R : 2 * R, :], low_ref[2 * R : 3 * R, :]],
+        [
+            lambda pair: up_ref[1, :, pair * 256 : (pair + 1) * 256],
+            lambda pair: up_ref[2, :, pair * 256 : (pair + 1) * 256],
+        ],
+        tok_ref,
+        lambda member, t: ((terms_k, terms_v)[member], t),
+    )
     core = me_ref[0] & 1
 
     @pl.when(core == 0)
     def _():
-        first(keep_ref)
-        second(send_ref)
+        keep_ref[...] = terms_k[...]
+        send_ref[...] = terms_v[...].astype(jnp.bfloat16)
 
     @pl.when(core == 1)
     def _():
-        first(send_ref)
-        second(keep_ref)
+        keep_ref[...] = terms_v[...]
+        send_ref[...] = terms_k[...].astype(jnp.bfloat16)
 
     copy.wait()
 
 
-def query_grads(home, tokens, low_t, up_projection):
+def query_grads(me, home, tokens, low_t, up_projection):
     return pl.pallas_call(
         query_grads_kernel,
-        grid=(1,),
-        in_specs=[
-            whole(HEADS, 2, BLK, HD),
-            whole(BLK, D),
-            whole(R, BLK),
-            whole(1, R, HQ),
-        ],
-        out_specs=[whole(BLK, HQ), whole(BLK, HQ), whole(TILES, 48, 128)],
+        grid_spec=pltpu.PrefetchScalarGridSpec(
+            num_scalar_prefetch=1,
+            grid=(1,),
+            in_specs=[
+                whole(HEADS, 2, BLK, HD),
+                whole(BLK, D),
+                whole(R, BLK),
+                whole(1, R, HQ),
+            ],
+            out_specs=[whole(BLK, HQ), whole(BLK, HQ), whole(TILES, 24, 128), whole(TILES, 24, 128)],
+            scratch_shapes=[pltpu.VMEM((TILES, 48, 128), jnp.float32)],
+        ),
         out_shape=[
             jax.ShapeDtypeStruct((BLK, HQ), jnp.bfloat16),
             jax.ShapeDtypeStruct((BLK, 3 * HQ), jnp.bfloat16),
-            jax.ShapeDtypeStruct((TILES, 48, 128), jnp.float32),
+            jax.ShapeDtypeStruct((TILES, 24, 128), jnp.float32),
+            jax.ShapeDtypeStruct((TILES, 24, 128), jnp.bfloat16),
         ],
         compiler_params=pltpu.CompilerParams(vmem_limit_bytes=24 * 1024 * 1024),
         cost_estimate=pl.CostEstimate(
             flops=2 * BLK * R * (D + 2 * HQ), bytes_accessed=8 * 2**20, transcendentals=0
         ),
         name="query_grads",
-    )(home, tokens, low_t, up_projection)
-
-
-def key_value_grads(me, grad_proj, terms_q, home, tokens, low_t, up_projection):
-    piece = jax.ShapeDtypeStruct((TILES, 72, 128), jnp.float32)
+    )(me, home, tokens, low_t, up_projection)
+
+
+def key_value_grads(me, grad_proj, home, tokens, low_t, up_projection):
     return pl.pallas_call(
         key_value_grads_kernel,
         grid_spec=pltpu.PrefetchScalarGridSpec(
@@ -385,50 +420,53 @@
             grid=(1,),
             in_specs=[
                 ANY,
-                whole(TILES, 48, 128),
                 whole(HEADS, 2, BLK, HD),
                 whole(BLK, D),
                 whole(3 * R, BLK),
                 whole(3, R, HQ),
             ],
-            out_specs=[
-                ANY,
-                whole(TILES, 72, 128),
-                whole(TILES, 72, 128),
-            ],
+            out_specs=[ANY, whole(TILES, 48, 128), whole(TILES, 48, 128)],
             scratch_shapes=[
-                pltpu.VMEM((TILES, 96, 128), jnp.float32),
+                pltpu.VMEM((TILES, 48, 128), jnp.float32),
+                pltpu.VMEM((TILES, 48, 128), jnp.float32),
                 pltpu.VMEM((BLK, 2 * HQ), jnp.bfloat16),
                 pltpu.SemaphoreType.DMA,
             ],
         ),
-        out_shape=[jax.ShapeDtypeStruct((BLK, 3 * HQ), jnp.bfloat16), piece, piece],
+        out_shape=[
+            jax.ShapeDtypeStruct((BLK, 3 * HQ), jnp.bfloat16),
+            jax.ShapeDtypeStruct((TILES, 48, 128), jnp.float32),
+            jax.ShapeDtypeStruct((TILES, 48, 128), jnp.bfloat16),
+        ],
         input_output_aliases={1: 0},
-        compiler_params=pltpu.CompilerParams(vmem_limit_bytes=28 * 1024 * 1024),
+        compiler_params=pltpu.CompilerParams(vmem_limit_bytes=24 * 1024 * 1024),
         cost_estimate=pl.CostEstimate(
-            flops=4 * BLK * R * (D + 2 * HQ), bytes_accessed=10 * 2**20, transcendentals=0
+            flops=4 * BLK * R * (D + 2 * HQ), bytes_accessed=8 * 2**20, transcendentals=0
         ),
         name="key_value_grads",
-    )(me, grad_proj, terms_q, home, tokens, low_t, up_projection)
+    )(me, grad_proj, home, tokens, low_t, up_projection)
 
 
 def finish_kernel(lane_ref, mine_ref, other_ref, down_ref, up_ref, full, down_t, up_t):
     lane = lane_ref[0]
 
+    def fill(first, second):
+        full[0:72] = first[...]
+        full[72:96] = second[48:72]
+        full[96:144] = second[0:48]
+
     @pl.when(lane < 4)
     def _():
-        full[0:72] = mine_ref[...]
-        full[72:144] = other_ref[...]
+        fill(mine_ref, other_ref)
 
     @pl.when(lane >= 4)
     def _():
-        full[0:72] = other_ref[...]
-        full[72:144] = mine_ref[...]
-
-    for m in range(3):
-        down_t[...] = full[m * 48 : m * 48 + 32, :].T
+        fill(other_ref, mine_ref)
+
+    for m, start in enumerate((48, 0, 96)):
+        down_t[...] = full[start : start + 32, :].T
         down_ref[m] = down_t[pl.ds(lane * 16, 16), :]
-        up_t[...] = full[m * 48 + 32 : m * 48 + 48, :].T
+        up_t[...] = full[start + 32 : start + 48, :].T
         up_ref[m, :, 0:16] = up_t[pl.ds(lane * 8, 8), :]
         up_ref[m, :, 16:32] = up_t[pl.ds(lane * 8 + 64, 8), :]
 
@@ -475,17 +513,20 @@
         ids, me, query, (key_value, swap(key_value), far, swap(far))
     )
 
-    far_sum = (far_part + swap(farcore_part).astype(jnp.float32)).astype(jnp.bfloat16)
-    returned = lax.ppermute(far_sum, "ctx", TO_EARLIER)
+    def both_cores(keep, send):
+        return (keep + swap(send).astype(jnp.float32)).astype(jnp.bfloat16)
+
+    far_sum = far_part.astype(jnp.float32) + swap(farcore_part).astype(jnp.float32)
+    returned = lax.ppermute(far_sum.astype(jnp.bfloat16), "ctx", TO_EARLIER)
     out_home = to_heads(out)
     total = own + swap(core_part).astype(jnp.float32) + returned.astype(jnp.float32)
     total, out_home = after(total.astype(jnp.bfloat16), out_home)
     total_home = to_heads(total)
-    attn_rows, grad_proj, terms_q = query_grads(out_home, tokens, low_t, up_projection)
-    grad_proj, keep, send = key_value_grads(
-        me, grad_proj, terms_q, total_home, tokens, low_t, up_projection
-    )
-    pieces = (keep + swap(send)).astype(jnp.bfloat16)
+    attn_rows, grad_proj, keep, send = query_grads(me, out_home, tokens, low_t, up_projection)
+    pieces_q = both_cores(keep, send)
+    total_home, pieces_q = after(total_home, pieces_q)
+    grad_proj, keep, send = key_value_grads(me, grad_proj, total_home, tokens, low_t, up_projection)
+    pieces = jnp.concatenate([both_cores(keep, send), pieces_q], axis=1)
     pieces = lax.all_to_all(pieces, "ctx", 0, 0, axis_index_groups=TILE_GROUPS, tiled=True)
     mine = jnp.sum(pieces.astype(jnp.float32), axis=0)
     others = [

time: 313 us -> 307 us (0.981)
  Pallas kernels: 45.7 us -> 41.3 us
    pallas_call x1, Pallas kernels: 26 us -> 21.4 us  [attend(): pl.pallas_call(attend_kernel, grid_spec=pltpu.PrefetchScalarGridSpec(num_...]
    ppermute x6 -> x7, starting transfers between devices: 15.4 us -> 16.5 us  [swap(): return lax.ppermute(x, 'ctx', CORE_PAIRS)]
  transfers between devices with their start and end apart: 15 -> 16, of which waited for: 9 -> 11; matrix products, arithmetic and copies ran while one was open for 2% -> 2% of each run, Pallas kernels for 3% -> 3%
where the time goes in v3:
time: 307 us; the launch traced here: 306 us
  waiting for transfers between devices  182 us (59%)
  starting transfers between devices  55.8 us (18%)
  Pallas kernels  41.3 us (13%)
  blocking collectives  20.7 us (7%)
  other arithmetic  4.95 us (2%)
    all_to_all x4, waiting for transfers between devices, to_heads(): lax.all_to_all(x, 'ctx', 0, 0, axis_index_groups=HEAD_GROUPS, tiled=True)  92.7 us
    ppermute x1, waiting for transfers between devices, shards(): returned = lax.ppermute(far_sum.astype(jnp.bfloat16), 'ctx', TO_EARLIER)  48.6 us
    ppermute x1, waiting for transfers between devices, shards(): far = lax.ppermute(key_value, 'ctx', TO_LATER)  33.5 us
    all_to_all x4, starting transfers between devices, to_heads(): lax.all_to_all(x, 'ctx', 0, 0, axis_index_groups=HEAD_GROUPS, tiled=True)  29.2 us
    pallas_call x1, Pallas kernels, attend(): pl.pallas_call(attend_kernel, grid_spec=pltpu.PrefetchScalarGridSpec(num_...  21.4 us
    all_to_all x1, blocking collectives, shards(): lax.all_to_all(pieces, 'ctx', 0, 0, axis_index_groups=TILE_GROUPS, tiled=...  20.7 us
    ppermute x7, starting transfers between devices, swap(): return lax.ppermute(x, 'ctx', CORE_PAIRS)  16.5 us
  transfers between devices with their start and end apart: 16, of which 11 were waited for; matrix products, arithmetic and copies ran while one was open for 2% of the time, Pallas kernels for 3%

profile of v3, /device:TPU:1, one launch (start us, length us, event | category | flops | bytes accessed | tf_op | source)
XLA Modules:
  0.0 306.3 jit_solution(9377062685749680935)
XLA Ops:
  0.6 5.0 %make_key_value.1 = (bf16[16,2,256,128]{3,2,1,0:T(8,128)(2,1)}, bf16[256,96]{1,0:T(8,128)(2,1)}) custom-call(bf16[256,4096]{1,0:T(8,128)(2,1)} %bitcast.10, bf16[3,32,4096]{2,1,0:T(8,128)(2,1)} %bitcast.20, bf16[256,6144]{1,0:T(8,128)(2,1)} %bitcast.15, bf16[256,6144]{1,0:T(8,128)(2,1)} %bitcast.16, bf16[3,32,2048]{2,1,0:T(8,128)(2,1)} %up_ref.7), custom_call_target="tpu_custom_call" | custom-call | flops 268435456 | bytes 7340032 | tf_op jit(solution)/shard_map/make_key_value/pallas_call | solution.py:87
  5.6 10.1 %all-to-all-start = ((bf16[16,2,256,128]{3,2,1,0:T(8,128)(2,1)}), bf16[16,2,256,128]{3,2,1,0:T(8,128)(2,1)S(1)}, u32[]{:S(2)}, u32[]{:S(2)}) async-start(bf16[16,2,256,128]{3,2,1,0:T(8,128)(2,1)} %get-tuple-element.27), calls=%async_computation | async-start | bytes 4194304 | tf_op jit(solution)/shard_map/all_to_all | solution.py:49
  15.8 4.2 %make_query.1 = bf16[16,2,256,128]{3,2,1,0:T(8,128)(2,1)} custom-call(bf16[256,96]{1,0:T(8,128)(2,1)} %get-tuple-element.26.low_ref, bf16[256,6144]{1,0:T(8,128)(2,1)} %bitcast.17, bf16[3,32,2048]{2,1,0:T(8,128)(2,1)} %up_ref.7, bf16[256,2048]{1,0:T(8,128)(2,1)} %bitcast.19), custom_call_target="tpu_custom_call" | custom-call | flops 33554432 | bytes 4194304 | tf_op jit(solution)/shard_map/make_query/pallas_call | solution.py:120
  20.0 43.4 %all-to-all-done.kv0 = bf16[16,2,256,128]{3,2,1,0:T(8,128)(2,1)S(1)} async-done(((bf16[16,2,256,128]{3,2,1,0:T(8,128)(2,1)}), bf16[16,2,256,128]{3,2,1,0:T(8,128)(2,1)S(1)}, u32[]{:S(2)}, u32[]{:S(2)}) %all-to-all-start) | async-done | bytes 2097184 | tf_op jit(solution)/shard_map/all_to_all | solution.py:49
  63.4 5.1 %collective-permute-start.1 = (bf16[16,2,256,128]{3,2,1,0:T(8,128)(2,1)S(1)}, bf16[16,2,256,128]{3,2,1,0:T(8,128)(2,1)}, u32[]{:S(2)}, u32[]{:S(2)}) collective-permute-start(bf16[16,2,256,128]{3,2,1,0:T(8,128)(2,1)S(1)} %all-to-all-done.kv0), channel_id=1, source_target_pairs={{0,192},{4,196},{8,200},{12,204},{16,208},{20,212},{24,216},{28,22... | collective-permute-start | bytes 6291464 | tf_op jit(solution)/shard_map/ppermute | solution.py:510
  68.5 6.6 %all-to-all-start.1 = ((bf16[16,2,256,128]{3,2,1,0:T(8,128)(2,1)}), bf16[16,2,256,128]{3,2,1,0:T(8,128)(2,1)}, u32[]{:S(2)}, u32[]{:S(2)}) async-start(bf16[16,2,256,128]{3,2,1,0:T(8,128)(2,1)} %make_query.1), calls=%async_computation.1 | async-start | bytes 4194304 | tf_op jit(solution)/shard_map/all_to_all | solution.py:49
  75.2 1.2 collective-permute-start
  76.3 33.5 %collective-permute-done.1.kv2 = bf16[16,2,256,128]{3,2,1,0:T(8,128)(2,1)} collective-permute-done((bf16[16,2,256,128]{3,2,1,0:T(8,128)(2,1)S(1)}, bf16[16,2,256,128]{3,2,1,0:T(8,128)(2,1)}, u32[]{:S(2)}, u32[]{:S(2)}) %collective-permute-start.1) | collective-permute-done | bytes 2097184 | tf_op jit(solution)/shard_map/ppermute | solution.py:510
  109.8 3.3 %collective-permute-start.2 = (bf16[16,2,256,128]{3,2,1,0:T(8,128)(2,1)}, bf16[16,2,256,128]{3,2,1,0:T(8,128)(2,1)}, u32[]{:S(2)}, u32[]{:S(2)}) collective-permute-start(bf16[16,2,256,128]{3,2,1,0:T(8,128)(2,1)} %collective-permute-done.1.kv2), channel_id=1, source_target_pairs={{0,4},{4,0},{8,12},{12,8},{16,20},{20,16},{24,28},{28,24},{32,36},... | collective-permute-start | bytes 6291464 | tf_op jit(solution)/shard_map/ppermute | solution.py:53
  113.0 0.0 copy-done.6
  113.0 0.1 copy.12
  113.1 0.7 reshape_squeeze.3.ids_ref
  113.8 0.0 collective-permute-done.kv1
  113.8 8.8 %all-to-all-done.1.qg_ref = bf16[16,2,256,128]{3,2,1,0:T(8,128)(2,1)} async-done(((bf16[16,2,256,128]{3,2,1,0:T(8,128)(2,1)}), bf16[16,2,256,128]{3,2,1,0:T(8,128)(2,1)}, u32[]{:S(2)}, u32[]{:S(2)}) %all-to-all-start.1) | async-done | bytes 2097184 | tf_op jit(solution)/shard_map/all_to_all | solution.py:49
  122.7 0.0 collective-permute-done.2.kv3
  122.7 21.4 %attend.1 = (bf16[16,2,256,128]{3,2,1,0:T(8,128)(2,1)}, f32[16,2,256,128]{3,2,1,0:T(8,128)}, bf16[16,2,256,128]{3,2,1,0:T(8,128)(2,1)}, bf16[16,2,256,128]{3,2,1,0:T(8,128)(2,1)}, bf16[16,2,256,128]{3,2,1,0:T(8,128)(2,1)}) custom-call(s32[192]{0:T(256)} %reshape_squeeze.3.ids_ref, s32[1]{0:T(128)} %bitcast.me_ref, ...), custom_call_target="tpu_custom_call" | custom-call | flops 4831838208 | bytes 27262976 | tf_op jit(solution)/shard_map/attend/pallas_call | solution.py:277
  144.1 2.8 collective-permute-start.4
  146.9 5.3 %all-to-all-start.2 = ((bf16[16,2,256,128]{3,2,1,0:T(8,128)(2,1)}), bf16[16,2,256,128]{3,2,1,0:T(8,128)(2,1)}, u32[]{:S(2)}, u32[]{:S(2)}) async-start(bf16[16,2,256,128]{3,2,1,0:T(8,128)(2,1)} %get-tuple-element.34), calls=%async_computation.2 | async-start | bytes 4194304 | tf_op jit(solution)/shard_map/all_to_all | solution.py:49
  152.2 0.4 collective-permute-start.3
  152.6 0.0 collective-permute-done.4
  152.6 2.5 add_convert_fusion.1
  155.1 1.3 collective-permute-start.5
  156.4 0.3 collective-permute-done.3
  156.6 48.6 %collective-permute-done.5 = bf16[16,2,256,128]{3,2,1,0:T(8,128)(2,1)S(1)} collective-permute-done((bf16[16,2,256,128]{3,2,1,0:T(8,128)(2,1)S(1)}, bf16[16,2,256,128]{3,2,1,0:T(8,128)(2,1)S(1)}, u32[]{:S(2)}, u32[]{:S(2)}) %collective-permute-start.5) | collective-permute-done | bytes 2097184 | tf_op jit(solution)/shard_map/ppermute | solution.py:520
  205.2 2.2 add_convert_fusion
  207.4 0.0 all-to-all-done.2.home_ref
  207.4 7.2 %all-to-all-start.3 = ((bf16[16,2,256,128]{3,2,1,0:T(8,128)(2,1)}), bf16[16,2,256,128]{3,2,1,0:T(8,128)(2,1)}, u32[]{:S(2)}, u32[]{:S(2)}) async-start(bf16[16,2,256,128]{3,2,1,0:T(8,128)(2,1)} %add_convert_fusion), calls=%async_computation.3 | async-start | bytes 4194304 | tf_op jit(solution)/shard_map/all_to_all | solution.py:49
  214.6 0.1 copy.13
  214.8 4.8 %query_grads.1 = (bf16[256,2048]{1,0:T(8,128)(2,1)}, bf16[256,6144]{1,0:T(8,128)(2,1)}, f32[32,24,128]{2,1,0:T(8,128)S(1)}, bf16[32,24,128]{2,1,0:T(8,128)(2,1)S(1)}) custom-call(s32[1]{0:T(128)} %bitcast.me_ref, bf16[16,2,256,128]{3,2,1,0:T(8,128)(2,1)} %all-to-all-done.2.home_ref, bf16[256,4096]{1,0:T(8,128)(2,1)S(1)} %bitcast.11, ...), custom_call_target="tpu_custom_call" | custom-call | flops 134217728 | bytes 8388608 | tf_op jit(solution)/shard_map/query_grads/pallas_call | solution.py:387
  219.5 1.1 collective-permute-start.6
  220.6 1.1 collective-permute-done.6
  221.7 0.1 add_convert_fusion.3
  221.7 40.4 %all-to-all-done.3.home_ref = bf16[16,2,256,128]{3,2,1,0:T(8,128)(2,1)} async-done(((bf16[16,2,256,128]{3,2,1,0:T(8,128)(2,1)}), bf16[16,2,256,128]{3,2,1,0:T(8,128)(2,1)}, u32[]{:S(2)}, u32[]{:S(2)}) %all-to-all-start.3) | async-done | bytes 2097184 | tf_op jit(solution)/shard_map/all_to_all | solution.py:49
  262.1 5.0 %key_value_grads.1 = (bf16[256,6144]{1,0:T(8,128)(2,1)}, f32[32,48,128]{2,1,0:T(8,128)S(1)}, bf16[32,48,128]{2,1,0:T(8,128)(2,1)S(1)}) custom-call(s32[1]{0:T(128)} %bitcast.me_ref, bf16[256,6144]{1,0:T(8,128)(2,1)} %get-tuple-element.37._, bf16[16,2,256,128]{3,2,1,0:T(8,128)(2,1)} %all-to-all-done.3.home_ref, ...), custom_call_target="tpu_custom_call", output_to_operand_aliasing={{0}: (1, {})} | custom-call | flops 268435456 | bytes 8388608 | tf_op jit(solution)/shard_map/key_value_grads/pallas_call | solution.py:416
  267.1 2.8 collective-permute-start.7
  270.0 1.3 collective-permute-done.7
  271.3 0.1 add_convert_fusion.2
  271.4 20.7 %all_to_all.25 = bf16[32,72,128]{2,1,0:T(8,128)(2,1)S(1)} all-to-all(bf16[32,72,128]{2,1,0:T(8,128)(2,1)S(1)} %pad_maximum_fusion), channel_id=1, replica_groups={{0,8,16,24,32,40,48,56,64,72,80,88,96,104,112,120,128,136,144,152,160,1..., dimensions={0} | all-to-all | bytes 1179648 | tf_op jit(solution)/shard_map/all_to_all | solution.py:530
  292.2 0.1 convert_reduce_fusion
  292.2 2.5 collective-permute-start.10
  294.8 0.5 collective-permute-start.9
  295.3 0.6 collective-permute-start.8
  295.9 0.0 collective-permute-done.10
  295.9 3.2 %collective-permute-done.9 = f32[72,128]{1,0:T(8,128)S(1)} collective-permute-done((f32[72,128]{1,0:T(8,128)S(1)}, f32[72,128]{1,0:T(8,128)S(1)}, u32[]{:S(2)}, u32[]{:S(2)}) %collective-permute-start.9) | collective-permute-done | bytes 36896 | tf_op jit(solution)/shard_map/ppermute | solution.py:533
  299.1 0.4 collective-permute-done.8
  299.5 5.0 %collective-permute-start.11 = (f32[72,128]{1,0:T(8,128)S(1)}, f32[72,128]{1,0:T(8,128)S(1)}, u32[]{:S(2)}, u32[]{:S(2)}) collective-permute-start(f32[72,128]{1,0:T(8,128)S(1)} %add_add_fusion.mine_ref), channel_id=1, source_target_pairs={{0,4},{4,0},{8,12},{12,8},{16,20},{20,16},{24,28},{28,24},{32,36},... | collective-permute-start | bytes 110600 | tf_op jit(solution)/shard_map/ppermute | solution.py:53
  304.6 0.9 collective-permute-done.11.other_ref
  305.4 0.9 finish.1
  (15 shorter events, 0.1 us)
Async XLA Ops:
  5.6 57.8 %all-to-all-start = ((bf16[16,2,256,128]{3,2,1,0:T(8,128)(2,1)}), bf16[16,2,256,128]{3,2,1,0:T(8,128)(2,1)S(1)}, u32[]{:S(2)}, u32[]{:S(2)}) async-start(bf16[16,2,256,128]{3,2,1,0:T(8,128)(2,1)} %get-tuple-element.27), calls=%async_computation | async-start | bytes 4194304 | tf_op jit(solution)/shard_map/all_to_all | solution.py:49
  20.0 93.1 %copy-start.6 = (s32[1,64,3]{1,0,2:T(1,128)S(1)}, s32[1,64,3]{1,0,2:T(1,128)}, u32[]{:S(2)}) copy-start(s32[1,64,3]{1,0,2:T(1,128)} %param.10) | copy-start | bytes 2308
  63.4 49.6 %copy-start.4 = (bf16[16,2,256,128]{3,2,1,0:T(8,128)(2,1)}, bf16[16,2,256,128]{3,2,1,0:T(8,128)(2,1)S(1)}, u32[]{:S(2)}) copy-start(bf16[16,2,256,128]{3,2,1,0:T(8,128)(2,1)S(1)} %all-to-all-done.kv0) | copy-start | bytes 6291460
  63.4 46.4 %collective-permute-start.1 = (bf16[16,2,256,128]{3,2,1,0:T(8,128)(2,1)S(1)}, bf16[16,2,256,128]{3,2,1,0:T(8,128)(2,1)}, u32[]{:S(2)}, u32[]{:S(2)}) collective-permute-start(bf16[16,2,256,128]{3,2,1,0:T(8,128)(2,1)S(1)} %all-to-all-done.kv0), channel_id=1, source_target_pairs={{0,192},{4,196},{8,200},{12,204},{16,208},{20,212},{24,216},{28,22... | collective-permute-start | bytes 6291464 | tf_op jit(solution)/shard_map/ppermute | solution.py:510
  68.5 54.1 %all-to-all-start.1 = ((bf16[16,2,256,128]{3,2,1,0:T(8,128)(2,1)}), bf16[16,2,256,128]{3,2,1,0:T(8,128)(2,1)}, u32[]{:S(2)}, u32[]{:S(2)}) async-start(bf16[16,2,256,128]{3,2,1,0:T(8,128)(2,1)} %make_query.1), calls=%async_computation.1 | async-start | bytes 4194304 | tf_op jit(solution)/shard_map/all_to_all | solution.py:49
  75.2 38.7 %collective-permute-start = (bf16[16,2,256,128]{3,2,1,0:T(8,128)(2,1)S(1)}, bf16[16,2,256,128]{3,2,1,0:T(8,128)(2,1)}, u32[]{:S(2)}, u32[]{:S(2)}) collective-permute-start(bf16[16,2,256,128]{3,2,1,0:T(8,128)(2,1)S(1)} %all-to-all-done.kv0), channel_id=1, source_target_pairs={{0,4},{4,0},{8,12},{12,8},{16,20},{20,16},{24,28},{28,24},{32,36},... | collective-permute-start | bytes 6291464 | tf_op jit(solution)/shard_map/ppermute | solution.py:53
  109.8 12.9 %collective-permute-start.2 = (bf16[16,2,256,128]{3,2,1,0:T(8,128)(2,1)}, bf16[16,2,256,128]{3,2,1,0:T(8,128)(2,1)}, u32[]{:S(2)}, u32[]{:S(2)}) collective-permute-start(bf16[16,2,256,128]{3,2,1,0:T(8,128)(2,1)} %collective-permute-done.1.kv2), channel_id=1, source_target_pairs={{0,4},{4,0},{8,12},{12,8},{16,20},{20,16},{24,28},{28,24},{32,36},... | collective-permute-start | bytes 6291464 | tf_op jit(solution)/shard_map/ppermute | solution.py:53
  144.1 8.5 %collective-permute-start.4 = (bf16[16,2,256,128]{3,2,1,0:T(8,128)(2,1)}, bf16[16,2,256,128]{3,2,1,0:T(8,128)(2,1)}, u32[]{:S(2)}, u32[]{:S(2)}) collective-permute-start(bf16[16,2,256,128]{3,2,1,0:T(8,128)(2,1)} %get-tuple-element.33), channel_id=1, source_target_pairs={{0,4},{4,0},{8,12},{12,8},{16,20},{20,16},{24,28},{28,24},{32,36},... | collective-permute-start | bytes 6291464 | tf_op jit(solution)/shard_map/ppermute | solution.py:53
  146.9 5.7 %copy-start.3 = (bf16[16,2,256,128]{3,2,1,0:T(8,128)(2,1)S(1)}, bf16[16,2,256,128]{3,2,1,0:T(8,128)(2,1)}, u32[]{:S(2)}) copy-start(bf16[16,2,256,128]{3,2,1,0:T(8,128)(2,1)} %get-tuple-element.32) | copy-start | bytes 6291460
  146.9 60.5 %all-to-all-start.2 = ((bf16[16,2,256,128]{3,2,1,0:T(8,128)(2,1)}), bf16[16,2,256,128]{3,2,1,0:T(8,128)(2,1)}, u32[]{:S(2)}, u32[]{:S(2)}) async-start(bf16[16,2,256,128]{3,2,1,0:T(8,128)(2,1)} %get-tuple-element.34), calls=%async_computation.2 | async-start | bytes 4194304 | tf_op jit(solution)/shard_map/all_to_all | solution.py:49
  152.2 4.5 %collective-permute-start.3 = (bf16[16,2,256,128]{3,2,1,0:T(8,128)(2,1)}, bf16[16,2,256,128]{3,2,1,0:T(8,128)(2,1)S(1)}, u32[]{:S(2)}, u32[]{:S(2)}) collective-permute-start(bf16[16,2,256,128]{3,2,1,0:T(8,128)(2,1)} %get-tuple-element.31), channel_id=1, source_target_pairs={{0,4},{4,0},{8,12},{12,8},{16,20},{20,16},{24,28},{28,24},{32,36},... | collective-permute-start | bytes 6291464 | tf_op jit(solution)/shard_map/ppermute | solution.py:53
  152.6 52.6 %copy-start.2 = (f32[16,2,256,128]{3,2,1,0:T(8,128)S(1)}, f32[16,2,256,128]{3,2,1,0:T(8,128)}, u32[]{:S(2)}) copy-start(f32[16,2,256,128]{3,2,1,0:T(8,128)} %get-tuple-element.30) | copy-start | bytes 12582916
  155.1 50.1 %collective-permute-start.5 = (bf16[16,2,256,128]{3,2,1,0:T(8,128)(2,1)S(1)}, bf16[16,2,256,128]{3,2,1,0:T(8,128)(2,1)S(1)}, u32[]{:S(2)}, u32[]{:S(2)}) collective-permute-start(bf16[16,2,256,128]{3,2,1,0:T(8,128)(2,1)S(1)} %add_convert_fusion.1), channel_id=1, source_target_pairs={{192,0},{196,4},{200,8},{204,12},{208,16},{212,20},{216,24},{220,2... | collective-permute-start | bytes 6291464 | tf_op jit(solution)/shard_map/ppermute | solution.py:520
  207.4 7.2 %copy-start.5 = (bf16[256,96]{1,0:T(8,128)(2,1)S(1)}, bf16[256,96]{1,0:T(8,128)(2,1)}, u32[]{:S(2)}) copy-start(bf16[256,96]{1,0:T(8,128)(2,1)} %get-tuple-element.26.low_ref) | copy-start | bytes 147460
  207.4 7.3 %copy-start = (bf16[1,256,4096]{2,1,0:T(8,128)(2,1)S(1)}, bf16[1,256,4096]{2,1,0:T(8,128)(2,1)}, u32[]{:S(2)}) copy-start(bf16[1,256,4096]{2,1,0:T(8,128)(2,1)} %param.6) | copy-start | bytes 6291460
  207.4 7.3 %copy-start.1 = (bf16[3,32,2048]{2,1,0:T(8,128)(2,1)S(1)}, bf16[3,32,2048]{2,1,0:T(8,128)(2,1)}, u32[]{:S(2)}) copy-start(bf16[3,32,2048]{2,1,0:T(8,128)(2,1)} %up_ref.7) | copy-start | bytes 1179652
  207.4 54.7 %all-to-all-start.3 = ((bf16[16,2,256,128]{3,2,1,0:T(8,128)(2,1)}), bf16[16,2,256,128]{3,2,1,0:T(8,128)(2,1)}, u32[]{:S(2)}, u32[]{:S(2)}) async-start(bf16[16,2,256,128]{3,2,1,0:T(8,128)(2,1)} %add_convert_fusion), calls=%async_computation.3 | async-start | bytes 4194304 | tf_op jit(solution)/shard_map/all_to_all | solution.py:49
  219.5 2.1 collective-permute-start.6
  267.1 4.2 %collective-permute-start.7 = (bf16[32,48,128]{2,1,0:T(8,128)(2,1)S(1)}, bf16[32,48,128]{2,1,0:T(8,128)(2,1)S(1)}, u32[]{:S(2)}, u32[]{:S(2)}) collective-permute-start(bf16[32,48,128]{2,1,0:T(8,128)(2,1)S(1)} %get-tuple-element.44), channel_id=1, source_target_pairs={{0,4},{4,0},{8,12},{12,8},{16,20},{20,16},{24,28},{28,24},{32,36},... | collective-permute-start | bytes 1179656 | tf_op jit(solution)/shard_map/ppermute | solution.py:53
  292.2 3.7 %collective-permute-start.10 = (f32[72,128]{1,0:T(8,128)S(1)}, f32[72,128]{1,0:T(8,128)S(1)}, u32[]{:S(2)}, u32[]{:S(2)}) collective-permute-start(f32[72,128]{1,0:T(8,128)S(1)} %convert_reduce_fusion), channel_id=1, source_target_pairs={{0,3},{1,0},{2,1},{3,2},{4,7},{5,4},{6,5},{7,6},{8,11},{9,8},{10,9... | collective-permute-start | bytes 110600 | tf_op jit(solution)/shard_map/ppermute | solution.py:533
  294.8 4.3 %collective-permute-start.9 = (f32[72,128]{1,0:T(8,128)S(1)}, f32[72,128]{1,0:T(8,128)S(1)}, u32[]{:S(2)}, u32[]{:S(2)}) collective-permute-start(f32[72,128]{1,0:T(8,128)S(1)} %convert_reduce_fusion), channel_id=1, source_target_pairs={{0,2},{1,3},{2,0},{3,1},{4,6},{5,7},{6,4},{7,5},{8,10},{9,11},{10,... | collective-permute-start | bytes 110600 | tf_op jit(solution)/shard_map/ppermute | solution.py:533
  295.3 4.2 %collective-permute-start.8 = (f32[72,128]{1,0:T(8,128)S(1)}, f32[72,128]{1,0:T(8,128)S(1)}, u32[]{:S(2)}, u32[]{:S(2)}) collective-permute-start(f32[72,128]{1,0:T(8,128)S(1)} %convert_reduce_fusion), channel_id=1, source_target_pairs={{0,1},{1,2},{2,3},{3,0},{4,5},{5,6},{6,7},{7,4},{8,9},{9,10},{10,1... | collective-permute-start | bytes 110600 | tf_op jit(solution)/shard_map/ppermute | solution.py:533
  299.5 5.9 %collective-permute-start.11 = (f32[72,128]{1,0:T(8,128)S(1)}, f32[72,128]{1,0:T(8,128)S(1)}, u32[]{:S(2)}, u32[]{:S(2)}) collective-permute-start(f32[72,128]{1,0:T(8,128)S(1)} %add_add_fusion.mine_ref), channel_id=1, source_target_pairs={{0,4},{4,0},{8,12},{12,8},{16,20},{20,16},{24,28},{28,24},{32,36},... | collective-permute-start | bytes 110600 | tf_op jit(solution)/shard_map/ppermute | solution.py:53

commit v4 on v3

--- a/solution.py
+++ b/solution.py
@@ -42,7 +42,6 @@
 CORE_PAIRS = [(i, i ^ 1) for i in range(64)]
 TO_LATER = [(place(y, z, c), place(3 - y, z, c)) for y, z, c in EVERY if y < 2]
 TO_EARLIER = [(b, a) for a, b in TO_LATER]
-TILE_GROUPS = [[place(y, z, core) for y in range(4) for z in range(8)] for core in range(2)]
 
 
 def to_heads(x):
@@ -324,6 +323,12 @@
                 ref[slot, 0:32, :] = down_term[member * R : (member + 1) * R, side * 128 : (side + 1) * 128]
 
 
+def tile_slot(me, t):
+    half = t >> 4
+    row = (t >> 3) if half == 0 else 3 - (t >> 3)
+    return ((me >> 5) ^ half) * 16 + row * 8 + (t & 7)
+
+
 def query_grads_kernel(me_ref, home_ref, tok_ref, low_ref, up_ref, attn_ref, gp_ref, keep_ref, send_ref, terms):
     me = me_ref[0]
     for h in range(HEADS):
@@ -336,7 +341,7 @@
         [low_ref[...]],
         [lambda pair: up_ref[0, :, pair * 256 : (pair + 1) * 256]],
         tok_ref,
-        lambda member, t: (terms, t),
+        lambda member, t: (terms, tile_slot(me, t)),
     )
 
     @pl.when((me & 1) == 0)
@@ -366,7 +371,7 @@
             lambda pair: up_ref[2, :, pair * 256 : (pair + 1) * 256],
         ],
         tok_ref,
-        lambda member, t: ((terms_k, terms_v)[member], t),
+        lambda member, t: ((terms_k, terms_v)[member], tile_slot(me_ref[0], t)),
     )
     core = me_ref[0] & 1
 
@@ -513,8 +518,10 @@
         ids, me, query, (key_value, swap(key_value), far, swap(far))
     )
 
-    def both_cores(keep, send):
-        return (keep + swap(send).astype(jnp.float32)).astype(jnp.bfloat16)
+    def over_cores_and_halves(keep, send):
+        both = keep + swap(send).astype(jnp.float32)
+        sent = lax.ppermute(both[16:].astype(jnp.bfloat16), "ctx", TO_LATER + TO_EARLIER)
+        return (both[:16] + sent.astype(jnp.float32)).astype(jnp.bfloat16)
 
     far_sum = far_part.astype(jnp.float32) + swap(farcore_part).astype(jnp.float32)
     returned = lax.ppermute(far_sum.astype(jnp.bfloat16), "ctx", TO_EARLIER)
@@ -523,11 +530,10 @@
     total, out_home = after(total.astype(jnp.bfloat16), out_home)
     total_home = to_heads(total)
     attn_rows, grad_proj, keep, send = query_grads(me, out_home, tokens, low_t, up_projection)
-    pieces_q = both_cores(keep, send)
+    pieces_q = over_cores_and_halves(keep, send)
     total_home, pieces_q = after(total_home, pieces_q)
     grad_proj, keep, send = key_value_grads(me, grad_proj, total_home, tokens, low_t, up_projection)
-    pieces = jnp.concatenate([both_cores(keep, send), pieces_q], axis=1)
-    pieces = lax.all_to_all(pieces, "ctx", 0, 0, axis_index_groups=TILE_GROUPS, tiled=True)
+    pieces = to_heads(jnp.concatenate([over_cores_and_halves(keep, send), pieces_q], axis=1))
     mine = jnp.sum(pieces.astype(jnp.float32), axis=0)
     others = [
         lax.ppermute(mine, "dp", [(j, (j + step) % 4) for j in range(4)]) for step in (1, 2, 3)

time: 307 us -> 306 us (level)
  blocking collectives: 20.7 us -> 12.7 us
  waiting for transfers between devices: 182 us -> 189 us
    ppermute x0 -> x2, waiting for transfers between devices: none -> 12.6 us  [over_cores_and_halves(): lax.ppermute(both[16:].astype(jnp.bfloat16), 'ctx', TO_LATER + TO_EARLIER)]
    all_to_all x1, blocking collectives: 20.7 us -> 12.7 us  [to_heads(): lax.all_to_all(x, 'ctx', 0, 0, axis_index_groups=HEAD_GROUPS, tiled=True)]
    all_to_all x4, waiting for transfers between devices: 92.7 us -> 87 us  [to_heads(): lax.all_to_all(x, 'ctx', 0, 0, axis_index_groups=HEAD_GROUPS, tiled=True)]
  transfers between devices with their start and end apart: 16 -> 18, of which waited for: 11 -> 13; matrix products, arithmetic and copies ran while one was open for 2% -> 2% of each run, Pallas kernels for 3% -> 3%
where the time goes in v4:
time: 306 us; the launch traced here: 305 us
  waiting for transfers between devices  189 us (62%)
  starting transfers between devices  55.7 us (18%)
  Pallas kernels  41.3 us (13%)
  blocking collectives  12.7 us (4%)
  other arithmetic  4.94 us (2%)
    all_to_all x4, waiting for transfers between devices, to_heads(): lax.all_to_all(x, 'ctx', 0, 0, axis_index_groups=HEAD_GROUPS, tiled=True)  87 us
    ppermute x1, waiting for transfers between devices, shards(): returned = lax.ppermute(far_sum.astype(jnp.bfloat16), 'ctx', TO_EARLIER)  48.6 us
    ppermute x1, waiting for transfers between devices, shards(): far = lax.ppermute(key_value, 'ctx', TO_LATER)  33.4 us
    all_to_all x4, starting transfers between devices, to_heads(): lax.all_to_all(x, 'ctx', 0, 0, axis_index_groups=HEAD_GROUPS, tiled=True)  29.2 us
    pallas_call x1, Pallas kernels, attend(): pl.pallas_call(attend_kernel, grid_spec=pltpu.PrefetchScalarGridSpec(num_...  21.4 us
    ppermute x7, starting transfers between devices, swap(): return lax.ppermute(x, 'ctx', CORE_PAIRS)  16.1 us
    all_to_all x1, blocking collectives, to_heads(): lax.all_to_all(x, 'ctx', 0, 0, axis_index_groups=HEAD_GROUPS, tiled=True)  12.7 us
    ppermute x2, waiting for transfers between devices, over_cores_and_halves(): lax.ppermute(both[16:].astype(jnp.bfloat16), 'ctx', TO_LATER + TO_EARLIER)  12.6 us
  transfers between devices with their start and end apart: 18, of which 13 were waited for; matrix products, arithmetic and copies ran while one was open for 2% of the time, Pallas kernels for 3%

profile of v4, /device:TPU:1, one launch (start us, length us, event | category | flops | bytes accessed | tf_op | source)
XLA Modules:
  0.0 305.2 jit_solution(15318700669247163334)
XLA Ops:
  0.6 5.0 %make_key_value.1 = (bf16[16,2,256,128]{3,2,1,0:T(8,128)(2,1)}, bf16[256,96]{1,0:T(8,128)(2,1)}) custom-call(bf16[256,4096]{1,0:T(8,128)(2,1)} %bitcast.10, bf16[3,32,4096]{2,1,0:T(8,128)(2,1)} %bitcast.20, bf16[256,6144]{1,0:T(8,128)(2,1)} %bitcast.15, bf16[256,6144]{1,0:T(8,128)(2,1)} %bitcast.16, bf16[3,32,2048]{2,1,0:T(8,128)(2,1)} %up_ref.7), custom_call_target="tpu_custom_call" | custom-call | flops 268435456 | bytes 7340032 | tf_op jit(solution)/shard_map/make_key_value/pallas_call | solution.py:86
  5.6 10.1 %all-to-all-start = ((bf16[16,2,256,128]{3,2,1,0:T(8,128)(2,1)}), bf16[16,2,256,128]{3,2,1,0:T(8,128)(2,1)S(1)}, u32[]{:S(2)}, u32[]{:S(2)}) async-start(bf16[16,2,256,128]{3,2,1,0:T(8,128)(2,1)} %get-tuple-element.27), calls=%async_computation | async-start | bytes 4194304 | tf_op jit(solution)/shard_map/all_to_all | solution.py:48
  15.8 4.2 %make_query.1 = bf16[16,2,256,128]{3,2,1,0:T(8,128)(2,1)} custom-call(bf16[256,96]{1,0:T(8,128)(2,1)} %get-tuple-element.26.low_ref, bf16[256,6144]{1,0:T(8,128)(2,1)} %bitcast.17, bf16[3,32,2048]{2,1,0:T(8,128)(2,1)} %up_ref.7, bf16[256,2048]{1,0:T(8,128)(2,1)} %bitcast.19), custom_call_target="tpu_custom_call" | custom-call | flops 33554432 | bytes 4194304 | tf_op jit(solution)/shard_map/make_query/pallas_call | solution.py:119
  20.0 43.4 %all-to-all-done.kv0 = bf16[16,2,256,128]{3,2,1,0:T(8,128)(2,1)S(1)} async-done(((bf16[16,2,256,128]{3,2,1,0:T(8,128)(2,1)}), bf16[16,2,256,128]{3,2,1,0:T(8,128)(2,1)S(1)}, u32[]{:S(2)}, u32[]{:S(2)}) %all-to-all-start) | async-done | bytes 2097184 | tf_op jit(solution)/shard_map/all_to_all | solution.py:48
  63.4 5.1 %collective-permute-start.1 = (bf16[16,2,256,128]{3,2,1,0:T(8,128)(2,1)S(1)}, bf16[16,2,256,128]{3,2,1,0:T(8,128)(2,1)}, u32[]{:S(2)}, u32[]{:S(2)}) collective-permute-start(bf16[16,2,256,128]{3,2,1,0:T(8,128)(2,1)S(1)} %all-to-all-done.kv0), channel_id=1, source_target_pairs={{0,192},{4,196},{8,200},{12,204},{16,208},{20,212},{24,216},{28,22... | collective-permute-start | bytes 6291464 | tf_op jit(solution)/shard_map/ppermute | solution.py:515
  68.5 6.6 %all-to-all-start.1 = ((bf16[16,2,256,128]{3,2,1,0:T(8,128)(2,1)}), bf16[16,2,256,128]{3,2,1,0:T(8,128)(2,1)}, u32[]{:S(2)}, u32[]{:S(2)}) async-start(bf16[16,2,256,128]{3,2,1,0:T(8,128)(2,1)} %make_query.1), calls=%async_computation.1 | async-start | bytes 4194304 | tf_op jit(solution)/shard_map/all_to_all | solution.py:48
  75.2 1.2 collective-permute-start
  76.3 33.4 %collective-permute-done.1.kv2 = bf16[16,2,256,128]{3,2,1,0:T(8,128)(2,1)} collective-permute-done((bf16[16,2,256,128]{3,2,1,0:T(8,128)(2,1)S(1)}, bf16[16,2,256,128]{3,2,1,0:T(8,128)(2,1)}, u32[]{:S(2)}, u32[]{:S(2)}) %collective-permute-start.1) | collective-permute-done | bytes 2097184 | tf_op jit(solution)/shard_map/ppermute | solution.py:515
  109.8 3.3 %collective-permute-start.2 = (bf16[16,2,256,128]{3,2,1,0:T(8,128)(2,1)}, bf16[16,2,256,128]{3,2,1,0:T(8,128)(2,1)}, u32[]{:S(2)}, u32[]{:S(2)}) collective-permute-start(bf16[16,2,256,128]{3,2,1,0:T(8,128)(2,1)} %collective-permute-done.1.kv2), channel_id=1, source_target_pairs={{0,4},{4,0},{8,12},{12,8},{16,20},{20,16},{24,28},{28,24},{32,36},... | collective-permute-start | bytes 6291464 | tf_op jit(solution)/shard_map/ppermute | solution.py:52
  113.0 0.1 copy.12
  113.1 0.7 reshape_squeeze.3.ids_ref
  113.8 0.0 collective-permute-done.kv1
  113.8 8.9 %all-to-all-done.1.qg_ref = bf16[16,2,256,128]{3,2,1,0:T(8,128)(2,1)} async-done(((bf16[16,2,256,128]{3,2,1,0:T(8,128)(2,1)}), bf16[16,2,256,128]{3,2,1,0:T(8,128)(2,1)}, u32[]{:S(2)}, u32[]{:S(2)}) %all-to-all-start.1) | async-done | bytes 2097184 | tf_op jit(solution)/shard_map/all_to_all | solution.py:48
  122.7 21.4 %attend.1 = (bf16[16,2,256,128]{3,2,1,0:T(8,128)(2,1)}, f32[16,2,256,128]{3,2,1,0:T(8,128)}, bf16[16,2,256,128]{3,2,1,0:T(8,128)(2,1)}, bf16[16,2,256,128]{3,2,1,0:T(8,128)(2,1)}, bf16[16,2,256,128]{3,2,1,0:T(8,128)(2,1)}) custom-call(s32[192]{0:T(256)} %reshape_squeeze.3.ids_ref, s32[1]{0:T(128)} %bitcast.me_ref, ...), custom_call_target="tpu_custom_call" | custom-call | flops 4831838208 | bytes 27262976 | tf_op jit(solution)/shard_map/attend/pallas_call | solution.py:276
  144.1 2.8 collective-permute-start.4
  146.9 5.3 %all-to-all-start.2 = ((bf16[16,2,256,128]{3,2,1,0:T(8,128)(2,1)}), bf16[16,2,256,128]{3,2,1,0:T(8,128)(2,1)}, u32[]{:S(2)}, u32[]{:S(2)}) async-start(bf16[16,2,256,128]{3,2,1,0:T(8,128)(2,1)} %get-tuple-element.34), calls=%async_computation.2 | async-start | bytes 4194304 | tf_op jit(solution)/shard_map/all_to_all | solution.py:48
  152.2 0.4 collective-permute-start.3
  152.6 0.0 collective-permute-done.4
  152.6 2.5 add_convert_fusion.1
  155.1 1.3 collective-permute-start.5
  156.4 0.3 collective-permute-done.3
  156.6 48.6 %collective-permute-done.5 = bf16[16,2,256,128]{3,2,1,0:T(8,128)(2,1)S(1)} collective-permute-done((bf16[16,2,256,128]{3,2,1,0:T(8,128)(2,1)S(1)}, bf16[16,2,256,128]{3,2,1,0:T(8,128)(2,1)S(1)}, u32[]{:S(2)}, u32[]{:S(2)}) %collective-permute-start.5) | collective-permute-done | bytes 2097184 | tf_op jit(solution)/shard_map/ppermute | solution.py:527
  205.2 2.2 add_convert_fusion
  207.4 0.0 all-to-all-done.2.home_ref
  207.4 7.2 %all-to-all-start.3 = ((bf16[16,2,256,128]{3,2,1,0:T(8,128)(2,1)}), bf16[16,2,256,128]{3,2,1,0:T(8,128)(2,1)}, u32[]{:S(2)}, u32[]{:S(2)}) async-start(bf16[16,2,256,128]{3,2,1,0:T(8,128)(2,1)} %add_convert_fusion), calls=%async_computation.3 | async-start | bytes 4194304 | tf_op jit(solution)/shard_map/all_to_all | solution.py:48
  214.6 0.1 copy.13
  214.8 4.8 %query_grads.1 = (bf16[256,2048]{1,0:T(8,128)(2,1)}, bf16[256,6144]{1,0:T(8,128)(2,1)}, f32[32,24,128]{2,1,0:T(8,128)S(1)}, bf16[32,24,128]{2,1,0:T(8,128)(2,1)S(1)}) custom-call(s32[1]{0:T(128)} %bitcast.me_ref, bf16[16,2,256,128]{3,2,1,0:T(8,128)(2,1)} %all-to-all-done.2.home_ref, bf16[256,4096]{1,0:T(8,128)(2,1)S(1)} %bitcast.11, ...), custom_call_target="tpu_custom_call" | custom-call | flops 134217728 | bytes 8388608 | tf_op jit(solution)/shard_map/query_grads/pallas_call | solution.py:392
  219.6 1.1 collective-permute-start.6
  220.7 1.1 collective-permute-done.6
  221.8 0.3 collective-permute-start.7
  222.1 5.3 %collective-permute-done.7 = bf16[16,24,128]{2,1,0:T(8,128)(2,1)S(1)} collective-permute-done((bf16[16,24,128]{2,1,0:T(8,128)(2,1)S(1)}, bf16[16,24,128]{2,1,0:T(8,128)(2,1)S(1)}, u32[]{:S(2)}, u32[]{:S(2)}) %collective-permute-start.7) | collective-permute-done | bytes 98336 | tf_op jit(solution)/shard_map/ppermute | solution.py:523
  227.4 34.7 %all-to-all-done.3.home_ref = bf16[16,2,256,128]{3,2,1,0:T(8,128)(2,1)} async-done(((bf16[16,2,256,128]{3,2,1,0:T(8,128)(2,1)}), bf16[16,2,256,128]{3,2,1,0:T(8,128)(2,1)}, u32[]{:S(2)}, u32[]{:S(2)}) %all-to-all-start.3) | async-done | bytes 2097184 | tf_op jit(solution)/shard_map/all_to_all | solution.py:48
  262.1 5.0 %key_value_grads.1 = (bf16[256,6144]{1,0:T(8,128)(2,1)}, f32[32,48,128]{2,1,0:T(8,128)S(1)}, bf16[32,48,128]{2,1,0:T(8,128)(2,1)S(1)}) custom-call(s32[1]{0:T(128)} %bitcast.me_ref, bf16[256,6144]{1,0:T(8,128)(2,1)} %get-tuple-element.37._, bf16[16,2,256,128]{3,2,1,0:T(8,128)(2,1)} %all-to-all-done.3.home_ref, ...), custom_call_target="tpu_custom_call", output_to_operand_aliasing={{0}: (1, {})} | custom-call | flops 268435456 | bytes 8388608 | tf_op jit(solution)/shard_map/key_value_grads/pallas_call | solution.py:421
  267.1 2.8 collective-permute-start.8
  270.0 1.3 collective-permute-done.8
  271.3 0.1 convert_add_fusion
  271.4 0.1 collective-permute-start.9
  271.5 7.3 %collective-permute-done.9 = bf16[16,48,128]{2,1,0:T(8,128)(2,1)S(1)} collective-permute-done((bf16[16,48,128]{2,1,0:T(8,128)(2,1)S(1)}, bf16[16,48,128]{2,1,0:T(8,128)(2,1)S(1)}, u32[]{:S(2)}, u32[]{:S(2)}) %collective-permute-start.9) | collective-permute-done | bytes 196640 | tf_op jit(solution)/shard_map/ppermute | solution.py:523
  278.8 0.1 fusion
  278.9 12.7 %all_to_all.25 = bf16[16,72,128]{2,1,0:T(8,128)(2,1)S(1)} all-to-all(bf16[16,72,128]{2,1,0:T(8,128)(2,1)S(1)} %pad_maximum_fusion), channel_id=1, replica_groups={{0,8,16,24,32,40,48,56,64,72,80,88,96,104,112,120},{4,12,20,28,36,44,52..., dimensions={0} | all-to-all | bytes 589824 | tf_op jit(solution)/shard_map/all_to_all | solution.py:48
  291.7 2.5 collective-permute-start.12
  294.2 0.5 collective-permute-start.11
  294.7 0.6 collective-permute-start.10
  295.3 3.2 %collective-permute-done.11 = f32[72,128]{1,0:T(8,128)S(1)} collective-permute-done((f32[72,128]{1,0:T(8,128)S(1)}, f32[72,128]{1,0:T(8,128)S(1)}, u32[]{:S(2)}, u32[]{:S(2)}) %collective-permute-start.11) | collective-permute-done | bytes 36896 | tf_op jit(solution)/shard_map/ppermute | solution.py:539
  298.5 0.4 collective-permute-done.10
  298.9 4.6 %collective-permute-start.13 = (f32[72,128]{1,0:T(8,128)S(1)}, f32[72,128]{1,0:T(8,128)S(1)}, u32[]{:S(2)}, u32[]{:S(2)}) collective-permute-start(f32[72,128]{1,0:T(8,128)S(1)} %add_add_fusion.mine_ref), channel_id=1, source_target_pairs={{0,4},{4,0},{8,12},{12,8},{16,20},{20,16},{24,28},{28,24},{32,36},... | collective-permute-start | bytes 110600 | tf_op jit(solution)/shard_map/ppermute | solution.py:52
  303.5 0.9 collective-permute-done.13.other_ref
  304.3 0.9 finish.1
  (23 shorter events, 0.2 us)
Async XLA Ops:
  5.6 57.8 %all-to-all-start = ((bf16[16,2,256,128]{3,2,1,0:T(8,128)(2,1)}), bf16[16,2,256,128]{3,2,1,0:T(8,128)(2,1)S(1)}, u32[]{:S(2)}, u32[]{:S(2)}) async-start(bf16[16,2,256,128]{3,2,1,0:T(8,128)(2,1)} %get-tuple-element.27), calls=%async_computation | async-start | bytes 4194304 | tf_op jit(solution)/shard_map/all_to_all | solution.py:48
  20.0 93.1 %copy-start.6 = (s32[1,64,3]{1,0,2:T(1,128)S(1)}, s32[1,64,3]{1,0,2:T(1,128)}, u32[]{:S(2)}) copy-start(s32[1,64,3]{1,0,2:T(1,128)} %param.10) | copy-start | bytes 2308
  63.4 49.6 %copy-start.4 = (bf16[16,2,256,128]{3,2,1,0:T(8,128)(2,1)}, bf16[16,2,256,128]{3,2,1,0:T(8,128)(2,1)S(1)}, u32[]{:S(2)}) copy-start(bf16[16,2,256,128]{3,2,1,0:T(8,128)(2,1)S(1)} %all-to-all-done.kv0) | copy-start | bytes 6291460
  63.4 46.4 %collective-permute-start.1 = (bf16[16,2,256,128]{3,2,1,0:T(8,128)(2,1)S(1)}, bf16[16,2,256,128]{3,2,1,0:T(8,128)(2,1)}, u32[]{:S(2)}, u32[]{:S(2)}) collective-permute-start(bf16[16,2,256,128]{3,2,1,0:T(8,128)(2,1)S(1)} %all-to-all-done.kv0), channel_id=1, source_target_pairs={{0,192},{4,196},{8,200},{12,204},{16,208},{20,212},{24,216},{28,22... | collective-permute-start | bytes 6291464 | tf_op jit(solution)/shard_map/ppermute | solution.py:515
  68.5 54.1 %all-to-all-start.1 = ((bf16[16,2,256,128]{3,2,1,0:T(8,128)(2,1)}), bf16[16,2,256,128]{3,2,1,0:T(8,128)(2,1)}, u32[]{:S(2)}, u32[]{:S(2)}) async-start(bf16[16,2,256,128]{3,2,1,0:T(8,128)(2,1)} %make_query.1), calls=%async_computation.1 | async-start | bytes 4194304 | tf_op jit(solution)/shard_map/all_to_all | solution.py:48
  75.2 38.7 %collective-permute-start = (bf16[16,2,256,128]{3,2,1,0:T(8,128)(2,1)S(1)}, bf16[16,2,256,128]{3,2,1,0:T(8,128)(2,1)}, u32[]{:S(2)}, u32[]{:S(2)}) collective-permute-start(bf16[16,2,256,128]{3,2,1,0:T(8,128)(2,1)S(1)} %all-to-all-done.kv0), channel_id=1, source_target_pairs={{0,4},{4,0},{8,12},{12,8},{16,20},{20,16},{24,28},{28,24},{32,36},... | collective-permute-start | bytes 6291464 | tf_op jit(solution)/shard_map/ppermute | solution.py:52
  109.8 12.9 %collective-permute-start.2 = (bf16[16,2,256,128]{3,2,1,0:T(8,128)(2,1)}, bf16[16,2,256,128]{3,2,1,0:T(8,128)(2,1)}, u32[]{:S(2)}, u32[]{:S(2)}) collective-permute-start(bf16[16,2,256,128]{3,2,1,0:T(8,128)(2,1)} %collective-permute-done.1.kv2), channel_id=1, source_target_pairs={{0,4},{4,0},{8,12},{12,8},{16,20},{20,16},{24,28},{28,24},{32,36},... | collective-permute-start | bytes 6291464 | tf_op jit(solution)/shard_map/ppermute | solution.py:52
  144.1 8.5 %collective-permute-start.4 = (bf16[16,2,256,128]{3,2,1,0:T(8,128)(2,1)}, bf16[16,2,256,128]{3,2,1,0:T(8,128)(2,1)}, u32[]{:S(2)}, u32[]{:S(2)}) collective-permute-start(bf16[16,2,256,128]{3,2,1,0:T(8,128)(2,1)} %get-tuple-element.33), channel_id=1, source_target_pairs={{0,4},{4,0},{8,12},{12,8},{16,20},{20,16},{24,28},{28,24},{32,36},... | collective-permute-start | bytes 6291464 | tf_op jit(solution)/shard_map/ppermute | solution.py:52
  146.9 5.7 %copy-start.3 = (bf16[16,2,256,128]{3,2,1,0:T(8,128)(2,1)S(1)}, bf16[16,2,256,128]{3,2,1,0:T(8,128)(2,1)}, u32[]{:S(2)}) copy-start(bf16[16,2,256,128]{3,2,1,0:T(8,128)(2,1)} %get-tuple-element.32) | copy-start | bytes 6291460
  146.9 60.6 %all-to-all-start.2 = ((bf16[16,2,256,128]{3,2,1,0:T(8,128)(2,1)}), bf16[16,2,256,128]{3,2,1,0:T(8,128)(2,1)}, u32[]{:S(2)}, u32[]{:S(2)}) async-start(bf16[16,2,256,128]{3,2,1,0:T(8,128)(2,1)} %get-tuple-element.34), calls=%async_computation.2 | async-start | bytes 4194304 | tf_op jit(solution)/shard_map/all_to_all | solution.py:48
  152.2 4.5 %collective-permute-start.3 = (bf16[16,2,256,128]{3,2,1,0:T(8,128)(2,1)}, bf16[16,2,256,128]{3,2,1,0:T(8,128)(2,1)S(1)}, u32[]{:S(2)}, u32[]{:S(2)}) collective-permute-start(bf16[16,2,256,128]{3,2,1,0:T(8,128)(2,1)} %get-tuple-element.31), channel_id=1, source_target_pairs={{0,4},{4,0},{8,12},{12,8},{16,20},{20,16},{24,28},{28,24},{32,36},... | collective-permute-start | bytes 6291464 | tf_op jit(solution)/shard_map/ppermute | solution.py:52
  152.6 52.6 %copy-start.2 = (f32[16,2,256,128]{3,2,1,0:T(8,128)S(1)}, f32[16,2,256,128]{3,2,1,0:T(8,128)}, u32[]{:S(2)}) copy-start(f32[16,2,256,128]{3,2,1,0:T(8,128)} %get-tuple-element.30) | copy-start | bytes 12582916
  155.1 50.1 %collective-permute-start.5 = (bf16[16,2,256,128]{3,2,1,0:T(8,128)(2,1)S(1)}, bf16[16,2,256,128]{3,2,1,0:T(8,128)(2,1)S(1)}, u32[]{:S(2)}, u32[]{:S(2)}) collective-permute-start(bf16[16,2,256,128]{3,2,1,0:T(8,128)(2,1)S(1)} %add_convert_fusion.1), channel_id=1, source_target_pairs={{192,0},{196,4},{200,8},{204,12},{208,16},{212,20},{216,24},{220,2... | collective-permute-start | bytes 6291464 | tf_op jit(solution)/shard_map/ppermute | solution.py:527
  207.4 7.2 %copy-start.5 = (bf16[256,96]{1,0:T(8,128)(2,1)S(1)}, bf16[256,96]{1,0:T(8,128)(2,1)}, u32[]{:S(2)}) copy-start(bf16[256,96]{1,0:T(8,128)(2,1)} %get-tuple-element.26.low_ref) | copy-start | bytes 147460
  207.4 7.3 %copy-start = (bf16[1,256,4096]{2,1,0:T(8,128)(2,1)S(1)}, bf16[1,256,4096]{2,1,0:T(8,128)(2,1)}, u32[]{:S(2)}) copy-start(bf16[1,256,4096]{2,1,0:T(8,128)(2,1)} %param.6) | copy-start | bytes 6291460
  207.4 7.3 %copy-start.1 = (bf16[3,32,2048]{2,1,0:T(8,128)(2,1)S(1)}, bf16[3,32,2048]{2,1,0:T(8,128)(2,1)}, u32[]{:S(2)}) copy-start(bf16[3,32,2048]{2,1,0:T(8,128)(2,1)} %up_ref.7) | copy-start | bytes 1179652
  207.4 54.7 %all-to-all-start.3 = ((bf16[16,2,256,128]{3,2,1,0:T(8,128)(2,1)}), bf16[16,2,256,128]{3,2,1,0:T(8,128)(2,1)}, u32[]{:S(2)}, u32[]{:S(2)}) async-start(bf16[16,2,256,128]{3,2,1,0:T(8,128)(2,1)} %add_convert_fusion), calls=%async_computation.3 | async-start | bytes 4194304 | tf_op jit(solution)/shard_map/all_to_all | solution.py:48
  219.6 2.2 collective-permute-start.6
  221.8 5.6 %collective-permute-start.7 = (bf16[16,24,128]{2,1,0:T(8,128)(2,1)S(1)}, bf16[16,24,128]{2,1,0:T(8,128)(2,1)S(1)}, u32[]{:S(2)}, u32[]{:S(2)}) collective-permute-start(bf16[16,24,128]{2,1,0:T(8,128)(2,1)S(1)} %slice.31), channel_id=1, source_target_pairs={{0,192},{4,196},{8,200},{12,204},{16,208},{20,212},{24,216},{28,22... | collective-permute-start | bytes 294920 | tf_op jit(solution)/shard_map/ppermute | solution.py:523
  267.1 4.2 %collective-permute-start.8 = (bf16[32,48,128]{2,1,0:T(8,128)(2,1)S(1)}, bf16[32,48,128]{2,1,0:T(8,128)(2,1)S(1)}, u32[]{:S(2)}, u32[]{:S(2)}) collective-permute-start(bf16[32,48,128]{2,1,0:T(8,128)(2,1)S(1)} %get-tuple-element.44), channel_id=1, source_target_pairs={{0,4},{4,0},{8,12},{12,8},{16,20},{20,16},{24,28},{28,24},{32,36},... | collective-permute-start | bytes 1179656 | tf_op jit(solution)/shard_map/ppermute | solution.py:52
  271.4 7.4 %collective-permute-start.9 = (bf16[16,48,128]{2,1,0:T(8,128)(2,1)S(1)}, bf16[16,48,128]{2,1,0:T(8,128)(2,1)S(1)}, u32[]{:S(2)}, u32[]{:S(2)}) collective-permute-start(bf16[16,48,128]{2,1,0:T(8,128)(2,1)S(1)} %slice.30), channel_id=1, source_target_pairs={{0,192},{4,196},{8,200},{12,204},{16,208},{20,212},{24,216},{28,22... | collective-permute-start | bytes 589832 | tf_op jit(solution)/shard_map/ppermute | solution.py:523
  291.7 3.7 %collective-permute-start.12 = (f32[72,128]{1,0:T(8,128)S(1)}, f32[72,128]{1,0:T(8,128)S(1)}, u32[]{:S(2)}, u32[]{:S(2)}) collective-permute-start(f32[72,128]{1,0:T(8,128)S(1)} %convert_reduce_fusion), channel_id=1, source_target_pairs={{0,3},{1,0},{2,1},{3,2},{4,7},{5,4},{6,5},{7,6},{8,11},{9,8},{10,9... | collective-permute-start | bytes 110600 | tf_op jit(solution)/shard_map/ppermute | solution.py:539
  294.2 4.3 %collective-permute-start.11 = (f32[72,128]{1,0:T(8,128)S(1)}, f32[72,128]{1,0:T(8,128)S(1)}, u32[]{:S(2)}, u32[]{:S(2)}) collective-permute-start(f32[72,128]{1,0:T(8,128)S(1)} %convert_reduce_fusion), channel_id=1, source_target_pairs={{0,2},{1,3},{2,0},{3,1},{4,6},{5,7},{6,4},{7,5},{8,10},{9,11},{10,... | collective-permute-start | bytes 110600 | tf_op jit(solution)/shard_map/ppermute | solution.py:539
  294.7 4.2 %collective-permute-start.10 = (f32[72,128]{1,0:T(8,128)S(1)}, f32[72,128]{1,0:T(8,128)S(1)}, u32[]{:S(2)}, u32[]{:S(2)}) collective-permute-start(f32[72,128]{1,0:T(8,128)S(1)} %convert_reduce_fusion), channel_id=1, source_target_pairs={{0,1},{1,2},{2,3},{3,0},{4,5},{5,6},{6,7},{7,4},{8,9},{9,10},{10,1... | collective-permute-start | bytes 110600 | tf_op jit(solution)/shard_map/ppermute | solution.py:539
  298.9 5.4 %collective-permute-start.13 = (f32[72,128]{1,0:T(8,128)S(1)}, f32[72,128]{1,0:T(8,128)S(1)}, u32[]{:S(2)}, u32[]{:S(2)}) collective-permute-start(f32[72,128]{1,0:T(8,128)S(1)} %add_add_fusion.mine_ref), channel_id=1, source_target_pairs={{0,4},{4,0},{8,12},{12,8},{16,20},{20,16},{24,28},{28,24},{32,36},... | collective-permute-start | bytes 110600 | tf_op jit(solution)/shard_map/ppermute | solution.py:52

commit v5 on v4

--- a/solution.py
+++ b/solution.py
@@ -347,12 +347,12 @@
     @pl.when((me & 1) == 0)
     def _():
         keep_ref[...] = terms[:, 0:24, :]
-        send_ref[...] = terms[:, 24:48, :].astype(jnp.bfloat16)
+        send_ref[...] = terms[:, 24:48, :]
 
     @pl.when((me & 1) == 1)
     def _():
         keep_ref[...] = terms[:, 24:48, :]
-        send_ref[...] = terms[:, 0:24, :].astype(jnp.bfloat16)
+        send_ref[...] = terms[:, 0:24, :]
 
 
 def key_value_grads_kernel(
@@ -407,7 +407,7 @@
             jax.ShapeDtypeStruct((BLK, HQ), jnp.bfloat16),
             jax.ShapeDtypeStruct((BLK, 3 * HQ), jnp.bfloat16),
             jax.ShapeDtypeStruct((TILES, 24, 128), jnp.float32),
-            jax.ShapeDtypeStruct((TILES, 24, 128), jnp.bfloat16),
+            jax.ShapeDtypeStruct((TILES, 24, 128), jnp.float32),
         ],
         compiler_params=pltpu.CompilerParams(vmem_limit_bytes=24 * 1024 * 1024),
         cost_estimate=pl.CostEstimate(

time: 306 us -> 306 us (level)
  no operation moved by 1% of the time
where the time goes in v5:
time: 306 us; the launch traced here: 305 us
  waiting for transfers between devices  189 us (62%)
  starting transfers between devices  55.7 us (18%)
  Pallas kernels  41.3 us (13%)
  blocking collectives  12.7 us (4%)
  other arithmetic  4.95 us (2%)
    all_to_all x4, waiting for transfers between devices, to_heads(): lax.all_to_all(x, 'ctx', 0, 0, axis_index_groups=HEAD_GROUPS, tiled=True)  86.7 us
    ppermute x1, waiting for transfers between devices, shards(): returned = lax.ppermute(far_sum.astype(jnp.bfloat16), 'ctx', TO_EARLIER)  48.6 us
    ppermute x1, waiting for transfers between devices, shards(): far = lax.ppermute(key_value, 'ctx', TO_LATER)  33.4 us
    all_to_all x4, starting transfers between devices, to_heads(): lax.all_to_all(x, 'ctx', 0, 0, axis_index_groups=HEAD_GROUPS, tiled=True)  29.2 us
    pallas_call x1, Pallas kernels, attend(): pl.pallas_call(attend_kernel, grid_spec=pltpu.PrefetchScalarGridSpec(num_...  21.4 us
    ppermute x7, starting transfers between devices, swap(): return lax.ppermute(x, 'ctx', CORE_PAIRS)  16.1 us
    all_to_all x1, blocking collectives, to_heads(): lax.all_to_all(x, 'ctx', 0, 0, axis_index_groups=HEAD_GROUPS, tiled=True)  12.7 us
    ppermute x2, waiting for transfers between devices, over_cores_and_halves(): lax.ppermute(both[16:].astype(jnp.bfloat16), 'ctx', TO_LATER + TO_EARLIER)  12.6 us
  transfers between devices with their start and end apart: 18, of which 13 were waited for; matrix products, arithmetic and copies ran while one was open for 2% of the time, Pallas kernels for 3%

profile of v5, /device:TPU:1, one launch (start us, length us, event | category | flops | bytes accessed | tf_op | source)
XLA Modules:
  0.0 305.2 jit_solution(13513367287285111386)
XLA Ops:
  0.6 5.0 %make_key_value.1 = (bf16[16,2,256,128]{3,2,1,0:T(8,128)(2,1)}, bf16[256,96]{1,0:T(8,128)(2,1)}) custom-call(bf16[256,4096]{1,0:T(8,128)(2,1)} %bitcast.10, bf16[3,32,4096]{2,1,0:T(8,128)(2,1)} %bitcast.20, bf16[256,6144]{1,0:T(8,128)(2,1)} %bitcast.15, bf16[256,6144]{1,0:T(8,128)(2,1)} %bitcast.16, bf16[3,32,2048]{2,1,0:T(8,128)(2,1)} %up_ref.7), custom_call_target="tpu_custom_call" | custom-call | flops 268435456 | bytes 7340032 | tf_op jit(solution)/shard_map/make_key_value/pallas_call | solution.py:86
  5.6 10.1 %all-to-all-start = ((bf16[16,2,256,128]{3,2,1,0:T(8,128)(2,1)}), bf16[16,2,256,128]{3,2,1,0:T(8,128)(2,1)S(1)}, u32[]{:S(2)}, u32[]{:S(2)}) async-start(bf16[16,2,256,128]{3,2,1,0:T(8,128)(2,1)} %get-tuple-element.27), calls=%async_computation | async-start | bytes 4194304 | tf_op jit(solution)/shard_map/all_to_all | solution.py:48
  15.8 4.2 %make_query.1 = bf16[16,2,256,128]{3,2,1,0:T(8,128)(2,1)} custom-call(bf16[256,96]{1,0:T(8,128)(2,1)} %get-tuple-element.26.low_ref, bf16[256,6144]{1,0:T(8,128)(2,1)} %bitcast.17, bf16[3,32,2048]{2,1,0:T(8,128)(2,1)} %up_ref.7, bf16[256,2048]{1,0:T(8,128)(2,1)} %bitcast.19), custom_call_target="tpu_custom_call" | custom-call | flops 33554432 | bytes 4194304 | tf_op jit(solution)/shard_map/make_query/pallas_call | solution.py:119
  20.0 43.4 %all-to-all-done.kv0 = bf16[16,2,256,128]{3,2,1,0:T(8,128)(2,1)S(1)} async-done(((bf16[16,2,256,128]{3,2,1,0:T(8,128)(2,1)}), bf16[16,2,256,128]{3,2,1,0:T(8,128)(2,1)S(1)}, u32[]{:S(2)}, u32[]{:S(2)}) %all-to-all-start) | async-done | bytes 2097184 | tf_op jit(solution)/shard_map/all_to_all | solution.py:48
  63.4 5.1 %collective-permute-start.1 = (bf16[16,2,256,128]{3,2,1,0:T(8,128)(2,1)S(1)}, bf16[16,2,256,128]{3,2,1,0:T(8,128)(2,1)}, u32[]{:S(2)}, u32[]{:S(2)}) collective-permute-start(bf16[16,2,256,128]{3,2,1,0:T(8,128)(2,1)S(1)} %all-to-all-done.kv0), channel_id=1, source_target_pairs={{0,192},{4,196},{8,200},{12,204},{16,208},{20,212},{24,216},{28,22... | collective-permute-start | bytes 6291464 | tf_op jit(solution)/shard_map/ppermute | solution.py:515
  68.5 6.6 %all-to-all-start.1 = ((bf16[16,2,256,128]{3,2,1,0:T(8,128)(2,1)}), bf16[16,2,256,128]{3,2,1,0:T(8,128)(2,1)}, u32[]{:S(2)}, u32[]{:S(2)}) async-start(bf16[16,2,256,128]{3,2,1,0:T(8,128)(2,1)} %make_query.1), calls=%async_computation.1 | async-start | bytes 4194304 | tf_op jit(solution)/shard_map/all_to_all | solution.py:48
  75.2 1.2 collective-permute-start
  76.3 33.4 %collective-permute-done.1.kv2 = bf16[16,2,256,128]{3,2,1,0:T(8,128)(2,1)} collective-permute-done((bf16[16,2,256,128]{3,2,1,0:T(8,128)(2,1)S(1)}, bf16[16,2,256,128]{3,2,1,0:T(8,128)(2,1)}, u32[]{:S(2)}, u32[]{:S(2)}) %collective-permute-start.1) | collective-permute-done | bytes 2097184 | tf_op jit(solution)/shard_map/ppermute | solution.py:515
  109.8 3.3 %collective-permute-start.2 = (bf16[16,2,256,128]{3,2,1,0:T(8,128)(2,1)}, bf16[16,2,256,128]{3,2,1,0:T(8,128)(2,1)}, u32[]{:S(2)}, u32[]{:S(2)}) collective-permute-start(bf16[16,2,256,128]{3,2,1,0:T(8,128)(2,1)} %collective-permute-done.1.kv2), channel_id=1, source_target_pairs={{0,4},{4,0},{8,12},{12,8},{16,20},{20,16},{24,28},{28,24},{32,36},... | collective-permute-start | bytes 6291464 | tf_op jit(solution)/shard_map/ppermute | solution.py:52
  113.0 0.1 copy.12
  113.1 0.7 reshape_squeeze.3.ids_ref
  113.8 0.0 collective-permute-done.kv1
  113.8 8.9 %all-to-all-done.1.qg_ref = bf16[16,2,256,128]{3,2,1,0:T(8,128)(2,1)} async-done(((bf16[16,2,256,128]{3,2,1,0:T(8,128)(2,1)}), bf16[16,2,256,128]{3,2,1,0:T(8,128)(2,1)}, u32[]{:S(2)}, u32[]{:S(2)}) %all-to-all-start.1) | async-done | bytes 2097184 | tf_op jit(solution)/shard_map/all_to_all | solution.py:48
  122.7 21.4 %attend.1 = (bf16[16,2,256,128]{3,2,1,0:T(8,128)(2,1)}, f32[16,2,256,128]{3,2,1,0:T(8,128)}, bf16[16,2,256,128]{3,2,1,0:T(8,128)(2,1)}, bf16[16,2,256,128]{3,2,1,0:T(8,128)(2,1)}, bf16[16,2,256,128]{3,2,1,0:T(8,128)(2,1)}) custom-call(s32[192]{0:T(256)} %reshape_squeeze.3.ids_ref, s32[1]{0:T(128)} %bitcast.me_ref, ...), custom_call_target="tpu_custom_call" | custom-call | flops 4831838208 | bytes 27262976 | tf_op jit(solution)/shard_map/attend/pallas_call | solution.py:276
  144.1 2.8 collective-permute-start.4
  146.9 5.3 %all-to-all-start.2 = ((bf16[16,2,256,128]{3,2,1,0:T(8,128)(2,1)}), bf16[16,2,256,128]{3,2,1,0:T(8,128)(2,1)}, u32[]{:S(2)}, u32[]{:S(2)}) async-start(bf16[16,2,256,128]{3,2,1,0:T(8,128)(2,1)} %get-tuple-element.34), calls=%async_computation.2 | async-start | bytes 4194304 | tf_op jit(solution)/shard_map/all_to_all | solution.py:48
  152.2 0.4 collective-permute-start.3
  152.6 0.0 collective-permute-done.4
  152.6 2.5 add_convert_fusion.1
  155.1 1.3 collective-permute-start.5
  156.4 0.3 collective-permute-done.3
  156.6 48.6 %collective-permute-done.5 = bf16[16,2,256,128]{3,2,1,0:T(8,128)(2,1)S(1)} collective-permute-done((bf16[16,2,256,128]{3,2,1,0:T(8,128)(2,1)S(1)}, bf16[16,2,256,128]{3,2,1,0:T(8,128)(2,1)S(1)}, u32[]{:S(2)}, u32[]{:S(2)}) %collective-permute-start.5) | collective-permute-done | bytes 2097184 | tf_op jit(solution)/shard_map/ppermute | solution.py:527
  205.2 2.2 add_convert_fusion
  207.4 0.0 all-to-all-done.2.home_ref
  207.4 7.2 %all-to-all-start.3 = ((bf16[16,2,256,128]{3,2,1,0:T(8,128)(2,1)}), bf16[16,2,256,128]{3,2,1,0:T(8,128)(2,1)}, u32[]{:S(2)}, u32[]{:S(2)}) async-start(bf16[16,2,256,128]{3,2,1,0:T(8,128)(2,1)} %add_convert_fusion), calls=%async_computation.3 | async-start | bytes 4194304 | tf_op jit(solution)/shard_map/all_to_all | solution.py:48
  214.6 0.1 copy.13
  214.8 4.8 %query_grads.1 = (bf16[256,2048]{1,0:T(8,128)(2,1)}, bf16[256,6144]{1,0:T(8,128)(2,1)}, f32[32,24,128]{2,1,0:T(8,128)S(1)}, f32[32,24,128]{2,1,0:T(8,128)S(1)}) custom-call(s32[1]{0:T(128)} %bitcast.me_ref, bf16[16,2,256,128]{3,2,1,0:T(8,128)(2,1)} %all-to-all-done.2.home_ref, bf16[256,4096]{1,0:T(8,128)(2,1)S(1)} %bitcast.11, bf16[96,256]{1,0:T(8,128)(2,1)S(1)} %bitcast.13, ...), custom_call_target="tpu_custom_call" | custom-call | flops 134217728 | bytes 8388608 | tf_op jit(solution)/shard_map/query_grads/pallas_call | solution.py:392
  219.6 1.1 collective-permute-start.6
  220.7 1.3 collective-permute-done.6
  222.1 0.3 collective-permute-start.7
  222.4 5.3 %collective-permute-done.7 = bf16[16,24,128]{2,1,0:T(8,128)(2,1)S(1)} collective-permute-done((bf16[16,24,128]{2,1,0:T(8,128)(2,1)S(1)}, bf16[16,24,128]{2,1,0:T(8,128)(2,1)S(1)}, u32[]{:S(2)}, u32[]{:S(2)}) %collective-permute-start.7) | collective-permute-done | bytes 98336 | tf_op jit(solution)/shard_map/ppermute | solution.py:523
  227.7 34.4 %all-to-all-done.3.home_ref = bf16[16,2,256,128]{3,2,1,0:T(8,128)(2,1)} async-done(((bf16[16,2,256,128]{3,2,1,0:T(8,128)(2,1)}), bf16[16,2,256,128]{3,2,1,0:T(8,128)(2,1)}, u32[]{:S(2)}, u32[]{:S(2)}) %all-to-all-start.3) | async-done | bytes 2097184 | tf_op jit(solution)/shard_map/all_to_all | solution.py:48
  262.1 5.0 %key_value_grads.1 = (bf16[256,6144]{1,0:T(8,128)(2,1)}, f32[32,48,128]{2,1,0:T(8,128)S(1)}, bf16[32,48,128]{2,1,0:T(8,128)(2,1)S(1)}) custom-call(s32[1]{0:T(128)} %bitcast.me_ref, bf16[256,6144]{1,0:T(8,128)(2,1)} %get-tuple-element.37._, bf16[16,2,256,128]{3,2,1,0:T(8,128)(2,1)} %all-to-all-done.3.home_ref, ...), custom_call_target="tpu_custom_call", output_to_operand_aliasing={{0}: (1, {})} | custom-call | flops 268435456 | bytes 8388608 | tf_op jit(solution)/shard_map/key_value_grads/pallas_call | solution.py:421
  267.1 2.8 collective-permute-start.8
  270.0 1.3 collective-permute-done.8
  271.3 0.1 convert_add_fusion
  271.4 0.1 collective-permute-start.9
  271.5 7.3 %collective-permute-done.9 = bf16[16,48,128]{2,1,0:T(8,128)(2,1)S(1)} collective-permute-done((bf16[16,48,128]{2,1,0:T(8,128)(2,1)S(1)}, bf16[16,48,128]{2,1,0:T(8,128)(2,1)S(1)}, u32[]{:S(2)}, u32[]{:S(2)}) %collective-permute-start.9) | collective-permute-done | bytes 196640 | tf_op jit(solution)/shard_map/ppermute | solution.py:523
  278.8 0.1 fusion
  278.9 12.7 %all_to_all.25 = bf16[16,72,128]{2,1,0:T(8,128)(2,1)S(1)} all-to-all(bf16[16,72,128]{2,1,0:T(8,128)(2,1)S(1)} %pad_maximum_fusion), channel_id=1, replica_groups={{0,8,16,24,32,40,48,56,64,72,80,88,96,104,112,120},{4,12,20,28,36,44,52..., dimensions={0} | all-to-all | bytes 589824 | tf_op jit(solution)/shard_map/all_to_all | solution.py:48
  291.7 2.5 collective-permute-start.12
  294.2 0.5 collective-permute-start.11
  294.7 0.6 collective-permute-start.10
  295.3 3.2 %collective-permute-done.11 = f32[72,128]{1,0:T(8,128)S(1)} collective-permute-done((f32[72,128]{1,0:T(8,128)S(1)}, f32[72,128]{1,0:T(8,128)S(1)}, u32[]{:S(2)}, u32[]{:S(2)}) %collective-permute-start.11) | collective-permute-done | bytes 36896 | tf_op jit(solution)/shard_map/ppermute | solution.py:539
  298.5 0.4 collective-permute-done.10
  298.9 4.6 %collective-permute-start.13 = (f32[72,128]{1,0:T(8,128)S(1)}, f32[72,128]{1,0:T(8,128)S(1)}, u32[]{:S(2)}, u32[]{:S(2)}) collective-permute-start(f32[72,128]{1,0:T(8,128)S(1)} %add_add_fusion.mine_ref), channel_id=1, source_target_pairs={{0,4},{4,0},{8,12},{12,8},{16,20},{20,16},{24,28},{28,24},{32,36},... | collective-permute-start | bytes 110600 | tf_op jit(solution)/shard_map/ppermute | solution.py:52
  303.5 0.9 collective-permute-done.13.other_ref
  304.3 0.9 finish.1
  (23 shorter events, 0.2 us)
Async XLA Ops:
  5.6 57.8 %all-to-all-start = ((bf16[16,2,256,128]{3,2,1,0:T(8,128)(2,1)}), bf16[16,2,256,128]{3,2,1,0:T(8,128)(2,1)S(1)}, u32[]{:S(2)}, u32[]{:S(2)}) async-start(bf16[16,2,256,128]{3,2,1,0:T(8,128)(2,1)} %get-tuple-element.27), calls=%async_computation | async-start | bytes 4194304 | tf_op jit(solution)/shard_map/all_to_all | solution.py:48
  20.0 93.1 %copy-start.6 = (s32[1,64,3]{1,0,2:T(1,128)S(1)}, s32[1,64,3]{1,0,2:T(1,128)}, u32[]{:S(2)}) copy-start(s32[1,64,3]{1,0,2:T(1,128)} %param.10) | copy-start | bytes 2308
  63.4 49.6 %copy-start.4 = (bf16[16,2,256,128]{3,2,1,0:T(8,128)(2,1)}, bf16[16,2,256,128]{3,2,1,0:T(8,128)(2,1)S(1)}, u32[]{:S(2)}) copy-start(bf16[16,2,256,128]{3,2,1,0:T(8,128)(2,1)S(1)} %all-to-all-done.kv0) | copy-start | bytes 6291460
  63.4 46.4 %collective-permute-start.1 = (bf16[16,2,256,128]{3,2,1,0:T(8,128)(2,1)S(1)}, bf16[16,2,256,128]{3,2,1,0:T(8,128)(2,1)}, u32[]{:S(2)}, u32[]{:S(2)}) collective-permute-start(bf16[16,2,256,128]{3,2,1,0:T(8,128)(2,1)S(1)} %all-to-all-done.kv0), channel_id=1, source_target_pairs={{0,192},{4,196},{8,200},{12,204},{16,208},{20,212},{24,216},{28,22... | collective-permute-start | bytes 6291464 | tf_op jit(solution)/shard_map/ppermute | solution.py:515
  68.5 54.1 %all-to-all-start.1 = ((bf16[16,2,256,128]{3,2,1,0:T(8,128)(2,1)}), bf16[16,2,256,128]{3,2,1,0:T(8,128)(2,1)}, u32[]{:S(2)}, u32[]{:S(2)}) async-start(bf16[16,2,256,128]{3,2,1,0:T(8,128)(2,1)} %make_query.1), calls=%async_computation.1 | async-start | bytes 4194304 | tf_op jit(solution)/shard_map/all_to_all | solution.py:48
  75.2 38.7 %collective-permute-start = (bf16[16,2,256,128]{3,2,1,0:T(8,128)(2,1)S(1)}, bf16[16,2,256,128]{3,2,1,0:T(8,128)(2,1)}, u32[]{:S(2)}, u32[]{:S(2)}) collective-permute-start(bf16[16,2,256,128]{3,2,1,0:T(8,128)(2,1)S(1)} %all-to-all-done.kv0), channel_id=1, source_target_pairs={{0,4},{4,0},{8,12},{12,8},{16,20},{20,16},{24,28},{28,24},{32,36},... | collective-permute-start | bytes 6291464 | tf_op jit(solution)/shard_map/ppermute | solution.py:52
  109.8 12.9 %collective-permute-start.2 = (bf16[16,2,256,128]{3,2,1,0:T(8,128)(2,1)}, bf16[16,2,256,128]{3,2,1,0:T(8,128)(2,1)}, u32[]{:S(2)}, u32[]{:S(2)}) collective-permute-start(bf16[16,2,256,128]{3,2,1,0:T(8,128)(2,1)} %collective-permute-done.1.kv2), channel_id=1, source_target_pairs={{0,4},{4,0},{8,12},{12,8},{16,20},{20,16},{24,28},{28,24},{32,36},... | collective-permute-start | bytes 6291464 | tf_op jit(solution)/shard_map/ppermute | solution.py:52
  144.1 8.5 %collective-permute-start.4 = (bf16[16,2,256,128]{3,2,1,0:T(8,128)(2,1)}, bf16[16,2,256,128]{3,2,1,0:T(8,128)(2,1)}, u32[]{:S(2)}, u32[]{:S(2)}) collective-permute-start(bf16[16,2,256,128]{3,2,1,0:T(8,128)(2,1)} %get-tuple-element.33), channel_id=1, source_target_pairs={{0,4},{4,0},{8,12},{12,8},{16,20},{20,16},{24,28},{28,24},{32,36},... | collective-permute-start | bytes 6291464 | tf_op jit(solution)/shard_map/ppermute | solution.py:52
  146.9 5.7 %copy-start.3 = (bf16[16,2,256,128]{3,2,1,0:T(8,128)(2,1)S(1)}, bf16[16,2,256,128]{3,2,1,0:T(8,128)(2,1)}, u32[]{:S(2)}) copy-start(bf16[16,2,256,128]{3,2,1,0:T(8,128)(2,1)} %get-tuple-element.32) | copy-start | bytes 6291460
  146.9 60.6 %all-to-all-start.2 = ((bf16[16,2,256,128]{3,2,1,0:T(8,128)(2,1)}), bf16[16,2,256,128]{3,2,1,0:T(8,128)(2,1)}, u32[]{:S(2)}, u32[]{:S(2)}) async-start(bf16[16,2,256,128]{3,2,1,0:T(8,128)(2,1)} %get-tuple-element.34), calls=%async_computation.2 | async-start | bytes 4194304 | tf_op jit(solution)/shard_map/all_to_all | solution.py:48
  152.2 4.5 %collective-permute-start.3 = (bf16[16,2,256,128]{3,2,1,0:T(8,128)(2,1)}, bf16[16,2,256,128]{3,2,1,0:T(8,128)(2,1)S(1)}, u32[]{:S(2)}, u32[]{:S(2)}) collective-permute-start(bf16[16,2,256,128]{3,2,1,0:T(8,128)(2,1)} %get-tuple-element.31), channel_id=1, source_target_pairs={{0,4},{4,0},{8,12},{12,8},{16,20},{20,16},{24,28},{28,24},{32,36},... | collective-permute-start | bytes 6291464 | tf_op jit(solution)/shard_map/ppermute | solution.py:52
  152.6 52.6 %copy-start.2 = (f32[16,2,256,128]{3,2,1,0:T(8,128)S(1)}, f32[16,2,256,128]{3,2,1,0:T(8,128)}, u32[]{:S(2)}) copy-start(f32[16,2,256,128]{3,2,1,0:T(8,128)} %get-tuple-element.30) | copy-start | bytes 12582916
  155.1 50.1 %collective-permute-start.5 = (bf16[16,2,256,128]{3,2,1,0:T(8,128)(2,1)S(1)}, bf16[16,2,256,128]{3,2,1,0:T(8,128)(2,1)S(1)}, u32[]{:S(2)}, u32[]{:S(2)}) collective-permute-start(bf16[16,2,256,128]{3,2,1,0:T(8,128)(2,1)S(1)} %add_convert_fusion.1), channel_id=1, source_target_pairs={{192,0},{196,4},{200,8},{204,12},{208,16},{212,20},{216,24},{220,2... | collective-permute-start | bytes 6291464 | tf_op jit(solution)/shard_map/ppermute | solution.py:527
  207.4 7.2 %copy-start.5 = (bf16[256,96]{1,0:T(8,128)(2,1)S(1)}, bf16[256,96]{1,0:T(8,128)(2,1)}, u32[]{:S(2)}) copy-start(bf16[256,96]{1,0:T(8,128)(2,1)} %get-tuple-element.26.low_ref) | copy-start | bytes 147460
  207.4 7.3 %copy-start = (bf16[1,256,4096]{2,1,0:T(8,128)(2,1)S(1)}, bf16[1,256,4096]{2,1,0:T(8,128)(2,1)}, u32[]{:S(2)}) copy-start(bf16[1,256,4096]{2,1,0:T(8,128)(2,1)} %param.6) | copy-start | bytes 6291460
  207.4 7.3 %copy-start.1 = (bf16[3,32,2048]{2,1,0:T(8,128)(2,1)S(1)}, bf16[3,32,2048]{2,1,0:T(8,128)(2,1)}, u32[]{:S(2)}) copy-start(bf16[3,32,2048]{2,1,0:T(8,128)(2,1)} %up_ref.7) | copy-start | bytes 1179652
  207.4 54.7 %all-to-all-start.3 = ((bf16[16,2,256,128]{3,2,1,0:T(8,128)(2,1)}), bf16[16,2,256,128]{3,2,1,0:T(8,128)(2,1)}, u32[]{:S(2)}, u32[]{:S(2)}) async-start(bf16[16,2,256,128]{3,2,1,0:T(8,128)(2,1)} %add_convert_fusion), calls=%async_computation.3 | async-start | bytes 4194304 | tf_op jit(solution)/shard_map/all_to_all | solution.py:48
  219.6 2.4 collective-permute-start.6
  222.1 5.6 %collective-permute-start.7 = (bf16[16,24,128]{2,1,0:T(8,128)(2,1)S(1)}, bf16[16,24,128]{2,1,0:T(8,128)(2,1)S(1)}, u32[]{:S(2)}, u32[]{:S(2)}) collective-permute-start(bf16[16,24,128]{2,1,0:T(8,128)(2,1)S(1)} %slice.31), channel_id=1, source_target_pairs={{0,192},{4,196},{8,200},{12,204},{16,208},{20,212},{24,216},{28,22... | collective-permute-start | bytes 294920 | tf_op jit(solution)/shard_map/ppermute | solution.py:523
  267.1 4.2 %collective-permute-start.8 = (bf16[32,48,128]{2,1,0:T(8,128)(2,1)S(1)}, bf16[32,48,128]{2,1,0:T(8,128)(2,1)S(1)}, u32[]{:S(2)}, u32[]{:S(2)}) collective-permute-start(bf16[32,48,128]{2,1,0:T(8,128)(2,1)S(1)} %get-tuple-element.44), channel_id=1, source_target_pairs={{0,4},{4,0},{8,12},{12,8},{16,20},{20,16},{24,28},{28,24},{32,36},... | collective-permute-start | bytes 1179656 | tf_op jit(solution)/shard_map/ppermute | solution.py:52
  271.4 7.4 %collective-permute-start.9 = (bf16[16,48,128]{2,1,0:T(8,128)(2,1)S(1)}, bf16[16,48,128]{2,1,0:T(8,128)(2,1)S(1)}, u32[]{:S(2)}, u32[]{:S(2)}) collective-permute-start(bf16[16,48,128]{2,1,0:T(8,128)(2,1)S(1)} %slice.30), channel_id=1, source_target_pairs={{0,192},{4,196},{8,200},{12,204},{16,208},{20,212},{24,216},{28,22... | collective-permute-start | bytes 589832 | tf_op jit(solution)/shard_map/ppermute | solution.py:523
  291.7 3.7 %collective-permute-start.12 = (f32[72,128]{1,0:T(8,128)S(1)}, f32[72,128]{1,0:T(8,128)S(1)}, u32[]{:S(2)}, u32[]{:S(2)}) collective-permute-start(f32[72,128]{1,0:T(8,128)S(1)} %convert_reduce_fusion), channel_id=1, source_target_pairs={{0,3},{1,0},{2,1},{3,2},{4,7},{5,4},{6,5},{7,6},{8,11},{9,8},{10,9... | collective-permute-start | bytes 110600 | tf_op jit(solution)/shard_map/ppermute | solution.py:539
  294.2 4.3 %collective-permute-start.11 = (f32[72,128]{1,0:T(8,128)S(1)}, f32[72,128]{1,0:T(8,128)S(1)}, u32[]{:S(2)}, u32[]{:S(2)}) collective-permute-start(f32[72,128]{1,0:T(8,128)S(1)} %convert_reduce_fusion), channel_id=1, source_target_pairs={{0,2},{1,3},{2,0},{3,1},{4,6},{5,7},{6,4},{7,5},{8,10},{9,11},{10,... | collective-permute-start | bytes 110600 | tf_op jit(solution)/shard_map/ppermute | solution.py:539
  294.7 4.2 %collective-permute-start.10 = (f32[72,128]{1,0:T(8,128)S(1)}, f32[72,128]{1,0:T(8,128)S(1)}, u32[]{:S(2)}, u32[]{:S(2)}) collective-permute-start(f32[72,128]{1,0:T(8,128)S(1)} %convert_reduce_fusion), channel_id=1, source_target_pairs={{0,1},{1,2},{2,3},{3,0},{4,5},{5,6},{6,7},{7,4},{8,9},{9,10},{10,1... | collective-permute-start | bytes 110600 | tf_op jit(solution)/shard_map/ppermute | solution.py:539
  298.9 5.4 %collective-permute-start.13 = (f32[72,128]{1,0:T(8,128)S(1)}, f32[72,128]{1,0:T(8,128)S(1)}, u32[]{:S(2)}, u32[]{:S(2)}) collective-permute-start(f32[72,128]{1,0:T(8,128)S(1)} %add_add_fusion.mine_ref), channel_id=1, source_target_pairs={{0,4},{4,0},{8,12},{12,8},{16,20},{20,16},{24,28},{28,24},{32,36},... | collective-permute-start | bytes 110600 | tf_op jit(solution)/shard_map/ppermute | solution.py:52

commit v6 on v5

--- a/solution.py
+++ b/solution.py
@@ -253,8 +253,7 @@
             copy.start()
             copies.append(copy)
 
-        send(acc.at[pl.ds(0, 16)], own_ref)
-        for n, (at, target) in enumerate(((48, farcore_ref), (32, far_ref), (16, core_ref))):
+        for n, (at, target) in enumerate(((48, farcore_ref), (32, far_ref), (0, own_ref), (16, core_ref))):
             def cast(i, _, n=n, at=at):
                 staged[n * 16 + i] = acc[at + i].astype(jnp.bfloat16)
                 return 0
@@ -268,7 +267,6 @@
 
 
 def attend(ids, me, query, key_values):
-    wide = jax.ShapeDtypeStruct((16, 2, BLK, HD), jnp.float32)
     narrow = jax.ShapeDtypeStruct((16, 2, BLK, HD), jnp.bfloat16)
     rows = pl.BlockSpec(
         (PER_STEP, 2, BLK, HD), lambda i, ids_ref, me_ref: (i ^ ((me_ref[0] >> 5) * 2), 0, 0, 0)
@@ -283,12 +281,12 @@
             scratch_shapes=[
                 pltpu.VMEM((64, 2, BLK, HD), jnp.bfloat16),
                 pltpu.VMEM((64, 2, BLK, HD), jnp.float32),
-                pltpu.VMEM((48, 2, BLK, HD), jnp.bfloat16),
+                pltpu.VMEM((64, 2, BLK, HD), jnp.bfloat16),
                 pltpu.SemaphoreType.DMA((4,)),
                 pltpu.SemaphoreType.DMA((4,)),
             ],
         ),
-        out_shape=[narrow, wide, narrow, narrow, narrow],
+        out_shape=[narrow] * 5,
         compiler_params=pltpu.CompilerParams(vmem_limit_bytes=VMEM_BYTES),
         cost_estimate=pl.CostEstimate(
             flops=16 * 6 * 2 * BLK * 3 * BLK * HD,
@@ -526,7 +524,7 @@
     far_sum = far_part.astype(jnp.float32) + swap(farcore_part).astype(jnp.float32)
     returned = lax.ppermute(far_sum.astype(jnp.bfloat16), "ctx", TO_EARLIER)
     out_home = to_heads(out)
-    total = own + swap(core_part).astype(jnp.float32) + returned.astype(jnp.float32)
+    total = own.astype(jnp.float32) + swap(core_part).astype(jnp.float32) + returned.astype(jnp.float32)
     total, out_home = after(total.astype(jnp.bfloat16), out_home)
     total_home = to_heads(total)
     attn_rows, grad_proj, keep, send = query_grads(me, out_home, tokens, low_t, up_projection)

time: 306 us -> 306 us (level)
  no operation moved by 1% of the time
where the time goes in v6:
time: 306 us; the launch traced here: 305 us
  waiting for transfers between devices  189 us (62%)
  starting transfers between devices  55.7 us (18%)
  Pallas kernels  41.1 us (13%)
  blocking collectives  12.7 us (4%)
  other arithmetic  5.09 us (2%)
    all_to_all x4, waiting for transfers between devices, to_heads(): lax.all_to_all(x, 'ctx', 0, 0, axis_index_groups=HEAD_GROUPS, tiled=True)  86.6 us
    ppermute x1, waiting for transfers between devices, shards(): returned = lax.ppermute(far_sum.astype(jnp.bfloat16), 'ctx', TO_EARLIER)  48.6 us
    ppermute x1, waiting for transfers between devices, shards(): far = lax.ppermute(key_value, 'ctx', TO_LATER)  33.5 us
    all_to_all x4, starting transfers between devices, to_heads(): lax.all_to_all(x, 'ctx', 0, 0, axis_index_groups=HEAD_GROUPS, tiled=True)  29.2 us
    pallas_call x1, Pallas kernels, attend(): pl.pallas_call(attend_kernel, grid_spec=pltpu.PrefetchScalarGridSpec(num_...  21.1 us
    ppermute x7, starting transfers between devices, swap(): return lax.ppermute(x, 'ctx', CORE_PAIRS)  16.1 us
    all_to_all x1, blocking collectives, to_heads(): lax.all_to_all(x, 'ctx', 0, 0, axis_index_groups=HEAD_GROUPS, tiled=True)  12.7 us
    ppermute x2, waiting for transfers between devices, over_cores_and_halves(): lax.ppermute(both[16:].astype(jnp.bfloat16), 'ctx', TO_LATER + TO_EARLIER)  12.6 us
  transfers between devices with their start and end apart: 18, of which 13 were waited for; matrix products, arithmetic and copies ran while one was open for 2% of the time, Pallas kernels for 3%

profile of v6, /device:TPU:1, one launch (start us, length us, event | category | flops | bytes accessed | tf_op | source)
XLA Modules:
  0.0 305.0 jit_solution(12750796729967517949)
XLA Ops:
  0.6 5.0 %make_key_value.1 = (bf16[16,2,256,128]{3,2,1,0:T(8,128)(2,1)}, bf16[256,96]{1,0:T(8,128)(2,1)}) custom-call(bf16[256,4096]{1,0:T(8,128)(2,1)} %bitcast.10, bf16[3,32,4096]{2,1,0:T(8,128)(2,1)} %bitcast.20, bf16[256,6144]{1,0:T(8,128)(2,1)} %bitcast.15, bf16[256,6144]{1,0:T(8,128)(2,1)} %bitcast.16, bf16[3,32,2048]{2,1,0:T(8,128)(2,1)} %up_ref.7), custom_call_target="tpu_custom_call" | custom-call | flops 268435456 | bytes 7340032 | tf_op jit(solution)/shard_map/make_key_value/pallas_call | solution.py:86
  5.6 10.1 %all-to-all-start = ((bf16[16,2,256,128]{3,2,1,0:T(8,128)(2,1)}), bf16[16,2,256,128]{3,2,1,0:T(8,128)(2,1)S(1)}, u32[]{:S(2)}, u32[]{:S(2)}) async-start(bf16[16,2,256,128]{3,2,1,0:T(8,128)(2,1)} %get-tuple-element.27), calls=%async_computation | async-start | bytes 4194304 | tf_op jit(solution)/shard_map/all_to_all | solution.py:48
  15.8 4.3 %make_query.1 = bf16[16,2,256,128]{3,2,1,0:T(8,128)(2,1)} custom-call(bf16[256,96]{1,0:T(8,128)(2,1)} %get-tuple-element.26.low_ref, bf16[256,6144]{1,0:T(8,128)(2,1)} %bitcast.17, bf16[3,32,2048]{2,1,0:T(8,128)(2,1)} %up_ref.7, bf16[256,2048]{1,0:T(8,128)(2,1)} %bitcast.19), custom_call_target="tpu_custom_call" | custom-call | flops 33554432 | bytes 4194304 | tf_op jit(solution)/shard_map/make_query/pallas_call | solution.py:119
  20.1 43.3 %all-to-all-done.kv0 = bf16[16,2,256,128]{3,2,1,0:T(8,128)(2,1)S(1)} async-done(((bf16[16,2,256,128]{3,2,1,0:T(8,128)(2,1)}), bf16[16,2,256,128]{3,2,1,0:T(8,128)(2,1)S(1)}, u32[]{:S(2)}, u32[]{:S(2)}) %all-to-all-start) | async-done | bytes 2097184 | tf_op jit(solution)/shard_map/all_to_all | solution.py:48
  63.4 5.1 %collective-permute-start.1 = (bf16[16,2,256,128]{3,2,1,0:T(8,128)(2,1)S(1)}, bf16[16,2,256,128]{3,2,1,0:T(8,128)(2,1)}, u32[]{:S(2)}, u32[]{:S(2)}) collective-permute-start(bf16[16,2,256,128]{3,2,1,0:T(8,128)(2,1)S(1)} %all-to-all-done.kv0), channel_id=1, source_target_pairs={{0,192},{4,196},{8,200},{12,204},{16,208},{20,212},{24,216},{28,22... | collective-permute-start | bytes 6291464 | tf_op jit(solution)/shard_map/ppermute | solution.py:513
  68.5 6.6 %all-to-all-start.1 = ((bf16[16,2,256,128]{3,2,1,0:T(8,128)(2,1)}), bf16[16,2,256,128]{3,2,1,0:T(8,128)(2,1)}, u32[]{:S(2)}, u32[]{:S(2)}) async-start(bf16[16,2,256,128]{3,2,1,0:T(8,128)(2,1)} %make_query.1), calls=%async_computation.1 | async-start | bytes 4194304 | tf_op jit(solution)/shard_map/all_to_all | solution.py:48
  75.1 1.2 collective-permute-start
  76.3 33.5 %collective-permute-done.1.kv2 = bf16[16,2,256,128]{3,2,1,0:T(8,128)(2,1)} collective-permute-done((bf16[16,2,256,128]{3,2,1,0:T(8,128)(2,1)S(1)}, bf16[16,2,256,128]{3,2,1,0:T(8,128)(2,1)}, u32[]{:S(2)}, u32[]{:S(2)}) %collective-permute-start.1) | collective-permute-done | bytes 2097184 | tf_op jit(solution)/shard_map/ppermute | solution.py:513
  109.8 3.3 %collective-permute-start.2 = (bf16[16,2,256,128]{3,2,1,0:T(8,128)(2,1)}, bf16[16,2,256,128]{3,2,1,0:T(8,128)(2,1)}, u32[]{:S(2)}, u32[]{:S(2)}) collective-permute-start(bf16[16,2,256,128]{3,2,1,0:T(8,128)(2,1)} %collective-permute-done.1.kv2), channel_id=1, source_target_pairs={{0,4},{4,0},{8,12},{12,8},{16,20},{20,16},{24,28},{28,24},{32,36},... | collective-permute-start | bytes 6291464 | tf_op jit(solution)/shard_map/ppermute | solution.py:52
  113.0 0.1 copy.12
  113.1 0.7 reshape_squeeze.3.ids_ref
  113.8 0.0 collective-permute-done.kv1
  113.8 8.8 %all-to-all-done.1.qg_ref = bf16[16,2,256,128]{3,2,1,0:T(8,128)(2,1)} async-done(((bf16[16,2,256,128]{3,2,1,0:T(8,128)(2,1)}), bf16[16,2,256,128]{3,2,1,0:T(8,128)(2,1)}, u32[]{:S(2)}, u32[]{:S(2)}) %all-to-all-start.1) | async-done | bytes 2097184 | tf_op jit(solution)/shard_map/all_to_all | solution.py:48
  122.7 0.0 collective-permute-done.2.kv3
  122.7 21.1 %attend.1 = (bf16[16,2,256,128]{3,2,1,0:T(8,128)(2,1)}, bf16[16,2,256,128]{3,2,1,0:T(8,128)(2,1)}, bf16[16,2,256,128]{3,2,1,0:T(8,128)(2,1)}, bf16[16,2,256,128]{3,2,1,0:T(8,128)(2,1)}, bf16[16,2,256,128]{3,2,1,0:T(8,128)(2,1)}) custom-call(s32[192]{0:T(256)} %reshape_squeeze.3.ids_ref, s32[1]{0:T(128)} %bitcast.me_ref, ...), custom_call_target="tpu_custom_call" | custom-call | flops 4831838208 | bytes 27262976 | tf_op jit(solution)/shard_map/attend/pallas_call | solution.py:274
  143.8 2.7 collective-permute-start.4
  146.6 5.3 %all-to-all-start.2 = ((bf16[16,2,256,128]{3,2,1,0:T(8,128)(2,1)}), bf16[16,2,256,128]{3,2,1,0:T(8,128)(2,1)}, u32[]{:S(2)}, u32[]{:S(2)}) async-start(bf16[16,2,256,128]{3,2,1,0:T(8,128)(2,1)} %get-tuple-element.34), calls=%async_computation.2 | async-start | bytes 4194304 | tf_op jit(solution)/shard_map/all_to_all | solution.py:48
  151.9 0.4 collective-permute-start.3
  152.3 2.5 add_convert_fusion.1
  154.8 1.3 collective-permute-start.5
  156.1 0.3 collective-permute-done.3
  156.3 48.6 %collective-permute-done.5 = bf16[16,2,256,128]{3,2,1,0:T(8,128)(2,1)S(1)} collective-permute-done((bf16[16,2,256,128]{3,2,1,0:T(8,128)(2,1)S(1)}, bf16[16,2,256,128]{3,2,1,0:T(8,128)(2,1)S(1)}, u32[]{:S(2)}, u32[]{:S(2)}) %collective-permute-start.5) | collective-permute-done | bytes 2097184 | tf_op jit(solution)/shard_map/ppermute | solution.py:525
  204.9 2.4 add_convert_fusion
  207.3 7.2 %all-to-all-start.3 = ((bf16[16,2,256,128]{3,2,1,0:T(8,128)(2,1)}), bf16[16,2,256,128]{3,2,1,0:T(8,128)(2,1)}, u32[]{:S(2)}, u32[]{:S(2)}) async-start(bf16[16,2,256,128]{3,2,1,0:T(8,128)(2,1)} %add_convert_fusion), calls=%async_computation.3 | async-start | bytes 4194304 | tf_op jit(solution)/shard_map/all_to_all | solution.py:48
  214.5 0.1 copy.13
  214.6 4.8 %query_grads.1 = (bf16[256,2048]{1,0:T(8,128)(2,1)}, bf16[256,6144]{1,0:T(8,128)(2,1)}, f32[32,24,128]{2,1,0:T(8,128)S(1)}, f32[32,24,128]{2,1,0:T(8,128)S(1)}) custom-call(s32[1]{0:T(128)} %bitcast.me_ref, bf16[16,2,256,128]{3,2,1,0:T(8,128)(2,1)} %all-to-all-done.2.home_ref, bf16[256,4096]{1,0:T(8,128)(2,1)S(1)} %bitcast.11, bf16[96,256]{1,0:T(8,128)(2,1)S(1)} %bitcast.13, ...), custom_call_target="tpu_custom_call" | custom-call | flops 134217728 | bytes 8388608 | tf_op jit(solution)/shard_map/query_grads/pallas_call | solution.py:390
  219.4 1.1 collective-permute-start.6
  220.5 1.3 collective-permute-done.6
  221.9 0.3 collective-permute-start.7
  222.2 5.3 %collective-permute-done.7 = bf16[16,24,128]{2,1,0:T(8,128)(2,1)S(1)} collective-permute-done((bf16[16,24,128]{2,1,0:T(8,128)(2,1)S(1)}, bf16[16,24,128]{2,1,0:T(8,128)(2,1)S(1)}, u32[]{:S(2)}, u32[]{:S(2)}) %collective-permute-start.7) | collective-permute-done | bytes 98336 | tf_op jit(solution)/shard_map/ppermute | solution.py:521
  227.5 34.4 %all-to-all-done.3.home_ref = bf16[16,2,256,128]{3,2,1,0:T(8,128)(2,1)} async-done(((bf16[16,2,256,128]{3,2,1,0:T(8,128)(2,1)}), bf16[16,2,256,128]{3,2,1,0:T(8,128)(2,1)}, u32[]{:S(2)}, u32[]{:S(2)}) %all-to-all-start.3) | async-done | bytes 2097184 | tf_op jit(solution)/shard_map/all_to_all | solution.py:48
  261.9 5.0 %key_value_grads.1 = (bf16[256,6144]{1,0:T(8,128)(2,1)}, f32[32,48,128]{2,1,0:T(8,128)S(1)}, bf16[32,48,128]{2,1,0:T(8,128)(2,1)S(1)}) custom-call(s32[1]{0:T(128)} %bitcast.me_ref, bf16[256,6144]{1,0:T(8,128)(2,1)} %get-tuple-element.37._, bf16[16,2,256,128]{3,2,1,0:T(8,128)(2,1)} %all-to-all-done.3.home_ref, ...), custom_call_target="tpu_custom_call", output_to_operand_aliasing={{0}: (1, {})} | custom-call | flops 268435456 | bytes 8388608 | tf_op jit(solution)/shard_map/key_value_grads/pallas_call | solution.py:419
  267.0 2.8 collective-permute-start.8
  269.8 1.3 collective-permute-done.8
  271.1 0.1 convert_add_fusion
  271.2 0.1 collective-permute-start.9
  271.3 7.3 %collective-permute-done.9 = bf16[16,48,128]{2,1,0:T(8,128)(2,1)S(1)} collective-permute-done((bf16[16,48,128]{2,1,0:T(8,128)(2,1)S(1)}, bf16[16,48,128]{2,1,0:T(8,128)(2,1)S(1)}, u32[]{:S(2)}, u32[]{:S(2)}) %collective-permute-start.9) | collective-permute-done | bytes 196640 | tf_op jit(solution)/shard_map/ppermute | solution.py:521
  278.7 0.1 fusion
  278.7 12.7 %all_to_all.25 = bf16[16,72,128]{2,1,0:T(8,128)(2,1)S(1)} all-to-all(bf16[16,72,128]{2,1,0:T(8,128)(2,1)S(1)} %pad_maximum_fusion), channel_id=1, replica_groups={{0,8,16,24,32,40,48,56,64,72,80,88,96,104,112,120},{4,12,20,28,36,44,52..., dimensions={0} | all-to-all | bytes 589824 | tf_op jit(solution)/shard_map/all_to_all | solution.py:48
  291.5 2.5 collective-permute-start.12
  294.0 0.5 collective-permute-start.11
  294.5 0.6 collective-permute-start.10
  295.1 0.0 collective-permute-done.12
  295.1 3.2 %collective-permute-done.11 = f32[72,128]{1,0:T(8,128)S(1)} collective-permute-done((f32[72,128]{1,0:T(8,128)S(1)}, f32[72,128]{1,0:T(8,128)S(1)}, u32[]{:S(2)}, u32[]{:S(2)}) %collective-permute-start.11) | collective-permute-done | bytes 36896 | tf_op jit(solution)/shard_map/ppermute | solution.py:537
  298.3 0.4 collective-permute-done.10
  298.7 4.6 %collective-permute-start.13 = (f32[72,128]{1,0:T(8,128)S(1)}, f32[72,128]{1,0:T(8,128)S(1)}, u32[]{:S(2)}, u32[]{:S(2)}) collective-permute-start(f32[72,128]{1,0:T(8,128)S(1)} %add_add_fusion.mine_ref), channel_id=1, source_target_pairs={{0,4},{4,0},{8,12},{12,8},{16,20},{20,16},{24,28},{28,24},{32,36},... | collective-permute-start | bytes 110600 | tf_op jit(solution)/shard_map/ppermute | solution.py:52
  303.3 0.9 collective-permute-done.13.other_ref
  304.2 0.9 finish.1
  (23 shorter events, 0.2 us)
Async XLA Ops:
  5.6 57.8 %all-to-all-start = ((bf16[16,2,256,128]{3,2,1,0:T(8,128)(2,1)}), bf16[16,2,256,128]{3,2,1,0:T(8,128)(2,1)S(1)}, u32[]{:S(2)}, u32[]{:S(2)}) async-start(bf16[16,2,256,128]{3,2,1,0:T(8,128)(2,1)} %get-tuple-element.27), calls=%async_computation | async-start | bytes 4194304 | tf_op jit(solution)/shard_map/all_to_all | solution.py:48
  20.1 92.9 %copy-start.6 = (s32[1,64,3]{1,0,2:T(1,128)S(1)}, s32[1,64,3]{1,0,2:T(1,128)}, u32[]{:S(2)}) copy-start(s32[1,64,3]{1,0,2:T(1,128)} %param.10) | copy-start | bytes 2308
  63.4 49.6 %copy-start.3 = (bf16[16,2,256,128]{3,2,1,0:T(8,128)(2,1)}, bf16[16,2,256,128]{3,2,1,0:T(8,128)(2,1)S(1)}, u32[]{:S(2)}) copy-start(bf16[16,2,256,128]{3,2,1,0:T(8,128)(2,1)S(1)} %all-to-all-done.kv0) | copy-start | bytes 6291460
  63.4 46.4 %collective-permute-start.1 = (bf16[16,2,256,128]{3,2,1,0:T(8,128)(2,1)S(1)}, bf16[16,2,256,128]{3,2,1,0:T(8,128)(2,1)}, u32[]{:S(2)}, u32[]{:S(2)}) collective-permute-start(bf16[16,2,256,128]{3,2,1,0:T(8,128)(2,1)S(1)} %all-to-all-done.kv0), channel_id=1, source_target_pairs={{0,192},{4,196},{8,200},{12,204},{16,208},{20,212},{24,216},{28,22... | collective-permute-start | bytes 6291464 | tf_op jit(solution)/shard_map/ppermute | solution.py:513
  68.5 54.1 %all-to-all-start.1 = ((bf16[16,2,256,128]{3,2,1,0:T(8,128)(2,1)}), bf16[16,2,256,128]{3,2,1,0:T(8,128)(2,1)}, u32[]{:S(2)}, u32[]{:S(2)}) async-start(bf16[16,2,256,128]{3,2,1,0:T(8,128)(2,1)} %make_query.1), calls=%async_computation.1 | async-start | bytes 4194304 | tf_op jit(solution)/shard_map/all_to_all | solution.py:48
  75.1 38.7 %collective-permute-start = (bf16[16,2,256,128]{3,2,1,0:T(8,128)(2,1)S(1)}, bf16[16,2,256,128]{3,2,1,0:T(8,128)(2,1)}, u32[]{:S(2)}, u32[]{:S(2)}) collective-permute-start(bf16[16,2,256,128]{3,2,1,0:T(8,128)(2,1)S(1)} %all-to-all-done.kv0), channel_id=1, source_target_pairs={{0,4},{4,0},{8,12},{12,8},{16,20},{20,16},{24,28},{28,24},{32,36},... | collective-permute-start | bytes 6291464 | tf_op jit(solution)/shard_map/ppermute | solution.py:52
  109.8 12.9 %collective-permute-start.2 = (bf16[16,2,256,128]{3,2,1,0:T(8,128)(2,1)}, bf16[16,2,256,128]{3,2,1,0:T(8,128)(2,1)}, u32[]{:S(2)}, u32[]{:S(2)}) collective-permute-start(bf16[16,2,256,128]{3,2,1,0:T(8,128)(2,1)} %collective-permute-done.1.kv2), channel_id=1, source_target_pairs={{0,4},{4,0},{8,12},{12,8},{16,20},{20,16},{24,28},{28,24},{32,36},... | collective-permute-start | bytes 6291464 | tf_op jit(solution)/shard_map/ppermute | solution.py:52
  143.8 8.5 %collective-permute-start.4 = (bf16[16,2,256,128]{3,2,1,0:T(8,128)(2,1)}, bf16[16,2,256,128]{3,2,1,0:T(8,128)(2,1)}, u32[]{:S(2)}, u32[]{:S(2)}) collective-permute-start(bf16[16,2,256,128]{3,2,1,0:T(8,128)(2,1)} %get-tuple-element.33), channel_id=1, source_target_pairs={{0,4},{4,0},{8,12},{12,8},{16,20},{20,16},{24,28},{28,24},{32,36},... | collective-permute-start | bytes 6291464 | tf_op jit(solution)/shard_map/ppermute | solution.py:52
  146.6 5.7 %copy-start.2 = (bf16[16,2,256,128]{3,2,1,0:T(8,128)(2,1)S(1)}, bf16[16,2,256,128]{3,2,1,0:T(8,128)(2,1)}, u32[]{:S(2)}) copy-start(bf16[16,2,256,128]{3,2,1,0:T(8,128)(2,1)} %get-tuple-element.32) | copy-start | bytes 6291460
  146.6 60.7 %all-to-all-start.2 = ((bf16[16,2,256,128]{3,2,1,0:T(8,128)(2,1)}), bf16[16,2,256,128]{3,2,1,0:T(8,128)(2,1)}, u32[]{:S(2)}, u32[]{:S(2)}) async-start(bf16[16,2,256,128]{3,2,1,0:T(8,128)(2,1)} %get-tuple-element.34), calls=%async_computation.2 | async-start | bytes 4194304 | tf_op jit(solution)/shard_map/all_to_all | solution.py:48
  151.9 4.5 %collective-permute-start.3 = (bf16[16,2,256,128]{3,2,1,0:T(8,128)(2,1)}, bf16[16,2,256,128]{3,2,1,0:T(8,128)(2,1)S(1)}, u32[]{:S(2)}, u32[]{:S(2)}) collective-permute-start(bf16[16,2,256,128]{3,2,1,0:T(8,128)(2,1)} %get-tuple-element.31), channel_id=1, source_target_pairs={{0,4},{4,0},{8,12},{12,8},{16,20},{20,16},{24,28},{28,24},{32,36},... | collective-permute-start | bytes 6291464 | tf_op jit(solution)/shard_map/ppermute | solution.py:52
  152.3 52.6 %copy-start.4 = (bf16[16,2,256,128]{3,2,1,0:T(8,128)(2,1)S(1)}, bf16[16,2,256,128]{3,2,1,0:T(8,128)(2,1)}, u32[]{:S(2)}) copy-start(bf16[16,2,256,128]{3,2,1,0:T(8,128)(2,1)} %get-tuple-element.30) | copy-start | bytes 6291460
  154.8 50.1 %collective-permute-start.5 = (bf16[16,2,256,128]{3,2,1,0:T(8,128)(2,1)S(1)}, bf16[16,2,256,128]{3,2,1,0:T(8,128)(2,1)S(1)}, u32[]{:S(2)}, u32[]{:S(2)}) collective-permute-start(bf16[16,2,256,128]{3,2,1,0:T(8,128)(2,1)S(1)} %add_convert_fusion.1), channel_id=1, source_target_pairs={{192,0},{196,4},{200,8},{204,12},{208,16},{212,20},{216,24},{220,2... | collective-permute-start | bytes 6291464 | tf_op jit(solution)/shard_map/ppermute | solution.py:525
  207.3 7.2 %copy-start.5 = (bf16[256,96]{1,0:T(8,128)(2,1)S(1)}, bf16[256,96]{1,0:T(8,128)(2,1)}, u32[]{:S(2)}) copy-start(bf16[256,96]{1,0:T(8,128)(2,1)} %get-tuple-element.26.low_ref) | copy-start | bytes 147460
  207.3 7.3 %copy-start = (bf16[1,256,4096]{2,1,0:T(8,128)(2,1)S(1)}, bf16[1,256,4096]{2,1,0:T(8,128)(2,1)}, u32[]{:S(2)}) copy-start(bf16[1,256,4096]{2,1,0:T(8,128)(2,1)} %param.6) | copy-start | bytes 6291460
  207.3 7.3 %copy-start.1 = (bf16[3,32,2048]{2,1,0:T(8,128)(2,1)S(1)}, bf16[3,32,2048]{2,1,0:T(8,128)(2,1)}, u32[]{:S(2)}) copy-start(bf16[3,32,2048]{2,1,0:T(8,128)(2,1)} %up_ref.7) | copy-start | bytes 1179652
  207.3 54.7 %all-to-all-start.3 = ((bf16[16,2,256,128]{3,2,1,0:T(8,128)(2,1)}), bf16[16,2,256,128]{3,2,1,0:T(8,128)(2,1)}, u32[]{:S(2)}, u32[]{:S(2)}) async-start(bf16[16,2,256,128]{3,2,1,0:T(8,128)(2,1)} %add_convert_fusion), calls=%async_computation.3 | async-start | bytes 4194304 | tf_op jit(solution)/shard_map/all_to_all | solution.py:48
  219.4 2.4 collective-permute-start.6
  221.9 5.6 %collective-permute-start.7 = (bf16[16,24,128]{2,1,0:T(8,128)(2,1)S(1)}, bf16[16,24,128]{2,1,0:T(8,128)(2,1)S(1)}, u32[]{:S(2)}, u32[]{:S(2)}) collective-permute-start(bf16[16,24,128]{2,1,0:T(8,128)(2,1)S(1)} %slice.31), channel_id=1, source_target_pairs={{0,192},{4,196},{8,200},{12,204},{16,208},{20,212},{24,216},{28,22... | collective-permute-start | bytes 294920 | tf_op jit(solution)/shard_map/ppermute | solution.py:521
  267.0 4.2 %collective-permute-start.8 = (bf16[32,48,128]{2,1,0:T(8,128)(2,1)S(1)}, bf16[32,48,128]{2,1,0:T(8,128)(2,1)S(1)}, u32[]{:S(2)}, u32[]{:S(2)}) collective-permute-start(bf16[32,48,128]{2,1,0:T(8,128)(2,1)S(1)} %get-tuple-element.44), channel_id=1, source_target_pairs={{0,4},{4,0},{8,12},{12,8},{16,20},{20,16},{24,28},{28,24},{32,36},... | collective-permute-start | bytes 1179656 | tf_op jit(solution)/shard_map/ppermute | solution.py:52
  271.2 7.4 %collective-permute-start.9 = (bf16[16,48,128]{2,1,0:T(8,128)(2,1)S(1)}, bf16[16,48,128]{2,1,0:T(8,128)(2,1)S(1)}, u32[]{:S(2)}, u32[]{:S(2)}) collective-permute-start(bf16[16,48,128]{2,1,0:T(8,128)(2,1)S(1)} %slice.30), channel_id=1, source_target_pairs={{0,192},{4,196},{8,200},{12,204},{16,208},{20,212},{24,216},{28,22... | collective-permute-start | bytes 589832 | tf_op jit(solution)/shard_map/ppermute | solution.py:521
  291.5 3.7 %collective-permute-start.12 = (f32[72,128]{1,0:T(8,128)S(1)}, f32[72,128]{1,0:T(8,128)S(1)}, u32[]{:S(2)}, u32[]{:S(2)}) collective-permute-start(f32[72,128]{1,0:T(8,128)S(1)} %convert_reduce_fusion), channel_id=1, source_target_pairs={{0,3},{1,0},{2,1},{3,2},{4,7},{5,4},{6,5},{7,6},{8,11},{9,8},{10,9... | collective-permute-start | bytes 110600 | tf_op jit(solution)/shard_map/ppermute | solution.py:537
  294.0 4.3 %collective-permute-start.11 = (f32[72,128]{1,0:T(8,128)S(1)}, f32[72,128]{1,0:T(8,128)S(1)}, u32[]{:S(2)}, u32[]{:S(2)}) collective-permute-start(f32[72,128]{1,0:T(8,128)S(1)} %convert_reduce_fusion), channel_id=1, source_target_pairs={{0,2},{1,3},{2,0},{3,1},{4,6},{5,7},{6,4},{7,5},{8,10},{9,11},{10,... | collective-permute-start | bytes 110600 | tf_op jit(solution)/shard_map/ppermute | solution.py:537
  294.5 4.2 %collective-permute-start.10 = (f32[72,128]{1,0:T(8,128)S(1)}, f32[72,128]{1,0:T(8,128)S(1)}, u32[]{:S(2)}, u32[]{:S(2)}) collective-permute-start(f32[72,128]{1,0:T(8,128)S(1)} %convert_reduce_fusion), channel_id=1, source_target_pairs={{0,1},{1,2},{2,3},{3,0},{4,5},{5,6},{6,7},{7,4},{8,9},{9,10},{10,1... | collective-permute-start | bytes 110600 | tf_op jit(solution)/shard_map/ppermute | solution.py:537
  298.7 5.4 %collective-permute-start.13 = (f32[72,128]{1,0:T(8,128)S(1)}, f32[72,128]{1,0:T(8,128)S(1)}, u32[]{:S(2)}, u32[]{:S(2)}) collective-permute-start(f32[72,128]{1,0:T(8,128)S(1)} %add_add_fusion.mine_ref), channel_id=1, source_target_pairs={{0,4},{4,0},{8,12},{12,8},{16,20},{20,16},{24,28},{28,24},{32,36},... | collective-permute-start | bytes 110600 | tf_op jit(solution)/shard_map/ppermute | solution.py:52
